TPU v7x, 32 devices: a whole 2x2x4 slice. The times are simulated.
32 devices in a mesh: groups: 2 (over x), heads: 16 (over z, y, core).
Axes of the slice: x: 2, y: 2, z: 4, core: 2. Of those that a mesh axis runs over, the one named last changes fastest.
Arguments:
- prompt_x: bfloat16 [16, 8192, 256], P('groups', 'heads'), parts along dimension 0, may hold values from -6 to 6
- prompt_b: bfloat16 [16, 256, 1024], P('groups'), parts along dimension 0, may hold values from -6 to 6
- prompt_c: bfloat16 [16, 256, 1024], P('groups'), parts along dimension 0, may hold values from -6 to 6
- prompt_dt: bfloat16 [128, 16, 256], P('heads', 'groups'), parts along dimension 1, may hold values from 0 to 2, as said below
- decay_rate: float32 [128], replicated, may hold values from 0.5 to 2
- skip_gain: float32 [128], replicated, may hold values from 0.5 to 1.5
- lengths: int32 [16], P('groups'), parts along dimension 0, may hold values from 64 to 256, as said below
- owner_list: int32 [32, 2], P('groups'), parts along dimension 0, may hold values from 0 to 7, as said below
- page_table: int32 [16, 128], P('groups'), parts along dimension 0, may hold values from 0 to 1023, as said below
- cache_pages: bfloat16 [2048, 16, 256], P(('groups', 'heads')), parts along dimension 0, may hold values from -8 to 8
- row_slot: int32 [64], P('groups'), parts along dimension 0, may hold values from 0 to 1
- step_x: bfloat16 [64, 3, 8192], P(('groups', 'heads')), parts along dimension 0, may hold values from -6 to 6
- step_b: bfloat16 [64, 3, 1024], P(('groups', 'heads')), parts along dimension 0, may hold values from -6 to 6
- step_c: bfloat16 [64, 3, 1024], P(('groups', 'heads')), parts along dimension 0, may hold values from -6 to 6
- step_dt: bfloat16 [64, 3, 128], P(('groups', 'heads')), parts along dimension 0, may hold values from 0 to 2, as said below
- queries: bfloat16 [64, 3, 8192], P(('groups', 'heads')), parts along dimension 0, may hold values from -8 to 8
- fresh_cache: bfloat16 [64, 3, 2048], P(('groups', 'heads')), parts along dimension 0, may hold values from -8 to 8
Outputs:
- prompt_out: bfloat16 [16, 8192, 256], P('groups', 'heads'), parts along dimension 0
- mixer_out: bfloat16 [64, 3, 8192], P(('groups', 'heads')), parts along dimension 0
- attention_out: bfloat16 [64, 3, 8192], P(('groups', 'heads')), parts along dimension 0
There are 2 independent parts, one for each index of `groups`. A program takes and returns all parts, laid end to end along the dimension named above; an argument that names none is the same for every part. Nothing has to cross between parts.
Inputs may be any that keep to these rules, and one draw needn't show every extreme that they name: `lengths`: every prompt holds 64 positions or more; in every draw one prompt holds exactly 256. `owner_list`: each row names 2 different prompts; every prompt is named in some row. `page_table`: every pool row is named by exactly one entry; entry [r, j] lies among the 64 pool rows that start at (j // 8) * 8 * 8. `prompt_dt`: positive. `step_dt`: positive.
All inputs are finite; a program needn't handle non-finite values.
Results may differ from a plain program's by a relative error of at most 0.0047.
Values may be sent and summed in bfloat16 or wider, within the bound.
No kernel may reach another device: no remote copies, remote signals or barrier semaphores. Data moves between devices by JAX's collectives and lax.ppermute only.
A program may use at most 192 MiB of HBM per device.

v0:
```python
import functools
import math

import jax
import jax.numpy as jnp
from jax import lax
from jax.experimental import pallas as pl
from jax.experimental.pallas import tpu as pltpu
from jax.sharding import PartitionSpec as P

NS = 256
HP = 64
HPG = 32
KVH = 8
HD = 128
PAGE = 16
LANES = 128
SUB = 8
HALF = 512
LEVELS = (128, 64, 32, 16)
LOG2E = math.log2(math.e)
SCORE = LOG2E / math.sqrt(HD)
NONE = -1e30
FLOOR = -1e29
EARLY = 2
VMEM_LIMIT = 40 * 1024 * 1024

f32 = jnp.float32
bf16 = jnp.bfloat16


def iota(shape, dim):
    return lax.broadcasted_iota(jnp.int32, shape, dim)


def dot_nt(left, right):
    return lax.dot_general(left, right, (((1,), (1,)), ((), ())), preferred_element_type=f32)


def stack_rows(source, held):
    rows, steps = source.shape[0], source.shape[1]
    held[...] = jnp.zeros_like(held)
    for i in range(rows):
        held[i * steps : (i + 1) * steps, :] = source[i].astype(f32)


def pack_kernel(group, ways, q_ref, c_ref, out_ref, q_held, c_held):
    owners = out_ref.shape[0]
    stack_rows(q_ref, q_held)
    stack_rows(c_ref, c_held)
    span = 2 * HALF
    for v in range(KVH):
        both = jnp.concatenate(
            [q_held[:, v * span : v * span + HALF], q_held[:, v * span + HALF : (v + 1) * span]], axis=0
        ).astype(bf16)
        for way in range(ways):
            out_ref[v * ways + way, :, :HALF] = both
    for e in range(c_ref.shape[2] // NS):
        low = c_held[:, e * NS : e * NS + LANES]
        high = c_held[:, e * NS + LANES : (e + 1) * NS]
        both = jnp.concatenate([low, high], axis=0).astype(bf16)
        for d in range(owners):
            if (d * group) // HPG == e:
                out_ref[d, :, HALF:] = both


def head_factors(first, dt_ref, rate_ref, skip_ref, len_ref, levels, w_in, w_out, w_skip, w_tail):
    group, prompts, length = dt_ref.shape
    row = iota((prompts, length), 0)
    lens = jnp.zeros((prompts, length), jnp.int32)
    for r in range(prompts):
        lens = jnp.where(row == r, len_ref[r], lens)
    valid = iota((prompts, length), 1) < lens
    moved = [jnp.where(valid, dt_ref[h].astype(f32), 0.0) for h in range(group)]
    every = jnp.concatenate(moved, axis=0).astype(bf16)
    j = iota((length, length), 0)
    i = iota((length, length), 1)
    rates = [rate_ref[first + h] * LOG2E for h in range(group)]
    if w_tail is not None:
        after = jnp.where(j > i, 1.0, 0.0).astype(bf16)
        total = jnp.dot(every, after, preferred_element_type=f32)
        for h in range(group):
            part = total[h * prompts : (h + 1) * prompts]
            w_tail[:, h, :] = jnp.exp2(-(rates[h] * part)) * moved[h]
    if not levels:
        return
    for h in range(group):
        w_skip[:, h, :] = jnp.where(valid, skip_ref[first + h], 0.0)
    for l, n in enumerate(levels):
        middle = (i // (2 * n)) * (2 * n) + (n - 1)
        signs = (jnp.where(j <= i, 1.0, 0.0) - jnp.where(j <= middle, 1.0, 0.0)).astype(bf16)
        total = jnp.dot(every, signs, preferred_element_type=f32)
        for h in range(group):
            gap = rates[h] * total[h * prompts : (h + 1) * prompts]
            if n == LEVELS[-1]:
                up, down = jnp.exp2(gap), jnp.exp2(-gap)
            else:
                up, down = jnp.exp2(jnp.minimum(gap, 0.0)), jnp.exp2(-jnp.maximum(gap, 0.0))
            w_in[l, :, h, :] = up * moved[h]
            w_out[l, :, h, :] = jnp.where(valid, down, 0.0)


def level_masks(masks):
    length = masks.shape[-1]
    j = iota((length, length), 0)
    i = iota((length, length), 1)
    for l, n in enumerate(LEVELS):
        same = (j // (2 * n)) == (i // (2 * n))
        if n == LEVELS[-1]:
            keep = same & (j <= i)
        else:
            keep = same & ((j % (2 * n)) < n) & ((i % (2 * n)) >= n)
        masks[l] = jnp.where(keep, 1.0, 0.0).astype(bf16)


def prompt_result(r, x_held, b_held, c_held, w_in, w_out, w_skip, masks, out_held):
    width, length = x_held.shape[1], x_held.shape[2]
    group = width // HP
    half = length // 2
    inputs = x_held[r].astype(f32).reshape(group, HP, length)
    scores = dot_nt(b_held[r], c_held[r]).astype(bf16)
    total = inputs * w_skip[r][:, None, :]
    left, right = total[..., :half], total[..., half:]
    for l, n in enumerate(LEVELS):
        if 2 * n == length:
            scaled = (inputs[..., :half] * w_in[l, r][:, None, :half]).astype(bf16).reshape(width, half)
            added = jnp.dot(scaled, scores[:half, half:], preferred_element_type=f32)
            right = right + added.reshape(group, HP, half) * w_out[l, r][:, None, half:]
        else:
            scaled = (inputs * w_in[l, r][:, None, :]).astype(bf16).reshape(width, length)
            added = jnp.dot(scaled, scores * masks[l], preferred_element_type=f32)
            added = added.reshape(group, HP, length) * w_out[l, r][:, None, :]
            left = left + added[..., :half]
            right = right + added[..., half:]
    out_held[r] = jnp.concatenate([left, right], axis=-1).reshape(width, length).astype(bf16)


def state_kernel(
    rate_ref,
    skip_ref,
    len_ref,
    owner_ref,
    table_ref,
    slot_ref,
    dt_ref,
    x_any,
    b_any,
    c_any,
    state_ref,
    tag_ref,
    req_ref,
    out_any,
    x_held,
    b_held,
    c_held,
    out_held,
    w_in,
    w_out,
    w_skip,
    w_tail,
    masks,
    x_sem,
    b_sem,
    c_sem,
    out_sem,
):
    group, prompts, length = dt_ref.shape
    me = lax.axis_index("heads")
    first = me * group
    column = pl.multiple_of((first // HPG) * NS, NS)

    def x_copy(r):
        return pltpu.make_async_copy(x_any.at[r], x_held.at[r], x_sem.at[r])

    def b_copy(r):
        return pltpu.make_async_copy(b_any.at[r, :, pl.ds(column, NS)], b_held.at[r], b_sem.at[r])

    def c_copy(r):
        return pltpu.make_async_copy(c_any.at[r, :, pl.ds(column, NS)], c_held.at[r], c_sem.at[r])

    def out_copy(r):
        return pltpu.make_async_copy(out_held.at[r], out_any.at[r], out_sem.at[r])

    for r in range(prompts):
        x_copy(r).start()
        b_copy(r).start()
    for r in range(EARLY):
        c_copy(r).start()

    head_factors(
        first, dt_ref, rate_ref, skip_ref, len_ref, LEVELS if EARLY else (), w_in, w_out, w_skip, w_tail
    )

    spread = table_ref.shape[1] // owner_ref.shape[0]
    key_page = iota((SUB, LANES), 0) * (LANES // PAGE) + iota((SUB, LANES), 1) // PAGE
    key_offset = iota((SUB, LANES), 1) % PAGE
    tag = jnp.full((SUB, LANES), -1, jnp.int32)
    per_head = table_ref.shape[1] // KVH
    for r in range(prompts):
        for page in range(spread):
            entry = me * spread + page
            row = table_ref[r, entry] - me * (prompts * spread)
            begin = lax.rem(entry, per_head) * PAGE
            inside = (key_page == row) & (key_offset < len_ref[r] - begin)
            tag = jnp.where(inside, r, tag)
    tag_ref[...] = tag

    owners = owner_ref.shape[0]
    rows_dev = slot_ref.shape[0] // owners
    steps = 3
    inner = iota((2 * SUB, LANES), 0) % SUB

    def fill(s, _):
        block = jnp.full((2 * SUB, LANES), -2, jnp.int32)
        for i in range(rows_dev):
            target = owner_ref[s, slot_ref[s * rows_dev + i]]
            block = jnp.where((inner >= i * steps) & (inner < (i + 1) * steps), target, block)
        req_ref[pl.ds(pl.multiple_of(s * 2 * SUB, 2 * SUB), 2 * SUB), :] = block
        return 0

    lax.fori_loop(0, owners, fill, 0)

    def one(r, _):
        x_copy(r).wait()
        b_copy(r).wait()
        width = x_held.shape[1]
        inputs = x_held[r].astype(f32).reshape(group, HP, length)
        scaled = (inputs * w_tail[r][:, None, :]).astype(bf16).reshape(width, length)
        state_ref[r] = jnp.dot(scaled, b_held[r], preferred_element_type=f32).astype(bf16)
        return 0

    lax.fori_loop(0, prompts, one, 0)

    if EARLY:
        level_masks(masks)

        def early(r, _):
            c_copy(r).wait()
            prompt_result(r, x_held, b_held, c_held, w_in, w_out, w_skip, masks, out_held)
            out_copy(r).start()
            return 0

        lax.fori_loop(0, EARLY, early, 0)
        for r in range(EARLY):
            out_copy(r).wait()


def serve_kernel(recv_ref, pages_ref, tag_ref, req_ref, state_ref, out_ref, bias):
    rows = recv_ref.shape[0]
    keys = pages_ref.shape[0]
    prompts, width = state_ref.shape[0], state_ref.shape[1]
    tag = tag_ref[...]
    for b in range(keys // LANES):
        mine = jnp.broadcast_to(tag[b : b + 1, :], (rows, LANES))
        bias[:, b * LANES : (b + 1) * LANES] = jnp.where(req_ref[...] == mine, 0.0, NONE)
    lane = iota((rows, LANES), 1)
    sums = jnp.zeros((rows, LANES), f32)
    for g in range(HALF // HD):
        scores = dot_nt(recv_ref[:, g * HD : (g + 1) * HD], pages_ref[:, :HD]) * SCORE + bias[...]
        highest = jnp.maximum(jnp.max(scores, axis=1, keepdims=True), FLOOR)
        weight = jnp.exp2(scores - highest)
        total = jnp.sum(weight, axis=1, keepdims=True)
        value = jnp.dot(weight.astype(bf16), pages_ref[:, HD:], preferred_element_type=f32)
        some = total > 0.0
        safe = jnp.where(some, total, 1.0)
        out_ref[:, g * HD : (g + 1) * HD] = (value / safe).astype(bf16)
        sums = jnp.where(lane % 4 == g, highest + jnp.log2(safe), sums)
    high = sums.astype(bf16)
    rest = sums - high.astype(f32)
    middle = rest.astype(bf16)
    low = rest - middle.astype(f32)
    third = lane // 4
    pieces = jnp.where(third == 0, high.astype(f32), jnp.where(third == 1, middle.astype(f32), low))
    held = projected_columns(width)
    out_ref[:, HALF + held :] = pieces.astype(bf16)

    blocks = rows // (2 * SUB)
    ahead = recv_ref[:, HALF:].astype(f32).reshape(blocks, 2, SUB, LANES)
    readout = jnp.concatenate([ahead[:, 0], ahead[:, 1]], axis=-1).reshape(blocks * SUB, NS)
    target = req_ref[...].reshape(blocks, 2, SUB, LANES)[:, 0].reshape(blocks * SUB, LANES)
    target = jnp.concatenate([target, target], axis=-1)
    found = jnp.zeros((blocks * SUB, width), f32)
    for r in range(prompts):
        picked = jnp.where(target == r, readout, 0.0).astype(bf16)
        found = found + dot_nt(picked, state_ref[r])
    if width == 2 * held:
        found = found.reshape(blocks, SUB, width)
        both = jnp.stack([found[..., :held], found[..., held:]], axis=1)
    else:
        found = jnp.concatenate([found, jnp.zeros((blocks * SUB, held - width), f32)], axis=-1)
        found = found.reshape(blocks, SUB, held)
        both = jnp.stack([found, found], axis=1)
    out_ref[:, HALF : HALF + held] = both.reshape(rows, held).astype(bf16)


def projected_columns(width):
    return max(LANES, width // 2)


def prompt_kernel(
    rate_ref,
    skip_ref,
    len_ref,
    dt_ref,
    rates_ref,
    skips_ref,
    send_ref,
    fresh_ref,
    sx_ref,
    sb_ref,
    sc_ref,
    sdt_ref,
    x_any,
    b_any,
    c_any,
    after_any,
    early_any,
    out_any,
    own_ref,
    ownsum_ref,
    fade_ref,
    local_ref,
    x_held,
    b_held,
    c_held,
    out_held,
    w_in,
    w_out,
    w_skip,
    masks,
    fresh_held,
    c_rows,
    x_rows,
    x_sem,
    b_sem,
    c_sem,
    out_sem,
):
    group, prompts, length = dt_ref.shape
    me = lax.axis_index("heads")
    first = me * group
    column = pl.multiple_of((first // HPG) * NS, NS)

    def x_copy(r):
        return pltpu.make_async_copy(x_any.at[r], x_held.at[r], x_sem.at[r])

    def b_copy(r):
        return pltpu.make_async_copy(b_any.at[r, :, pl.ds(column, NS)], b_held.at[r], b_sem.at[r])

    def c_copy(r):
        return pltpu.make_async_copy(c_any.at[r, :, pl.ds(column, NS)], c_held.at[r], c_sem.at[r])

    def out_copy(r):
        return pltpu.make_async_copy(out_held.at[r], out_any.at[r], out_sem.at[r])

    for r in range(EARLY, prompts):
        x_copy(r).start()
        b_copy(r).start()
        c_copy(r).start()

    head_factors(first, dt_ref, rate_ref, skip_ref, len_ref, LEVELS, w_in, w_out, w_skip, None)
    level_masks(masks)

    def one(r, _):
        x_copy(r).wait()
        b_copy(r).wait()
        c_copy(r).wait()
        prompt_result(r, x_held, b_held, c_held, w_in, w_out, w_skip, masks, out_held)
        out_copy(r).start()
        return 0

    lax.fori_loop(EARLY, prompts, one, 0)
    own_attention(send_ref, fresh_ref, fresh_held, own_ref, ownsum_ref)
    own_mixer(rates_ref, skips_ref, sx_ref, sb_ref, sc_ref, sdt_ref, c_rows, x_rows, fade_ref, local_ref)
    for r in range(EARLY, prompts):
        out_copy(r).wait()


def own_attention(send_ref, fresh_ref, fresh_held, own_ref, ownsum_ref):
    rows, steps = fresh_ref.shape[0], fresh_ref.shape[1]
    ways = send_ref.shape[0] // KVH
    stack_rows(fresh_ref, fresh_held)
    count = HALF // HD * 2 * SUB
    pair = iota((count, SUB), 0) % SUB
    key = iota((count, SUB), 1)
    seen = (key // steps == pair // steps) & (key <= pair) & (key < rows * steps)
    seen = seen | ((pair >= rows * steps) & (key == 0))
    for v in range(KVH):
        block = send_ref[v * ways]
        query = jnp.concatenate([block[:, g * HD : (g + 1) * HD] for g in range(HALF // HD)], axis=0)
        keys = fresh_held[:, v * HD : (v + 1) * HD].astype(bf16)
        values = fresh_held[:, (KVH + v) * HD : (KVH + v + 1) * HD].astype(bf16)
        scores = jnp.where(seen, dot_nt(query, keys) * SCORE, NONE)
        highest = jnp.max(scores, axis=1, keepdims=True)
        weight = jnp.exp2(scores - highest)
        total = jnp.sum(weight, axis=1, keepdims=True)
        weight = (weight / total).astype(bf16)
        own_ref[v] = jnp.dot(weight, values, preferred_element_type=f32)
        ownsum_ref[v] = jnp.broadcast_to(highest + jnp.log2(total), (count, HD))


def own_mixer(rates_ref, skips_ref, sx_ref, sb_ref, sc_ref, sdt_ref, c_rows, x_rows, fade_ref, local_ref):
    rows, steps, heads = sdt_ref.shape
    stack_rows(sc_ref, c_rows)
    for u in range(steps):
        x_rows[u] = jnp.zeros(x_rows.shape[1:], f32)
        for i in range(rows):
            x_rows[u, i * steps : (i + 1) * steps, :] = jnp.broadcast_to(
                sx_ref[i, u : u + 1, :].astype(f32), (steps, x_rows.shape[2])
            )
    pair = iota((SUB, heads), 0)
    step = pair % steps
    live = pair < rows * steps
    head = iota((SUB, heads), 1)

    def spread_rows(ref, u):
        picked = jnp.broadcast_to(ref[0, u : u + 1, :].astype(f32), (SUB, ref.shape[2]))
        which = iota(picked.shape, 0) // steps
        for i in range(1, rows):
            other = jnp.broadcast_to(ref[i, u : u + 1, :].astype(f32), (SUB, ref.shape[2]))
            picked = jnp.where(which == i, other, picked)
        return picked

    rates = jnp.broadcast_to(rates_ref[...], (SUB, heads)) * LOG2E
    skips = jnp.broadcast_to(skips_ref[...], (SUB, heads))
    moved = [spread_rows(sdt_ref, u) for u in range(steps)]
    kept = [jnp.where(u <= step, moved[u], 0.0) for u in range(steps)]
    parts = [jnp.where(live, jnp.exp2(-(rates * sum(kept))), 0.0)]
    for u in range(steps):
        products = c_rows[...] * spread_rows(sb_ref, u)
        inner = jnp.zeros((SUB, heads), f32)
        for e in range(products.shape[1] // NS):
            found = jnp.sum(products[:, e * NS : (e + 1) * NS], axis=1, keepdims=True)
            inner = jnp.where(head // HPG == e, found, inner)
        gap = jnp.zeros((SUB, heads), f32)
        for t in range(u + 1, steps):
            gap = gap + kept[t]
        weight = jnp.where(u <= step, jnp.exp2(-(rates * gap)) * moved[u] * inner, 0.0)
        weight = weight + jnp.where(u == step, skips, 0.0)
        parts.append(jnp.where(live, weight, 0.0))
    stacked = jnp.concatenate(parts, axis=0)
    high = stacked.astype(bf16)
    low = (stacked - high.astype(f32)).astype(bf16)
    both = jnp.concatenate([high.astype(f32), low.astype(f32)], axis=0)
    count = stacked.shape[0]
    chunk = SUB * HP
    widen = jnp.where(iota((heads, chunk), 0) % SUB == iota((heads, chunk), 1) // HP, 1.0, 0.0).astype(bf16)
    lane = iota(both.shape, 1)
    for d in range(heads // SUB):
        picked = jnp.where(lane // SUB == d, both, 0.0).astype(bf16)
        wide = jnp.dot(picked, widen, preferred_element_type=f32)
        wide = wide[:count] + wide[count:]
        columns = slice(d * chunk, (d + 1) * chunk)
        fade_ref[:, columns] = wide[:SUB]
        value = jnp.zeros((SUB, chunk), f32)
        for u in range(steps):
            value = value + wide[(u + 1) * SUB : (u + 2) * SUB] * x_rows[u, :, columns]
        local_ref[:, columns] = value


def merge_kernel(
    width, back_ref, own_ref, ownsum_ref, fade_ref, local_ref, mixer_ref, attention_ref, mixed, attended
):
    owners = back_ref.shape[0]
    ways = owners // KVH
    held = projected_columns(width)
    rows, steps = mixer_ref.shape[0], mixer_ref.shape[1]
    if width == 2 * held:
        for d in range(owners):
            for half in range(2):
                columns = slice(d * width + half * held, d * width + (half + 1) * held)
                found = back_ref[d, :, HALF : HALF + held].astype(f32)[half * SUB : (half + 1) * SUB]
                mixed[:, columns] = found * fade_ref[:, columns] + local_ref[:, columns]
    else:
        many = LANES // width
        for d in range(0, owners, many):
            found = jnp.concatenate(
                [back_ref[d + n, :, HALF : HALF + held].astype(f32)[:SUB, :width] for n in range(many)], axis=-1
            )
            columns = slice(d * width, (d + many) * width)
            mixed[:, columns] = found * fade_ref[:, columns] + local_ref[:, columns]
    for i in range(rows):
        mixer_ref[i] = mixed[i * steps : (i + 1) * steps, :].astype(bf16)
    for v in range(KVH):
        sums = []
        for way in range(ways):
            pieces = back_ref[v * ways + way, :, HALF + held :].astype(f32)
            sums.append(pieces[:, 0:4] + (pieces[:, 4:8] + pieces[:, 8:12]))
        for g in range(HALF // HD):
            mine = slice(g * 2 * SUB, (g + 1) * 2 * SUB)
            own_sum = ownsum_ref[v, mine, :]
            wide = [jnp.broadcast_to(one[:, g : g + 1], (2 * SUB, HD)) for one in sums]
            highest = functools.reduce(jnp.maximum, wide, own_sum)
            weight = jnp.exp2(own_sum - highest)
            total = weight
            value = weight * own_ref[v, mine, :]
            for way in range(ways):
                weight = jnp.exp2(wide[way] - highest)
                total = total + weight
                value = value + weight * back_ref[v * ways + way, :, g * HD : (g + 1) * HD].astype(f32)
            value = value / total
            start = v * 2 * HALF + g * HD
            attended[:, start : start + HD] = value[:SUB]
            attended[:, start + HALF : start + HALF + HD] = value[SUB:]
    for i in range(rows):
        attention_ref[i] = attended[i * steps : (i + 1) * steps, :].astype(bf16)


def call(kernel, out_shape, in_spaces, out_spaces, scratch, cost, aliases=None):
    def spec(space):
        return pl.BlockSpec(memory_space=space)

    return pl.pallas_call(
        kernel,
        out_shape=out_shape,
        in_specs=[spec(space) for space in in_spaces],
        out_specs=jax.tree.map(spec, out_spaces),
        scratch_shapes=scratch,
        input_output_aliases=aliases or {},
        compiler_params=pltpu.CompilerParams(vmem_limit_bytes=VMEM_LIMIT),
        cost_estimate=pl.CostEstimate(flops=cost[0], bytes_accessed=cost[1], transcendentals=0),
    )


def on_device(
    prompt_x,
    prompt_b,
    prompt_c,
    prompt_dt,
    decay_rate,
    skip_gain,
    lengths,
    owner_list,
    page_table,
    cache_pages,
    row_slot,
    step_x,
    step_b,
    step_c,
    step_dt,
    queries,
    fresh_cache,
):
    owners = lax.axis_size("heads")
    ways = owners // KVH
    group, prompts, length = prompt_dt.shape
    width = prompt_x.shape[1]
    keys = cache_pages.shape[0] * PAGE
    rows, steps = step_x.shape[0], step_x.shape[1]
    held = projected_columns(width)
    all_rows = owners * 2 * SUB
    shape = jax.ShapeDtypeStruct
    smem, vmem, anywhere = pltpu.SMEM, pltpu.VMEM, pl.ANY
    sem = pltpu.SemaphoreType.DMA((prompts,))
    levels = len(LEVELS)

    send = call(
        functools.partial(pack_kernel, group, ways),
        shape((owners, 2 * SUB, HALF + LANES), bf16),
        [vmem, vmem],
        vmem,
        [vmem((SUB, queries.shape[2]), f32), vmem((SUB, step_c.shape[2]), f32)],
        (0, 1 << 19),
    )(queries, step_c)
    recv = lax.all_to_all(send, "heads", split_axis=0, concat_axis=0, tiled=True)

    block = [
        vmem((prompts, width, length), bf16),
        vmem((prompts, length, NS), bf16),
        vmem((prompts, length, NS), bf16),
        vmem((prompts, width, length), bf16),
        vmem((levels, prompts, group, length), f32),
        vmem((levels, prompts, group, length), f32),
        vmem((prompts, group, length), f32),
    ]
    masks = vmem((levels, length, length), bf16)
    work = 2 * width * length * NS
    states, tag, requests, early_out = call(
        state_kernel,
        (
            shape((prompts, width, NS), bf16),
            shape((SUB, LANES), jnp.int32),
            shape((all_rows, LANES), jnp.int32),
            shape(prompt_x.shape, bf16),
        ),
        [smem] * 6 + [vmem] + [anywhere] * 3,
        (vmem, vmem, vmem, anywhere),
        block + [vmem((prompts, group, length), f32), masks, sem, sem, sem, sem],
        (work * (prompts + 5 * EARLY), 6 << 20),
    )(
        decay_rate,
        skip_gain,
        lengths,
        owner_list,
        page_table,
        row_slot,
        prompt_dt,
        prompt_x,
        prompt_b,
        prompt_c,
    )

    back = call(
        serve_kernel,
        shape((all_rows, HALF + held + LANES), bf16),
        [vmem] * 5,
        vmem,
        [vmem((all_rows, keys), f32)],
        (8 * all_rows * keys * HD, 4 << 20),
    )(
        recv.reshape(all_rows, HALF + LANES),
        cache_pages.reshape(keys, 2 * HD),
        tag,
        requests,
        states,
    )
    returned = lax.all_to_all(
        back.reshape(owners, 2 * SUB, back.shape[1]), "heads", split_axis=0, concat_axis=0, tiled=True
    )

    count = HALF // HD * 2 * SUB
    channels = step_x.shape[2]
    prompt_out, own, own_sum, fade, local = call(
        prompt_kernel,
        (
            shape(prompt_x.shape, bf16),
            shape((KVH, count, HD), f32),
            shape((KVH, count, HD), f32),
            shape((SUB, channels), f32),
            shape((SUB, channels), f32),
        ),
        [smem] * 3 + [vmem] * 9 + [anywhere] * 5,
        (anywhere, vmem, vmem, vmem, vmem),
        block
        + [
            masks,
            vmem((SUB, fresh_cache.shape[2]), f32),
            vmem((SUB, step_c.shape[2]), f32),
            vmem((steps, SUB, channels), f32),
            sem,
            sem,
            sem,
            sem,
        ],
        (work * 5 * (prompts - EARLY), 8 << 20),
        {16: 0},
    )(
        decay_rate,
        skip_gain,
        lengths,
        prompt_dt,
        decay_rate.reshape(1, -1),
        skip_gain.reshape(1, -1),
        send,
        fresh_cache,
        step_x,
        step_b,
        step_c,
        step_dt,
        prompt_x,
        prompt_b,
        prompt_c,
        back,
        early_out,
    )

    mixer_out, attention_out = call(
        functools.partial(merge_kernel, width),
        (shape(step_x.shape, bf16), shape(queries.shape, bf16)),
        [vmem] * 5,
        (vmem, vmem),
        [vmem((SUB, channels), f32), vmem((SUB, queries.shape[2]), f32)],
        (0, 2 << 20),
    )(returned, own, own_sum, fade, local)
    return (prompt_out, mixer_out, attention_out)


def solution(mesh):
    in_specs = (
        P("groups", "heads", None),
        P("groups", None, None),
        P("groups", None, None),
        P("heads", "groups", None),
        P(),
        P(),
        P("groups"),
        P("groups", None),
        P("groups", None),
        P(("groups", "heads"), None, None),
        P("groups"),
        P(("groups", "heads"), None, None),
        P(("groups", "heads"), None, None),
        P(("groups", "heads"), None, None),
        P(("groups", "heads"), None, None),
        P(("groups", "heads"), None, None),
        P(("groups", "heads"), None, None),
    )
    out_specs = (
        P("groups", "heads", None),
        P(("groups", "heads"), None, None),
        P(("groups", "heads"), None, None),
    )
    return jax.shard_map(
        on_device, mesh=mesh, in_specs=in_specs, out_specs=out_specs, check_vma=False
    )
```

profile of v0, /device:TPU:0, one launch (start us, length us, event | category | flops | bytes accessed | tf_op | source)
XLA Modules:
  0.0 56.4 jit_solution(12540241775694120770)
XLA Ops:
  0.6 0.7 %copy.22.c_ref.sc_ref = bf16[2,3,1024]{2,1,0:T(4,128)(2,1)S(1)} copy(bf16[2,3,1024]{2,0,1:T(2,128)(2,1)} %param.30) | data formatting | bytes 24576 | tf_op args[13]
  1.3 1.0 %copy.21.q_ref = bf16[2,3,8192]{2,1,0:T(4,128)(2,1)S(1)} copy(bf16[2,3,8192]{2,0,1:T(2,128)(2,1)} %param.32) | data formatting | bytes 196608 | tf_op args[15]
  2.3 0.8 %shard_map.184.send_ref = bf16[16,16,640]{2,1,0:T(8,128)(2,1)} custom-call(bf16[2,3,8192]{2,1,0:T(4,128)(2,1)S(1)} %copy.21.q_ref, bf16[2,3,1024]{2,1,0:T(4,128)(2,1)S(1)} %copy.22.c_ref.sc_ref), custom_call_target="tpu_custom_call" | custom-call | bytes 524288 | tf_op jit(solution)/shard_map/pallas_call | solution.py:557
  3.1 7.4 %all-to-all-start = ((bf16[16,16,640]{2,1,0:T(8,128)(2,1)}), bf16[16,16,640]{2,1,0:T(8,128)(2,1)S(1)}, u32[]{:S(2)}, u32[]{:S(2)}) async-start(bf16[16,16,640]{2,1,0:T(8,128)(2,1)} %shard_map.184.send_ref), calls=%async_computation | async-start | bytes 655360 | tf_op jit(solution)/shard_map/all_to_all | solution.py:565
  10.5 0.8 %copy.23.owner_ref = s32[16,2]{1,0:T(8,128)S(1)} copy(s32[16,2]{0,1:T(2,128)} %param.24) | data formatting | bytes 256 | tf_op args[7]
  11.3 2.2 %copy-done = bf16[8,256,1024]{2,1,0:T(8,128)(2,1)S(1)} copy-done((bf16[8,256,1024]{2,1,0:T(8,128)(2,1)S(1)}, bf16[8,256,1024]{2,1,0:T(8,128)(2,1)}, u32[]{:S(2)}) %copy-start) | copy-done | bytes 4194328
  13.5 2.2 %copy-done.2 = bf16[8,256,1024]{2,1,0:T(8,128)(2,1)S(1)} copy-done((bf16[8,256,1024]{2,1,0:T(8,128)(2,1)S(1)}, bf16[8,256,1024]{2,1,0:T(8,128)(2,1)}, u32[]{:S(2)}) %copy-start.2) | copy-done | bytes 4194328
  15.7 1.6 %copy-done.4 = bf16[8,512,256]{2,1,0:T(8,128)(2,1)S(1)} copy-done((bf16[8,512,256]{2,1,0:T(8,128)(2,1)S(1)}, bf16[8,512,256]{2,1,0:T(8,128)(2,1)}, u32[]{:S(2)}) %copy-start.4) | copy-done | bytes 2097176
  17.3 0.8 %copy-done.11 = bf16[8,8,256]{2,1,0:T(8,128)(2,1)S(1)} copy-done((bf16[8,8,256]{2,1,0:T(8,128)(2,1)S(1)}, bf16[8,8,256]{2,1,0:T(8,128)(2,1)}, u32[]{:S(2)}) %copy-start.11) | copy-done | bytes 32792
  19.3 0.7 %copy-done.17 = s32[8,128]{1,0:T(8,128)S(1)} copy-done((s32[8,128]{1,0:T(8,128)S(1)}, s32[8,128]{1,0:T(8,128)}, u32[]{:S(2)}) %copy-start.17) | copy-done | bytes 4120
  21.3 6.1 %shard_map.185 = (bf16[8,512,256]{2,1,0:T(8,128)(2,1)S(1)}, s32[8,128]{1,0:T(8,128)S(1)}, s32[256,128]{1,0:T(8,128)S(1)}, bf16[8,512,256]{2,1,0:T(8,128)(2,1)}) custom-call(f32[128]{0:T(128)S(1)} %copy-done.13, f32[128]{0:T(128)S(1)} %copy-done.15, s32[8]{0:T(128)S(1)} %copy-done.18, s32[16,2]{1,0:T(8,128)S(1)} %copy.23.owner_ref, s32[8,128]{1,0:T(8,128)S(1)} %copy-done.17, ...), custom_call_target="tpu_custom_call" | custom-call | flops 1207959552 | bytes 6291456 | tf_op jit(solution)/shard_map/pallas_call | solution.py:578
  27.5 1.3 %copy-done.6 = bf16[8,512,256]{2,1,0:T(8,128)(2,1)} copy-done((bf16[8,512,256]{2,1,0:T(8,128)(2,1)}, bf16[8,512,256]{2,1,0:T(8,128)(2,1)S(1)}, u32[]{:S(2)}) %copy-start.6) | copy-done | bytes 2097176
  28.8 1.6 %copy-done.7 = bf16[8,512,256]{2,1,0:T(8,128)(2,1)S(1)} copy-done((bf16[8,512,256]{2,1,0:T(8,128)(2,1)S(1)}, bf16[8,512,256]{2,1,0:T(8,128)(2,1)}, u32[]{:S(2)}) %copy-start.7) | copy-done | bytes 2097176
  30.5 3.6 %shard_map.186.after_any = bf16[256,896]{1,0:T(8,128)(2,1)} custom-call(bf16[256,640]{1,0:T(8,128)(2,1)S(1)} %bitcast.5, bf16[1024,256]{1,0:T(8,128)(2,1)S(1)} %bitcast.6, s32[8,128]{1,0:T(8,128)S(1)} %get-tuple-element.14.tag_ref, s32[256,128]{1,0:T(8,128)S(1)} %get-tuple-element.15.req_ref, bf16[8,512,256]{2,1,0:T(8,128)(2,1)S(1)} %copy-done.7), custom_call_target="tpu_custom_call" | custom-call | flops 268435456 | bytes 4194304 | tf_op jit(solution)/shard_map/pallas_call | solution.py:603
  34.0 6.0 %all-to-all-start.1 = ((bf16[16,16,896]{2,1,0:T(8,128)(2,1)}), bf16[16,16,896]{2,1,0:T(8,128)(2,1)S(1)}, u32[]{:S(2)}, u32[]{:S(2)}) async-start(bf16[16,16,896]{2,1,0:T(8,128)(2,1)} %bitcast.4), calls=%async_computation.1 | async-start | bytes 917504 | tf_op jit(solution)/shard_map/all_to_all | solution.py:617
  40.3 2.2 %copy-done.1 = bf16[8,256,1024]{2,1,0:T(8,128)(2,1)S(1)} copy-done((bf16[8,256,1024]{2,1,0:T(8,128)(2,1)S(1)}, bf16[8,256,1024]{2,1,0:T(8,128)(2,1)}, u32[]{:S(2)}) %copy-start.1) | copy-done | bytes 4194328
  42.5 2.2 %copy-done.3 = bf16[8,256,1024]{2,1,0:T(8,128)(2,1)S(1)} copy-done((bf16[8,256,1024]{2,1,0:T(8,128)(2,1)S(1)}, bf16[8,256,1024]{2,1,0:T(8,128)(2,1)}, u32[]{:S(2)}) %copy-start.3) | copy-done | bytes 4194328
  44.7 7.3 %shard_map.187 = (bf16[8,512,256]{2,1,0:T(8,128)(2,1)}, f32[8,64,128]{2,1,0:T(8,128)S(1)}, f32[8,64,128]{2,1,0:T(8,128)S(1)}, f32[8,8192]{1,0:T(8,128)S(1)}, f32[8,8192]{1,0:T(8,128)S(1)}) custom-call(f32[128]{0:T(128)S(1)} %copy-done.14, f32[128]{0:T(128)S(1)} %copy-done.16, s32[8]{0:T(128)S(1)} %copy-done.19, ...), custom_call_target="tpu_custom_call", output_to_operand_aliasing={{0}: (16, {})} | custom-call | flops 2013265920 | bytes 8388608 | tf_op jit(solution)/shard_map/pallas_call | solution.py:623
  51.9 0.7 %copy-done.9 = f32[8,8192]{1,0:T(8,128)} copy-done((f32[8,8192]{1,0:T(8,128)}, f32[8,8192]{1,0:T(8,128)S(1)}, u32[]{:S(2)}) %copy-start.9) | copy-done | bytes 262168
  52.6 0.7 %all-to-all-done.1.back_ref = bf16[16,16,896]{2,1,0:T(8,128)(2,1)S(1)} async-done(((bf16[16,16,896]{2,1,0:T(8,128)(2,1)}), bf16[16,16,896]{2,1,0:T(8,128)(2,1)S(1)}, u32[]{:S(2)}, u32[]{:S(2)}) %all-to-all-start.1) | async-done | bytes 458784 | tf_op jit(solution)/shard_map/all_to_all | solution.py:617
  53.3 0.9 %copy-done.10 = f32[8,8192]{1,0:T(8,128)S(1)} copy-done((f32[8,8192]{1,0:T(8,128)S(1)}, f32[8,8192]{1,0:T(8,128)}, u32[]{:S(2)}) %copy-start.10) | copy-done | bytes 262168
  54.2 0.7 %shard_map.188 = (bf16[2,3,8192]{2,1,0:T(4,128)(2,1)S(1)}, bf16[2,3,8192]{2,1,0:T(4,128)(2,1)S(1)}) custom-call(bf16[16,16,896]{2,1,0:T(8,128)(2,1)S(1)} %all-to-all-done.1.back_ref, f32[8,64,128]{2,1,0:T(8,128)S(1)} %get-tuple-element.19.own_ref, f32[8,64,128]{2,1,0:T(8,128)S(1)} %get-tuple-element.20.ownsum_ref, f32[8,8192]{1,0:T(8,128)S(1)} %get-tuple-element.21.fade_ref, ...), custom_call_target="tpu_custom_call" | custom-call | bytes 2097152 | tf_op jit(solution)/shard_map/pallas_call | solution.py:667
  54.9 0.8 %copy.29 = bf16[2,3,8192]{2,0,1:T(2,128)(2,1)} copy(bf16[2,3,8192]{2,1,0:T(4,128)(2,1)S(1)} %get-tuple-element.26) | data formatting | bytes 196608
  55.7 0.8 %copy.30 = bf16[2,3,8192]{2,0,1:T(2,128)(2,1)} copy(bf16[2,3,8192]{2,1,0:T(4,128)(2,1)S(1)} %get-tuple-element.27) | data formatting | bytes 196608
  (44 shorter events, 2.8 us)
Async XLA Ops:
  3.1 25.7 %all-to-all-start = ((bf16[16,16,640]{2,1,0:T(8,128)(2,1)}), bf16[16,16,640]{2,1,0:T(8,128)(2,1)S(1)}, u32[]{:S(2)}, u32[]{:S(2)}) async-start(bf16[16,16,640]{2,1,0:T(8,128)(2,1)} %shard_map.184.send_ref), calls=%async_computation | async-start | bytes 655360 | tf_op jit(solution)/shard_map/all_to_all | solution.py:565
  11.3 2.2 %copy-start = (bf16[8,256,1024]{2,1,0:T(8,128)(2,1)S(1)}, bf16[8,256,1024]{2,1,0:T(8,128)(2,1)}, u32[]{:S(2)}) copy-start(bf16[8,256,1024]{2,1,0:T(8,128)(2,1)} %b_any.3) | copy-start | bytes 12582916
  13.5 2.2 %copy-start.2 = (bf16[8,256,1024]{2,1,0:T(8,128)(2,1)S(1)}, bf16[8,256,1024]{2,1,0:T(8,128)(2,1)}, u32[]{:S(2)}) copy-start(bf16[8,256,1024]{2,1,0:T(8,128)(2,1)} %c_any.3) | copy-start | bytes 12582916
  15.7 1.6 %copy-start.4 = (bf16[8,512,256]{2,1,0:T(8,128)(2,1)S(1)}, bf16[8,512,256]{2,1,0:T(8,128)(2,1)}, u32[]{:S(2)}) copy-start(bf16[8,512,256]{2,1,0:T(8,128)(2,1)} %x_any.3) | copy-start | bytes 6291460
  17.3 0.8 %copy-start.11 = (bf16[8,8,256]{2,1,0:T(8,128)(2,1)S(1)}, bf16[8,8,256]{2,1,0:T(8,128)(2,1)}, u32[]{:S(2)}) copy-start(bf16[8,8,256]{2,1,0:T(8,128)(2,1)} %dt_ref.3) | copy-start | bytes 98308
  19.3 0.7 %copy-start.17 = (s32[8,128]{1,0:T(8,128)S(1)}, s32[8,128]{1,0:T(8,128)}, u32[]{:S(2)}) copy-start(s32[8,128]{1,0:T(8,128)} %table_ref.1) | copy-start | bytes 12292
  20.0 0.7 %copy-start.18 = (s32[8]{0:T(128)S(1)}, s32[8]{0:T(128)}, u32[]{:S(2)}) copy-start(s32[8]{0:T(128)} %len_ref.3) | copy-start | bytes 100
  21.3 7.5 %copy-start.8 = (bf16[64,16,256]{2,1,0:T(8,128)(2,1)S(1)}, bf16[64,16,256]{2,1,0:T(8,128)(2,1)}, u32[]{:S(2)}) copy-start(bf16[64,16,256]{2,1,0:T(8,128)(2,1)} %param.26) | copy-start | bytes 1572868
  27.4 1.3 %copy-start.6 = (bf16[8,512,256]{2,1,0:T(8,128)(2,1)}, bf16[8,512,256]{2,1,0:T(8,128)(2,1)S(1)}, u32[]{:S(2)}) copy-start(bf16[8,512,256]{2,1,0:T(8,128)(2,1)S(1)} %get-tuple-element.16.state_ref) | copy-start | bytes 6291460
  28.8 1.6 %copy-start.7 = (bf16[8,512,256]{2,1,0:T(8,128)(2,1)S(1)}, bf16[8,512,256]{2,1,0:T(8,128)(2,1)}, u32[]{:S(2)}) copy-start(bf16[8,512,256]{2,1,0:T(8,128)(2,1)} %copy-done.6) | copy-start | bytes 6291460
  30.4 9.7 %copy-start.21 = (bf16[2,3,8192]{2,0,1:T(2,128)(2,1)S(1)}, bf16[2,3,8192]{2,0,1:T(2,128)(2,1)}, u32[]{:S(2)}) copy-start(bf16[2,3,8192]{2,0,1:T(2,128)(2,1)} %param.28) | copy-start | bytes 294916
  30.4 9.8 %copy-start.22 = (bf16[2,3,2048]{2,0,1:T(2,128)(2,1)S(1)}, bf16[2,3,2048]{2,0,1:T(2,128)(2,1)}, u32[]{:S(2)}) copy-start(bf16[2,3,2048]{2,0,1:T(2,128)(2,1)} %param.33) | copy-start | bytes 73732
  30.4 9.8 %copy-start.23 = (bf16[2,3,1024]{2,0,1:T(2,128)(2,1)S(1)}, bf16[2,3,1024]{2,0,1:T(2,128)(2,1)}, u32[]{:S(2)}) copy-start(bf16[2,3,1024]{2,0,1:T(2,128)(2,1)} %param.29) | copy-start | bytes 36868
  30.4 9.8 %copy-start.24 = (bf16[2,3,128]{2,0,1:T(2,128)(2,1)S(1)}, bf16[2,3,128]{2,0,1:T(2,128)(2,1)}, u32[]{:S(2)}) copy-start(bf16[2,3,128]{2,0,1:T(2,128)(2,1)} %param.31) | copy-start | bytes 4612
  30.4 9.8 %copy-start.5 = (bf16[8,512,256]{2,1,0:T(8,128)(2,1)S(1)}, bf16[8,512,256]{2,1,0:T(8,128)(2,1)}, u32[]{:S(2)}) copy-start(bf16[8,512,256]{2,1,0:T(8,128)(2,1)} %x_any.3) | copy-start | bytes 6291460
  30.4 9.8 %copy-start.12 = (bf16[8,8,256]{2,1,0:T(8,128)(2,1)S(1)}, bf16[8,8,256]{2,1,0:T(8,128)(2,1)}, u32[]{:S(2)}) copy-start(bf16[8,8,256]{2,1,0:T(8,128)(2,1)} %dt_ref.3) | copy-start | bytes 98308
  30.4 9.8 %copy-start.14 = (f32[128]{0:T(128)S(1)}, f32[128]{0:T(128)}, u32[]{:S(2)}) copy-start(f32[128]{0:T(128)} %rate_ref.3) | copy-start | bytes 1540
  30.4 9.8 %copy-start.16 = (f32[128]{0:T(128)S(1)}, f32[128]{0:T(128)}, u32[]{:S(2)}) copy-start(f32[128]{0:T(128)} %skip_ref.3) | copy-start | bytes 1540
  30.4 9.8 %copy-start.19 = (s32[8]{0:T(128)S(1)}, s32[8]{0:T(128)}, u32[]{:S(2)}) copy-start(s32[8]{0:T(128)} %len_ref.3) | copy-start | bytes 100
  34.0 19.3 %all-to-all-start.1 = ((bf16[16,16,896]{2,1,0:T(8,128)(2,1)}), bf16[16,16,896]{2,1,0:T(8,128)(2,1)S(1)}, u32[]{:S(2)}, u32[]{:S(2)}) async-start(bf16[16,16,896]{2,1,0:T(8,128)(2,1)} %bitcast.4), calls=%async_computation.1 | async-start | bytes 917504 | tf_op jit(solution)/shard_map/all_to_all | solution.py:617
  40.3 2.2 %copy-start.1 = (bf16[8,256,1024]{2,1,0:T(8,128)(2,1)S(1)}, bf16[8,256,1024]{2,1,0:T(8,128)(2,1)}, u32[]{:S(2)}) copy-start(bf16[8,256,1024]{2,1,0:T(8,128)(2,1)} %b_any.3) | copy-start | bytes 12582916
  42.5 2.2 %copy-start.3 = (bf16[8,256,1024]{2,1,0:T(8,128)(2,1)S(1)}, bf16[8,256,1024]{2,1,0:T(8,128)(2,1)}, u32[]{:S(2)}) copy-start(bf16[8,256,1024]{2,1,0:T(8,128)(2,1)} %c_any.3) | copy-start | bytes 12582916
  51.9 0.7 %copy-start.9 = (f32[8,8192]{1,0:T(8,128)}, f32[8,8192]{1,0:T(8,128)S(1)}, u32[]{:S(2)}) copy-start(f32[8,8192]{1,0:T(8,128)S(1)} %get-tuple-element.22.local_ref) | copy-start | bytes 786436
  53.3 1.0 %copy-start.10 = (f32[8,8192]{1,0:T(8,128)S(1)}, f32[8,8192]{1,0:T(8,128)}, u32[]{:S(2)}) copy-start(f32[8,8192]{1,0:T(8,128)} %copy-done.9) | copy-start | bytes 786436
  (3 other events, 2.0 us)
where the time goes:
time: 57.3 us; the launch traced here: 56.4 us
  local copies, waits for them, and re-layouts  23.1 us (40%)
  Pallas kernels  18.4 us (32%)
  starting transfers between devices  13.4 us (23%)
  between operations  0.86 us (2%)
  waiting for transfers between devices  0.67 us (1%)
    unnamed x59, local copies, waits for them, and re-layouts  23.1 us
    all_to_all x1, starting transfers between devices, on_device(): lax.all_to_all(send, 'heads', split_axis=0, concat_axis=0, tiled=True)  7.39 us
    pallas_call x1, Pallas kernels, on_device(): call(prompt_kernel, (shape(prompt_x.shape, bf16), shape((KVH, count, HD),...  7.26 us
    pallas_call x1, Pallas kernels, on_device(): call(state_kernel, (shape((prompts, width, NS), bf16), shape((SUB, LANES)...  6.11 us
    all_to_all x1, starting transfers between devices, on_device(): lax.all_to_all(back.reshape(owners, 2 * SUB, back.shape[1]), 'heads', spl...  6.01 us
    pallas_call x1, Pallas kernels, on_device(): call(serve_kernel, shape((all_rows, HALF + held + LANES), bf16), [vmem] *...  3.56 us
  transfers between devices with their start and end apart: 2, of which 1 were waited for; matrix products, arithmetic and copies ran while one was open for 2% of the time, Pallas kernels for 24%

commit v1 on v0

--- a/solution.py
+++ b/solution.py
@@ -23,7 +23,7 @@
 NONE = -1e30
 FLOOR = -1e29
 EARLY = 2
-VMEM_LIMIT = 40 * 1024 * 1024
+VMEM_LIMIT = 64 * 1024 * 1024
 
 f32 = jnp.float32
 bf16 = jnp.bfloat16
@@ -38,14 +38,23 @@
 
 
 def stack_rows(source, held):
-    rows, steps = source.shape[0], source.shape[1]
+    steps, rows = source.shape[0], source.shape[1]
     held[...] = jnp.zeros_like(held)
-    for i in range(rows):
-        held[i * steps : (i + 1) * steps, :] = source[i].astype(f32)
-
-
-def pack_kernel(group, ways, q_ref, c_ref, out_ref, q_held, c_held):
+    for k in range(steps):
+        held[k * rows : (k + 1) * rows, :] = source[k].astype(f32)
+
+
+def fetches(pairs, sems):
+    copies = [pltpu.make_async_copy(src, dst, sems.at[n]) for n, (src, dst) in enumerate(pairs)]
+    for copy in copies:
+        copy.start()
+    return copies
+
+
+def pack_kernel(group, ways, q_any, c_any, out_ref, q_ref, c_ref, q_held, c_held, sems):
     owners = out_ref.shape[0]
+    for copy in fetches([(q_any, q_ref), (c_any, c_ref)], sems):
+        copy.wait()
     stack_rows(q_ref, q_held)
     stack_rows(c_ref, c_held)
     span = 2 * HALF
@@ -136,17 +145,17 @@
 
 
 def state_kernel(
-    rate_ref,
-    skip_ref,
-    len_ref,
-    owner_ref,
-    table_ref,
-    slot_ref,
-    dt_ref,
+    rate_any,
+    skip_any,
+    len_any,
+    owner_any,
+    table_any,
+    slot_any,
+    dt_any,
     x_any,
     b_any,
     c_any,
-    state_ref,
+    state_any,
     tag_ref,
     req_ref,
     out_any,
@@ -159,12 +168,34 @@
     w_skip,
     w_tail,
     masks,
+    state_held,
+    rate_ref,
+    skip_ref,
+    len_ref,
+    owner_ref,
+    table_ref,
+    slot_ref,
+    dt_ref,
     x_sem,
     b_sem,
     c_sem,
     out_sem,
+    state_sem,
+    sems,
 ):
     group, prompts, length = dt_ref.shape
+    smalls = fetches(
+        [
+            (dt_any, dt_ref),
+            (rate_any, rate_ref),
+            (skip_any, skip_ref),
+            (len_any, len_ref),
+            (owner_any, owner_ref),
+            (table_any, table_ref),
+            (slot_any, slot_ref),
+        ],
+        sems,
+    )
     me = lax.axis_index("heads")
     first = me * group
     column = pl.multiple_of((first // HPG) * NS, NS)
@@ -180,18 +211,23 @@
 
     def out_copy(r):
         return pltpu.make_async_copy(out_held.at[r], out_any.at[r], out_sem.at[r])
+
+    def state_copy(r):
+        return pltpu.make_async_copy(state_held.at[r], state_any.at[r], state_sem.at[r])
 
     for r in range(prompts):
         x_copy(r).start()
         b_copy(r).start()
     for r in range(EARLY):
         c_copy(r).start()
+    for copy in smalls:
+        copy.wait()
 
     head_factors(
         first, dt_ref, rate_ref, skip_ref, len_ref, LEVELS if EARLY else (), w_in, w_out, w_skip, w_tail
     )
 
-    spread = table_ref.shape[1] // owner_ref.shape[0]
+    spread = table_ref.shape[1] // owner_ref.shape[1]
     key_page = iota((SUB, LANES), 0) * (LANES // PAGE) + iota((SUB, LANES), 1) // PAGE
     key_offset = iota((SUB, LANES), 1) % PAGE
     tag = jnp.full((SUB, LANES), -1, jnp.int32)
@@ -205,16 +241,15 @@
             tag = jnp.where(inside, r, tag)
     tag_ref[...] = tag
 
-    owners = owner_ref.shape[0]
+    owners = owner_ref.shape[1]
     rows_dev = slot_ref.shape[0] // owners
-    steps = 3
     inner = iota((2 * SUB, LANES), 0) % SUB
 
     def fill(s, _):
         block = jnp.full((2 * SUB, LANES), -2, jnp.int32)
         for i in range(rows_dev):
-            target = owner_ref[s, slot_ref[s * rows_dev + i]]
-            block = jnp.where((inner >= i * steps) & (inner < (i + 1) * steps), target, block)
+            target = owner_ref[slot_ref[s * rows_dev + i], s]
+            block = jnp.where(inner % rows_dev == i, target, block)
         req_ref[pl.ds(pl.multiple_of(s * 2 * SUB, 2 * SUB), 2 * SUB), :] = block
         return 0
 
@@ -226,10 +261,11 @@
         width = x_held.shape[1]
         inputs = x_held[r].astype(f32).reshape(group, HP, length)
         scaled = (inputs * w_tail[r][:, None, :]).astype(bf16).reshape(width, length)
-        state_ref[r] = jnp.dot(scaled, b_held[r], preferred_element_type=f32).astype(bf16)
+        state_held[r] = jnp.dot(scaled, b_held[r], preferred_element_type=f32).astype(bf16)
+        state_copy(r).start()
         return 0
 
-    lax.fori_loop(0, prompts, one, 0)
+    lax.fori_loop(0, prompts, one, 0, unroll=2)
 
     if EARLY:
         level_masks(masks)
@@ -240,12 +276,35 @@
             out_copy(r).start()
             return 0
 
-        lax.fori_loop(0, EARLY, early, 0)
+        lax.fori_loop(0, EARLY, early, 0, unroll=2)
         for r in range(EARLY):
             out_copy(r).wait()
-
-
-def serve_kernel(recv_ref, pages_ref, tag_ref, req_ref, state_ref, out_ref, bias):
+    for r in range(prompts):
+        state_copy(r).wait()
+
+
+def serve_kernel(
+    recv_any,
+    pages_any,
+    tag_any,
+    req_any,
+    state_any,
+    out_ref,
+    recv_ref,
+    pages_ref,
+    tag_ref,
+    req_ref,
+    state_ref,
+    bias,
+    state_sem,
+    sems,
+):
+    smalls = fetches(
+        [(tag_any, tag_ref), (req_any, req_ref), (pages_any, pages_ref), (recv_any, recv_ref)], sems
+    )
+    states = fetches([(state_any.at[r], state_ref.at[r]) for r in range(state_any.shape[0])], state_sem)
+    for copy in smalls:
+        copy.wait()
     rows = recv_ref.shape[0]
     keys = pages_ref.shape[0]
     prompts, width = state_ref.shape[0], state_ref.shape[1]
@@ -282,6 +341,7 @@
     found = jnp.zeros((blocks * SUB, width), f32)
     for r in range(prompts):
         picked = jnp.where(target == r, readout, 0.0).astype(bf16)
+        states[r].wait()
         found = found + dot_nt(picked, state_ref[r])
     if width == 2 * held:
         found = found.reshape(blocks, SUB, width)
@@ -298,18 +358,18 @@
 
 
 def prompt_kernel(
-    rate_ref,
-    skip_ref,
-    len_ref,
-    dt_ref,
-    rates_ref,
-    skips_ref,
-    send_ref,
-    fresh_ref,
-    sx_ref,
-    sb_ref,
-    sc_ref,
-    sdt_ref,
+    rate_any,
+    skip_any,
+    len_any,
+    dt_any,
+    rates_any,
+    skips_any,
+    send_any,
+    fresh_any,
+    sx_any,
+    sb_any,
+    sc_any,
+    sdt_any,
     x_any,
     b_any,
     c_any,
@@ -331,12 +391,42 @@
     fresh_held,
     c_rows,
     x_rows,
+    rate_ref,
+    skip_ref,
+    len_ref,
+    dt_ref,
+    rates_ref,
+    skips_ref,
+    send_ref,
+    fresh_ref,
+    sx_ref,
+    sb_ref,
+    sc_ref,
+    sdt_ref,
     x_sem,
     b_sem,
     c_sem,
     out_sem,
+    sems,
 ):
     group, prompts, length = dt_ref.shape
+    smalls = fetches(
+        [
+            (dt_any, dt_ref),
+            (rate_any, rate_ref),
+            (skip_any, skip_ref),
+            (len_any, len_ref),
+            (rates_any, rates_ref),
+            (skips_any, skips_ref),
+            (send_any, send_ref),
+            (fresh_any, fresh_ref),
+            (sx_any, sx_ref),
+            (sb_any, sb_ref),
+            (sc_any, sc_ref),
+            (sdt_any, sdt_ref),
+        ],
+        sems,
+    )
     me = lax.axis_index("heads")
     first = me * group
     column = pl.multiple_of((first // HPG) * NS, NS)
@@ -357,6 +447,8 @@
         x_copy(r).start()
         b_copy(r).start()
         c_copy(r).start()
+    for copy in smalls:
+        copy.wait()
 
     head_factors(first, dt_ref, rate_ref, skip_ref, len_ref, LEVELS, w_in, w_out, w_skip, None)
     level_masks(masks)
@@ -369,7 +461,7 @@
         out_copy(r).start()
         return 0
 
-    lax.fori_loop(EARLY, prompts, one, 0)
+    lax.fori_loop(EARLY, prompts, one, 0, unroll=2)
     own_attention(send_ref, fresh_ref, fresh_held, own_ref, ownsum_ref)
     own_mixer(rates_ref, skips_ref, sx_ref, sb_ref, sc_ref, sdt_ref, c_rows, x_rows, fade_ref, local_ref)
     for r in range(EARLY, prompts):
@@ -377,13 +469,13 @@
 
 
 def own_attention(send_ref, fresh_ref, fresh_held, own_ref, ownsum_ref):
-    rows, steps = fresh_ref.shape[0], fresh_ref.shape[1]
+    steps, rows = fresh_ref.shape[0], fresh_ref.shape[1]
     ways = send_ref.shape[0] // KVH
     stack_rows(fresh_ref, fresh_held)
     count = HALF // HD * 2 * SUB
     pair = iota((count, SUB), 0) % SUB
     key = iota((count, SUB), 1)
-    seen = (key // steps == pair // steps) & (key <= pair) & (key < rows * steps)
+    seen = (key % rows == pair % rows) & (key <= pair) & (key < rows * steps)
     seen = seen | ((pair >= rows * steps) & (key == 0))
     for v in range(KVH):
         block = send_ref[v * ways]
@@ -400,26 +492,20 @@
 
 
 def own_mixer(rates_ref, skips_ref, sx_ref, sb_ref, sc_ref, sdt_ref, c_rows, x_rows, fade_ref, local_ref):
-    rows, steps, heads = sdt_ref.shape
+    steps, rows, heads = sdt_ref.shape
     stack_rows(sc_ref, c_rows)
     for u in range(steps):
-        x_rows[u] = jnp.zeros(x_rows.shape[1:], f32)
-        for i in range(rows):
-            x_rows[u, i * steps : (i + 1) * steps, :] = jnp.broadcast_to(
-                sx_ref[i, u : u + 1, :].astype(f32), (steps, x_rows.shape[2])
-            )
+        given = sx_ref[u].astype(f32)
+        for k in range(SUB // rows):
+            x_rows[u, k * rows : (k + 1) * rows, :] = given
     pair = iota((SUB, heads), 0)
-    step = pair % steps
+    step = pair // rows
     live = pair < rows * steps
     head = iota((SUB, heads), 1)
 
     def spread_rows(ref, u):
-        picked = jnp.broadcast_to(ref[0, u : u + 1, :].astype(f32), (SUB, ref.shape[2]))
-        which = iota(picked.shape, 0) // steps
-        for i in range(1, rows):
-            other = jnp.broadcast_to(ref[i, u : u + 1, :].astype(f32), (SUB, ref.shape[2]))
-            picked = jnp.where(which == i, other, picked)
-        return picked
+        given = ref[u].astype(f32)
+        return jnp.concatenate([given] * (SUB // rows), axis=0)
 
     rates = jnp.broadcast_to(rates_ref[...], (SUB, heads)) * LOG2E
     skips = jnp.broadcast_to(skips_ref[...], (SUB, heads))
@@ -459,12 +545,39 @@
 
 
 def merge_kernel(
-    width, back_ref, own_ref, ownsum_ref, fade_ref, local_ref, mixer_ref, attention_ref, mixed, attended
+    width,
+    back_any,
+    own_any,
+    ownsum_any,
+    fade_any,
+    local_any,
+    mixer_ref,
+    attention_ref,
+    back_ref,
+    own_ref,
+    ownsum_ref,
+    fade_ref,
+    local_ref,
+    mixed,
+    attended,
+    sems,
 ):
+    copies = fetches(
+        [
+            (back_any, back_ref),
+            (own_any, own_ref),
+            (ownsum_any, ownsum_ref),
+            (fade_any, fade_ref),
+            (local_any, local_ref),
+        ],
+        sems,
+    )
+    for copy in copies:
+        copy.wait()
     owners = back_ref.shape[0]
     ways = owners // KVH
     held = projected_columns(width)
-    rows, steps = mixer_ref.shape[0], mixer_ref.shape[1]
+    steps, rows = mixer_ref.shape[0], mixer_ref.shape[1]
     if width == 2 * held:
         for d in range(owners):
             for half in range(2):
@@ -479,8 +592,8 @@
             )
             columns = slice(d * width, (d + many) * width)
             mixed[:, columns] = found * fade_ref[:, columns] + local_ref[:, columns]
-    for i in range(rows):
-        mixer_ref[i] = mixed[i * steps : (i + 1) * steps, :].astype(bf16)
+    for k in range(steps):
+        mixer_ref[k] = mixed[k * rows : (k + 1) * rows, :].astype(bf16)
     for v in range(KVH):
         sums = []
         for way in range(ways):
@@ -502,8 +615,8 @@
             start = v * 2 * HALF + g * HD
             attended[:, start : start + HD] = value[:SUB]
             attended[:, start + HALF : start + HALF + HD] = value[SUB:]
-    for i in range(rows):
-        attention_ref[i] = attended[i * steps : (i + 1) * steps, :].astype(bf16)
+    for k in range(steps):
+        attention_ref[k] = attended[k * rows : (k + 1) * rows, :].astype(bf16)
 
 
 def call(kernel, out_shape, in_spaces, out_spaces, scratch, cost, aliases=None):
@@ -546,20 +659,36 @@
     group, prompts, length = prompt_dt.shape
     width = prompt_x.shape[1]
     keys = cache_pages.shape[0] * PAGE
-    rows, steps = step_x.shape[0], step_x.shape[1]
+    steps = step_x.shape[1]
     held = projected_columns(width)
     all_rows = owners * 2 * SUB
     shape = jax.ShapeDtypeStruct
-    smem, vmem, anywhere = pltpu.SMEM, pltpu.VMEM, pl.ANY
+    smem, vmem, hbm = pltpu.SMEM, pltpu.VMEM, pltpu.HBM
     sem = pltpu.SemaphoreType.DMA((prompts,))
     levels = len(LEVELS)
+    step_x, step_b, step_c, step_dt, queries, fresh_cache = (
+        jnp.swapaxes(one, 0, 1) for one in (step_x, step_b, step_c, step_dt, queries, fresh_cache)
+    )
+    owner_list = owner_list.T
+
+    def like(space, array):
+        return space(array.shape, array.dtype)
+
+    def sems(count):
+        return pltpu.SemaphoreType.DMA((count,))
 
     send = call(
         functools.partial(pack_kernel, group, ways),
         shape((owners, 2 * SUB, HALF + LANES), bf16),
-        [vmem, vmem],
+        [hbm, hbm],
         vmem,
-        [vmem((SUB, queries.shape[2]), f32), vmem((SUB, step_c.shape[2]), f32)],
+        [
+            like(vmem, queries),
+            like(vmem, step_c),
+            vmem((SUB, queries.shape[2]), f32),
+            vmem((SUB, step_c.shape[2]), f32),
+            sems(2),
+        ],
         (0, 1 << 19),
     )(queries, step_c)
     recv = lax.all_to_all(send, "heads", split_axis=0, concat_axis=0, tiled=True)
@@ -583,9 +712,12 @@
             shape((all_rows, LANES), jnp.int32),
             shape(prompt_x.shape, bf16),
         ),
-        [smem] * 6 + [vmem] + [anywhere] * 3,
-        (vmem, vmem, vmem, anywhere),
-        block + [vmem((prompts, group, length), f32), masks, sem, sem, sem, sem],
+        [hbm] * 10,
+        (hbm, vmem, vmem, hbm),
+        block
+        + [vmem((prompts, group, length), f32), masks, vmem((prompts, width, NS), bf16)]
+        + [like(smem, one) for one in (decay_rate, skip_gain, lengths, owner_list, page_table, row_slot)]
+        + [like(vmem, prompt_dt), sem, sem, sem, sem, sem, sems(7)],
         (work * (prompts + 5 * EARLY), 6 << 20),
     )(
         decay_rate,
@@ -603,9 +735,18 @@
     back = call(
         serve_kernel,
         shape((all_rows, HALF + held + LANES), bf16),
-        [vmem] * 5,
+        [hbm] * 5,
         vmem,
-        [vmem((all_rows, keys), f32)],
+        [
+            vmem((all_rows, HALF + LANES), bf16),
+            vmem((keys, 2 * HD), bf16),
+            like(vmem, tag),
+            like(vmem, requests),
+            like(vmem, states),
+            vmem((all_rows, keys), f32),
+            sem,
+            sems(4),
+        ],
         (8 * all_rows * keys * HD, 4 << 20),
     )(
         recv.reshape(all_rows, HALF + LANES),
@@ -620,6 +761,7 @@
 
     count = HALF // HD * 2 * SUB
     channels = step_x.shape[2]
+    rates, skips = decay_rate.reshape(1, -1), skip_gain.reshape(1, -1)
     prompt_out, own, own_sum, fade, local = call(
         prompt_kernel,
         (
@@ -629,18 +771,31 @@
             shape((SUB, channels), f32),
             shape((SUB, channels), f32),
         ),
-        [smem] * 3 + [vmem] * 9 + [anywhere] * 5,
-        (anywhere, vmem, vmem, vmem, vmem),
+        [hbm] * 17,
+        (hbm, vmem, vmem, vmem, vmem),
         block
         + [
             masks,
             vmem((SUB, fresh_cache.shape[2]), f32),
             vmem((SUB, step_c.shape[2]), f32),
             vmem((steps, SUB, channels), f32),
+            like(smem, decay_rate),
+            like(smem, skip_gain),
+            like(smem, lengths),
+            like(vmem, prompt_dt),
+            like(vmem, rates),
+            like(vmem, skips),
+            like(vmem, send),
+            like(vmem, fresh_cache),
+            like(vmem, step_x),
+            like(vmem, step_b),
+            like(vmem, step_c),
+            like(vmem, step_dt),
             sem,
             sem,
             sem,
             sem,
+            sems(12),
         ],
         (work * 5 * (prompts - EARLY), 8 << 20),
         {16: 0},
@@ -649,8 +804,8 @@
         skip_gain,
         lengths,
         prompt_dt,
-        decay_rate.reshape(1, -1),
-        skip_gain.reshape(1, -1),
+        rates,
+        skips,
         send,
         fresh_cache,
         step_x,
@@ -667,12 +822,13 @@
     mixer_out, attention_out = call(
         functools.partial(merge_kernel, width),
         (shape(step_x.shape, bf16), shape(queries.shape, bf16)),
-        [vmem] * 5,
+        [hbm] * 5,
         (vmem, vmem),
-        [vmem((SUB, channels), f32), vmem((SUB, queries.shape[2]), f32)],
+        [like(vmem, one) for one in (returned, own, own_sum, fade, local)]
+        + [vmem((SUB, channels), f32), vmem((SUB, queries.shape[2]), f32), sems(5)],
         (0, 2 << 20),
     )(returned, own, own_sum, fade, local)
-    return (prompt_out, mixer_out, attention_out)
+    return (prompt_out, jnp.swapaxes(mixer_out, 0, 1), jnp.swapaxes(attention_out, 0, 1))
 
 
 def solution(mesh):

time: 57.3 us -> 47.4 us (0.83)
  local copies, waits for them, and re-layouts: 23.1 us -> 0 us
  waiting for transfers between devices: 0.67 us -> 8.72 us
  Pallas kernels: 18.4 us -> 25.9 us
  starting transfers between devices: 13.4 us -> 11.7 us
    unnamed x59 -> x0, local copies, waits for them, and re-layouts: 23.1 us -> none
    all_to_all x1, waiting for transfers between devices: 0.01 us -> 4.15 us  [on_device(): lax.all_to_all(send, 'heads', split_axis=0, concat_axis=0, tiled=True)]
    all_to_all x1, waiting for transfers between devices: 0.66 us -> 4.57 us  [on_device(): lax.all_to_all(back.reshape(owners, 2 * SUB, back.shape[1]), 'heads', spl...]
    pallas_call x1, Pallas kernels: 3.56 us -> 5.78 us  [on_device(): call(serve_kernel, shape((all_rows, HALF + held + LANES), bf16), [hbm] *...]
    pallas_call x1, Pallas kernels: 0.67 us -> 2.68 us  [on_device(): call(functools.partial(merge_kernel, width), (shape(step_x.shape, bf16),...]
    all_to_all x1, starting transfers between devices: 6.01 us -> 4.24 us  [on_device(): lax.all_to_all(back.reshape(owners, 2 * SUB, back.shape[1]), 'heads', spl...]
    pallas_call x1, Pallas kernels: 7.26 us -> 8.68 us  [on_device(): call(prompt_kernel, (shape(prompt_x.shape, bf16), shape((KVH, count, HD),...]
    pallas_call x1, Pallas kernels: 0.8 us -> 1.75 us  [on_device(): call(functools.partial(pack_kernel, group, ways), shape((owners, 2 * SUB,...]
  transfers between devices with their start and end apart: 2 -> 2, of which waited for: 1 -> 2; matrix products, arithmetic and copies ran while one was open for 2% -> 0% of each run, Pallas kernels for 24% -> 33%
where the time goes in v1:
time: 47.4 us; the launch traced here: 47 us
  Pallas kernels  25.9 us (55%)
  starting transfers between devices  11.7 us (25%)
  waiting for transfers between devices  8.72 us (18%)
  between operations  0.68 us (1%)
    pallas_call x1, Pallas kernels, on_device(): call(prompt_kernel, (shape(prompt_x.shape, bf16), shape((KVH, count, HD),...  8.68 us
    all_to_all x1, starting transfers between devices, on_device(): lax.all_to_all(send, 'heads', split_axis=0, concat_axis=0, tiled=True)  7.44 us
    pallas_call x1, Pallas kernels, on_device(): call(state_kernel, (shape((prompts, width, NS), bf16), shape((SUB, LANES)...  7 us
    pallas_call x1, Pallas kernels, on_device(): call(serve_kernel, shape((all_rows, HALF + held + LANES), bf16), [hbm] *...  5.78 us
    all_to_all x1, waiting for transfers between devices, on_device(): lax.all_to_all(back.reshape(owners, 2 * SUB, back.shape[1]), 'heads', spl...  4.57 us
    all_to_all x1, starting transfers between devices, on_device(): lax.all_to_all(back.reshape(owners, 2 * SUB, back.shape[1]), 'heads', spl...  4.24 us
    all_to_all x1, waiting for transfers between devices, on_device(): lax.all_to_all(send, 'heads', split_axis=0, concat_axis=0, tiled=True)  4.15 us
    pallas_call x1, Pallas kernels, on_device(): call(functools.partial(merge_kernel, width), (shape(step_x.shape, bf16),...  2.68 us
  transfers between devices with their start and end apart: 2, of which 2 were waited for; matrix products, arithmetic and copies ran while one was open for 0% of the time, Pallas kernels for 33%

profile of v1, /device:TPU:0, one launch (start us, length us, event | category | flops | bytes accessed | tf_op | source)
XLA Modules:
  0.0 47.0 jit_solution(4457791439368564257)
XLA Ops:
  0.6 1.7 %shard_map.184.send_any = bf16[16,16,640]{2,1,0:T(8,128)(2,1)} custom-call(bf16[3,2,8192]{2,1,0:T(2,128)(2,1)} %bitcast.17, bf16[3,2,1024]{2,1,0:T(2,128)(2,1)} %bitcast.18), custom_call_target="tpu_custom_call" | custom-call | bytes 524288 | tf_op jit(solution)/shard_map/pallas_call | solution.py:680
  2.4 7.4 %all-to-all-start = ((bf16[16,16,640]{2,1,0:T(8,128)(2,1)}), bf16[16,16,640]{2,1,0:T(8,128)(2,1)}, u32[]{:S(2)}, u32[]{:S(2)}) async-start(bf16[16,16,640]{2,1,0:T(8,128)(2,1)} %shard_map.184.send_any), calls=%async_computation | async-start | bytes 655360 | tf_op jit(solution)/shard_map/all_to_all | solution.py:694
  9.8 7.0 %shard_map.185 = (bf16[8,512,256]{2,1,0:T(8,128)(2,1)}, s32[8,128]{1,0:T(8,128)}, s32[256,128]{1,0:T(8,128)}, bf16[8,512,256]{2,1,0:T(8,128)(2,1)}) custom-call(f32[128]{0:T(128)} %rate_any.3, f32[128]{0:T(128)} %skip_any.3, s32[8]{0:T(128)} %len_any.3, s32[2,16]{1,0:T(2,128)} %bitcast.25, s32[8,128]{1,0:T(8,128)} %table_any.1, s32[32]{0:T(128)} %slot_any.1, ...), custom_call_target="tpu_custom_call" | custom-call | flops 1207959552 | bytes 6291456 | tf_op jit(solution)/shard_map/pallas_call | solution.py:707
  16.8 4.2 %all-to-all-done = bf16[16,16,640]{2,1,0:T(8,128)(2,1)} async-done(((bf16[16,16,640]{2,1,0:T(8,128)(2,1)}), bf16[16,16,640]{2,1,0:T(8,128)(2,1)}, u32[]{:S(2)}, u32[]{:S(2)}) %all-to-all-start) | async-done | bytes 327712 | tf_op jit(solution)/shard_map/all_to_all | solution.py:694
  21.0 5.8 %shard_map.186.after_any = bf16[256,896]{1,0:T(8,128)(2,1)} custom-call(bf16[256,640]{1,0:T(8,128)(2,1)} %bitcast.8.recv_any, bf16[1024,256]{1,0:T(8,128)(2,1)} %bitcast.15, s32[8,128]{1,0:T(8,128)} %get-tuple-element.14.tag_any, s32[256,128]{1,0:T(8,128)} %get-tuple-element.15.req_any, bf16[8,512,256]{2,1,0:T(8,128)(2,1)} %get-tuple-element.16.state_any), custom_call_target="tpu_custom_call" | custom-call | flops 268435456 | bytes 4194304 | tf_op jit(solution)/shard_map/pallas_call | solution.py:735
  26.8 4.2 %all-to-all-start.1 = ((bf16[16,16,896]{2,1,0:T(8,128)(2,1)}), bf16[16,16,896]{2,1,0:T(8,128)(2,1)}, u32[]{:S(2)}, u32[]{:S(2)}) async-start(bf16[16,16,896]{2,1,0:T(8,128)(2,1)} %bitcast.14), calls=%async_computation.1 | async-start | bytes 917504 | tf_op jit(solution)/shard_map/all_to_all | solution.py:758
  31.0 8.7 %shard_map.187 = (bf16[8,512,256]{2,1,0:T(8,128)(2,1)}, f32[8,64,128]{2,1,0:T(8,128)}, f32[8,64,128]{2,1,0:T(8,128)}, f32[8,8192]{1,0:T(8,128)}, f32[8,8192]{1,0:T(8,128)}) custom-call(f32[128]{0:T(128)} %rate_any.3, f32[128]{0:T(128)} %skip_any.3, s32[8]{0:T(128)} %len_any.3, bf16[8,8,256]{2,1,0:T(8,128)(2,1)} %dt_any.3, ...), custom_call_target="tpu_custom_call", output_to_operand_aliasing={{0}: (16, {})} | custom-call | flops 2013265920 | bytes 8388608 | tf_op jit(solution)/shard_map/pallas_call | solution.py:765
  39.7 4.6 %all-to-all-done.1.back_any = bf16[16,16,896]{2,1,0:T(8,128)(2,1)} async-done(((bf16[16,16,896]{2,1,0:T(8,128)(2,1)}), bf16[16,16,896]{2,1,0:T(8,128)(2,1)}, u32[]{:S(2)}, u32[]{:S(2)}) %all-to-all-start.1) | async-done | bytes 458784 | tf_op jit(solution)/shard_map/all_to_all | solution.py:758
  44.3 2.7 %shard_map.188 = (bf16[3,2,8192]{2,1,0:T(2,128)(2,1)}, bf16[3,2,8192]{2,1,0:T(2,128)(2,1)}) custom-call(bf16[16,16,896]{2,1,0:T(8,128)(2,1)} %all-to-all-done.1.back_any, f32[8,64,128]{2,1,0:T(8,128)} %get-tuple-element.19.own_any, f32[8,64,128]{2,1,0:T(8,128)} %get-tuple-element.20.ownsum_any, f32[8,8192]{1,0:T(8,128)} %get-tuple-element.21.fade_any, ...), custom_call_target="tpu_custom_call" | custom-call | bytes 2097152 | tf_op jit(solution)/shard_map/pallas_call | solution.py:822
Async XLA Ops:
  2.4 18.6 %all-to-all-start = ((bf16[16,16,640]{2,1,0:T(8,128)(2,1)}), bf16[16,16,640]{2,1,0:T(8,128)(2,1)}, u32[]{:S(2)}, u32[]{:S(2)}) async-start(bf16[16,16,640]{2,1,0:T(8,128)(2,1)} %shard_map.184.send_any), calls=%async_computation | async-start | bytes 655360 | tf_op jit(solution)/shard_map/all_to_all | solution.py:694
  26.8 17.5 %all-to-all-start.1 = ((bf16[16,16,896]{2,1,0:T(8,128)(2,1)}), bf16[16,16,896]{2,1,0:T(8,128)(2,1)}, u32[]{:S(2)}, u32[]{:S(2)}) async-start(bf16[16,16,896]{2,1,0:T(8,128)(2,1)} %bitcast.14), calls=%async_computation.1 | async-start | bytes 917504 | tf_op jit(solution)/shard_map/all_to_all | solution.py:758

commit v2 on v1

--- a/solution.py
+++ b/solution.py
@@ -22,6 +22,7 @@
 SCORE = LOG2E / math.sqrt(HD)
 NONE = -1e30
 FLOOR = -1e29
+SUMS_ROW = 6
 EARLY = 2
 VMEM_LIMIT = 64 * 1024 * 1024
 
@@ -52,25 +53,19 @@
 
 
 def pack_kernel(group, ways, q_any, c_any, out_ref, q_ref, c_ref, q_held, c_held, sems):
-    owners = out_ref.shape[0]
+    owners = out_ref.shape[0] // SUB
     for copy in fetches([(q_any, q_ref), (c_any, c_ref)], sems):
         copy.wait()
     stack_rows(q_ref, q_held)
     stack_rows(c_ref, c_held)
     span = 2 * HALF
-    for v in range(KVH):
-        both = jnp.concatenate(
-            [q_held[:, v * span : v * span + HALF], q_held[:, v * span + HALF : (v + 1) * span]], axis=0
-        ).astype(bf16)
-        for way in range(ways):
-            out_ref[v * ways + way, :, :HALF] = both
-    for e in range(c_ref.shape[2] // NS):
-        low = c_held[:, e * NS : e * NS + LANES]
-        high = c_held[:, e * NS + LANES : (e + 1) * NS]
-        both = jnp.concatenate([low, high], axis=0).astype(bf16)
-        for d in range(owners):
-            if (d * group) // HPG == e:
-                out_ref[d, :, HALF:] = both
+    for d in range(0, owners, 2):
+        v, e = d // ways, (d * group) // HPG
+        low = q_held[:, v * span : v * span + HALF]
+        high = q_held[:, v * span + HALF : (v + 1) * span]
+        out_ref[d * SUB : (d + 2) * SUB, :HALF] = jnp.concatenate([low, high], axis=0).astype(bf16)
+        readout = c_held[:, e * NS : (e + 1) * NS]
+        out_ref[d * SUB : (d + 2) * SUB, HALF:] = jnp.concatenate([readout, readout], axis=0).astype(bf16)
 
 
 def head_factors(first, dt_ref, rate_ref, skip_ref, len_ref, levels, w_in, w_out, w_skip, w_tail):
@@ -230,30 +225,32 @@
     spread = table_ref.shape[1] // owner_ref.shape[1]
     key_page = iota((SUB, LANES), 0) * (LANES // PAGE) + iota((SUB, LANES), 1) // PAGE
     key_offset = iota((SUB, LANES), 1) % PAGE
-    tag = jnp.full((SUB, LANES), -1, jnp.int32)
     per_head = table_ref.shape[1] // KVH
-    for r in range(prompts):
-        for page in range(spread):
-            entry = me * spread + page
-            row = table_ref[r, entry] - me * (prompts * spread)
-            begin = lax.rem(entry, per_head) * PAGE
-            inside = (key_page == row) & (key_offset < len_ref[r] - begin)
-            tag = jnp.where(inside, r, tag)
-    tag_ref[...] = tag
+    for n, holder in enumerate((me, me + 1 - 2 * lax.rem(me, 2))):
+        tag = jnp.full((SUB, LANES), -1, jnp.int32)
+        for r in range(prompts):
+            for page in range(spread):
+                entry = holder * spread + page
+                row = table_ref[r, entry] - holder * (prompts * spread)
+                begin = lax.rem(entry, per_head) * PAGE
+                inside = (key_page == row) & (key_offset < len_ref[r] - begin)
+                tag = jnp.where(inside, r, tag)
+        tag_ref[n] = tag
 
     owners = owner_ref.shape[1]
     rows_dev = slot_ref.shape[0] // owners
-    inner = iota((2 * SUB, LANES), 0) % SUB
+    inner = iota((2 * SUB, LANES), 0)
 
     def fill(s, _):
         block = jnp.full((2 * SUB, LANES), -2, jnp.int32)
-        for i in range(rows_dev):
-            target = owner_ref[slot_ref[s * rows_dev + i], s]
-            block = jnp.where(inner % rows_dev == i, target, block)
+        for n in range(2):
+            for i in range(rows_dev):
+                target = owner_ref[slot_ref[(2 * s + n) * rows_dev + i], 2 * s + n]
+                block = jnp.where((inner // SUB == n) & (inner % rows_dev == i), target, block)
         req_ref[pl.ds(pl.multiple_of(s * 2 * SUB, 2 * SUB), 2 * SUB), :] = block
         return 0
 
-    lax.fori_loop(0, owners, fill, 0)
+    lax.fori_loop(0, owners // 2, fill, 0)
 
     def one(r, _):
         x_copy(r).wait()
@@ -286,6 +283,7 @@
 def serve_kernel(
     recv_any,
     pages_any,
+    other_any,
     tag_any,
     req_any,
     state_any,
@@ -299,62 +297,66 @@
     state_sem,
     sems,
 ):
+    marks = fetches([(tag_any, tag_ref), (req_any, req_ref)], sems.at[pl.ds(0, 2)])
     smalls = fetches(
-        [(tag_any, tag_ref), (req_any, req_ref), (pages_any, pages_ref), (recv_any, recv_ref)], sems
+        [(recv_any, recv_ref), (pages_any, pages_ref.at[0]), (other_any, pages_ref.at[1])],
+        sems.at[pl.ds(2, 3)],
     )
     states = fetches([(state_any.at[r], state_ref.at[r]) for r in range(state_any.shape[0])], state_sem)
+    for copy in marks:
+        copy.wait()
+    rows = recv_ref.shape[0]
+    holders, keys = pages_ref.shape[0], pages_ref.shape[1]
+    prompts, width = state_ref.shape[0], state_ref.shape[1]
+    for n in range(holders):
+        tag = tag_ref[n]
+        for b in range(keys // LANES):
+            mine = jnp.broadcast_to(tag[b : b + 1, :], (rows, LANES))
+            bias[n, :, b * LANES : (b + 1) * LANES] = jnp.where(req_ref[...] == mine, 0.0, NONE)
     for copy in smalls:
         copy.wait()
-    rows = recv_ref.shape[0]
-    keys = pages_ref.shape[0]
-    prompts, width = state_ref.shape[0], state_ref.shape[1]
-    tag = tag_ref[...]
-    for b in range(keys // LANES):
-        mine = jnp.broadcast_to(tag[b : b + 1, :], (rows, LANES))
-        bias[:, b * LANES : (b + 1) * LANES] = jnp.where(req_ref[...] == mine, 0.0, NONE)
     lane = iota((rows, LANES), 1)
     sums = jnp.zeros((rows, LANES), f32)
+    values = []
     for g in range(HALF // HD):
-        scores = dot_nt(recv_ref[:, g * HD : (g + 1) * HD], pages_ref[:, :HD]) * SCORE + bias[...]
-        highest = jnp.maximum(jnp.max(scores, axis=1, keepdims=True), FLOOR)
-        weight = jnp.exp2(scores - highest)
-        total = jnp.sum(weight, axis=1, keepdims=True)
-        value = jnp.dot(weight.astype(bf16), pages_ref[:, HD:], preferred_element_type=f32)
+        query = recv_ref[:, g * HD : (g + 1) * HD]
+        scores = [dot_nt(query, pages_ref[n, :, :HD]) * SCORE + bias[n] for n in range(holders)]
+        highest = jnp.full((rows, 1), FLOOR, f32)
+        for one in scores:
+            highest = jnp.maximum(highest, jnp.max(one, axis=1, keepdims=True))
+        total = jnp.zeros((rows, 1), f32)
+        value = jnp.zeros((rows, HD), f32)
+        for n in range(holders):
+            weight = jnp.exp2(scores[n] - highest)
+            total = total + jnp.sum(weight, axis=1, keepdims=True)
+            value = value + jnp.dot(weight.astype(bf16), pages_ref[n, :, HD:], preferred_element_type=f32)
         some = total > 0.0
         safe = jnp.where(some, total, 1.0)
-        out_ref[:, g * HD : (g + 1) * HD] = (value / safe).astype(bf16)
+        values.append(value / safe)
         sums = jnp.where(lane % 4 == g, highest + jnp.log2(safe), sums)
-    high = sums.astype(bf16)
-    rest = sums - high.astype(f32)
-    middle = rest.astype(bf16)
-    low = rest - middle.astype(f32)
-    third = lane // 4
-    pieces = jnp.where(third == 0, high.astype(f32), jnp.where(third == 1, middle.astype(f32), low))
-    held = projected_columns(width)
-    out_ref[:, HALF + held :] = pieces.astype(bf16)
-
-    blocks = rows // (2 * SUB)
-    ahead = recv_ref[:, HALF:].astype(f32).reshape(blocks, 2, SUB, LANES)
-    readout = jnp.concatenate([ahead[:, 0], ahead[:, 1]], axis=-1).reshape(blocks * SUB, NS)
-    target = req_ref[...].reshape(blocks, 2, SUB, LANES)[:, 0].reshape(blocks * SUB, LANES)
-    target = jnp.concatenate([target, target], axis=-1)
-    found = jnp.zeros((blocks * SUB, width), f32)
+    high = sums.astype(bf16).astype(f32)
+    rest = sums - high
+    middle = rest.astype(bf16).astype(f32)
+    piece = lane % 16 // 4
+    pieces = jnp.where(piece == 0, high, jnp.where(piece == 1, middle, rest - middle))
+    pair = iota((rows, LANES), 0) % SUB
+    pieces = jnp.where((lane // 16 == pair) & (piece < 3), pieces, 0.0)
+    packed = jnp.sum(pieces.reshape(rows // SUB, SUB, LANES), axis=1, keepdims=True)
+    packed = jnp.broadcast_to(packed, (rows // SUB, SUB, LANES)).reshape(rows, LANES)
+    values[0] = jnp.where(pair == SUMS_ROW, packed, values[0])
+    for g in range(HALF // HD):
+        out_ref[:, g * HD : (g + 1) * HD] = values[g].astype(bf16)
+
+    readout = recv_ref[:, HALF:].astype(f32)
+    target = jnp.concatenate([req_ref[...], req_ref[...]], axis=-1)
+    found = jnp.zeros((rows, width), f32)
     for r in range(prompts):
         picked = jnp.where(target == r, readout, 0.0).astype(bf16)
         states[r].wait()
         found = found + dot_nt(picked, state_ref[r])
-    if width == 2 * held:
-        found = found.reshape(blocks, SUB, width)
-        both = jnp.stack([found[..., :held], found[..., held:]], axis=1)
-    else:
-        found = jnp.concatenate([found, jnp.zeros((blocks * SUB, held - width), f32)], axis=-1)
-        found = found.reshape(blocks, SUB, held)
-        both = jnp.stack([found, found], axis=1)
-    out_ref[:, HALF : HALF + held] = both.reshape(rows, held).astype(bf16)
-
-
-def projected_columns(width):
-    return max(LANES, width // 2)
+    if width < LANES:
+        found = jnp.concatenate([found, jnp.zeros((rows, LANES - width), f32)], axis=-1)
+    out_ref[:, HALF:] = found.astype(bf16)
 
 
 def prompt_kernel(
@@ -470,7 +472,7 @@
 
 def own_attention(send_ref, fresh_ref, fresh_held, own_ref, ownsum_ref):
     steps, rows = fresh_ref.shape[0], fresh_ref.shape[1]
-    ways = send_ref.shape[0] // KVH
+    ways = send_ref.shape[0] // SUB // KVH
     stack_rows(fresh_ref, fresh_held)
     count = HALF // HD * 2 * SUB
     pair = iota((count, SUB), 0) % SUB
@@ -478,7 +480,7 @@
     seen = (key % rows == pair % rows) & (key <= pair) & (key < rows * steps)
     seen = seen | ((pair >= rows * steps) & (key == 0))
     for v in range(KVH):
-        block = send_ref[v * ways]
+        block = send_ref[v * ways * SUB : (v * ways + 2) * SUB]
         query = jnp.concatenate([block[:, g * HD : (g + 1) * HD] for g in range(HALF // HD)], axis=0)
         keys = fresh_held[:, v * HD : (v + 1) * HD].astype(bf16)
         values = fresh_held[:, (KVH + v) * HD : (KVH + v + 1) * HD].astype(bf16)
@@ -574,43 +576,40 @@
     )
     for copy in copies:
         copy.wait()
-    owners = back_ref.shape[0]
+    owners = back_ref.shape[0] // SUB
     ways = owners // KVH
-    held = projected_columns(width)
     steps, rows = mixer_ref.shape[0], mixer_ref.shape[1]
-    if width == 2 * held:
-        for d in range(owners):
-            for half in range(2):
-                columns = slice(d * width + half * held, d * width + (half + 1) * held)
-                found = back_ref[d, :, HALF : HALF + held].astype(f32)[half * SUB : (half + 1) * SUB]
-                mixed[:, columns] = found * fade_ref[:, columns] + local_ref[:, columns]
-    else:
-        many = LANES // width
-        for d in range(0, owners, many):
-            found = jnp.concatenate(
-                [back_ref[d + n, :, HALF : HALF + held].astype(f32)[:SUB, :width] for n in range(many)], axis=-1
-            )
-            columns = slice(d * width, (d + many) * width)
-            mixed[:, columns] = found * fade_ref[:, columns] + local_ref[:, columns]
+    for d in range(0, owners, 2):
+        found = back_ref[d * SUB : (d + 2) * SUB, HALF : HALF + width].astype(f32)
+        found = jnp.concatenate([found[:SUB], found[SUB:]], axis=-1)
+        columns = slice(d * width, (d + 2) * width)
+        mixed[:, columns] = found * fade_ref[:, columns] + local_ref[:, columns]
     for k in range(steps):
         mixer_ref[k] = mixed[k * rows : (k + 1) * rows, :].astype(bf16)
+    lane = iota((2, SUB, LANES), 2)
+    mine = (lane // 16 == iota((2, SUB, LANES), 1)) & (lane % 16 < 12)
     for v in range(KVH):
-        sums = []
-        for way in range(ways):
-            pieces = back_ref[v * ways + way, :, HALF + held :].astype(f32)
-            sums.append(pieces[:, 0:4] + (pieces[:, 4:8] + pieces[:, 8:12]))
+        blocks, pieces = [], []
+        for d in range(v * ways, (v + 1) * ways, 2):
+            block = back_ref[d * SUB : (d + 2) * SUB, :HALF].astype(f32)
+            packed = block[:, :LANES].reshape(2, SUB, LANES)[:, SUMS_ROW : SUMS_ROW + 1, :]
+            blocks.append(block)
+            pieces.append(jnp.where(mine, jnp.broadcast_to(packed, (2, SUB, LANES)), 0.0))
         for g in range(HALF // HD):
-            mine = slice(g * 2 * SUB, (g + 1) * 2 * SUB)
-            own_sum = ownsum_ref[v, mine, :]
-            wide = [jnp.broadcast_to(one[:, g : g + 1], (2 * SUB, HD)) for one in sums]
+            part = slice(g * 2 * SUB, (g + 1) * 2 * SUB)
+            own_sum = ownsum_ref[v, part, :]
+            wide = []
+            for piece in pieces:
+                one = jnp.sum(jnp.where(lane % 4 == g, piece, 0.0), axis=-1, keepdims=True)
+                wide.append(jnp.broadcast_to(one, (2, SUB, HD)).reshape(2 * SUB, HD))
             highest = functools.reduce(jnp.maximum, wide, own_sum)
             weight = jnp.exp2(own_sum - highest)
             total = weight
-            value = weight * own_ref[v, mine, :]
-            for way in range(ways):
-                weight = jnp.exp2(wide[way] - highest)
+            value = weight * own_ref[v, part, :]
+            for one, block in zip(wide, blocks):
+                weight = jnp.exp2(one - highest)
                 total = total + weight
-                value = value + weight * back_ref[v * ways + way, :, g * HD : (g + 1) * HD].astype(f32)
+                value = value + weight * block[:, g * HD : (g + 1) * HD]
             value = value / total
             start = v * 2 * HALF + g * HD
             attended[:, start : start + HD] = value[:SUB]
@@ -660,8 +659,7 @@
     width = prompt_x.shape[1]
     keys = cache_pages.shape[0] * PAGE
     steps = step_x.shape[1]
-    held = projected_columns(width)
-    all_rows = owners * 2 * SUB
+    all_rows = owners * SUB
     shape = jax.ShapeDtypeStruct
     smem, vmem, hbm = pltpu.SMEM, pltpu.VMEM, pltpu.HBM
     sem = pltpu.SemaphoreType.DMA((prompts,))
@@ -677,9 +675,10 @@
     def sems(count):
         return pltpu.SemaphoreType.DMA((count,))
 
+    other_pages = lax.ppermute(cache_pages, "heads", [(d, d + 1 - 2 * (d % 2)) for d in range(owners)])
     send = call(
         functools.partial(pack_kernel, group, ways),
-        shape((owners, 2 * SUB, HALF + LANES), bf16),
+        shape((all_rows, HALF + NS), bf16),
         [hbm, hbm],
         vmem,
         [
@@ -708,7 +707,7 @@
         state_kernel,
         (
             shape((prompts, width, NS), bf16),
-            shape((SUB, LANES), jnp.int32),
+            shape((2, SUB, LANES), jnp.int32),
             shape((all_rows, LANES), jnp.int32),
             shape(prompt_x.shape, bf16),
         ),
@@ -734,30 +733,29 @@
 
     back = call(
         serve_kernel,
-        shape((all_rows, HALF + held + LANES), bf16),
-        [hbm] * 5,
+        shape((all_rows, HALF + max(LANES, width)), bf16),
+        [hbm] * 6,
         vmem,
         [
-            vmem((all_rows, HALF + LANES), bf16),
-            vmem((keys, 2 * HD), bf16),
+            like(vmem, recv),
+            vmem((2, keys, 2 * HD), bf16),
             like(vmem, tag),
             like(vmem, requests),
             like(vmem, states),
-            vmem((all_rows, keys), f32),
+            vmem((2, all_rows, keys), f32),
             sem,
-            sems(4),
+            sems(5),
         ],
         (8 * all_rows * keys * HD, 4 << 20),
     )(
-        recv.reshape(all_rows, HALF + LANES),
+        recv,
         cache_pages.reshape(keys, 2 * HD),
+        other_pages.reshape(keys, 2 * HD),
         tag,
         requests,
         states,
     )
-    returned = lax.all_to_all(
-        back.reshape(owners, 2 * SUB, back.shape[1]), "heads", split_axis=0, concat_axis=0, tiled=True
-    )
+    returned = lax.all_to_all(back, "heads", split_axis=0, concat_axis=0, tiled=True)
 
     count = HALF // HD * 2 * SUB
     channels = step_x.shape[2]

time: 47.4 us -> 41.9 us (0.88)
  waiting for transfers between devices: 8.72 us -> 3.33 us
    all_to_all x1, waiting for transfers between devices: 4.57 us -> 1.35 us  [on_device(): lax.all_to_all(back, 'heads', split_axis=0, concat_axis=0, tiled=True)]
    all_to_all x1, waiting for transfers between devices: 4.15 us -> 1.98 us  [on_device(): lax.all_to_all(send, 'heads', split_axis=0, concat_axis=0, tiled=True)]
    ppermute x0 -> x1, starting transfers between devices: none -> 0.52 us  [on_device(): lax.ppermute(cache_pages, 'heads', [(d, d + 1 - 2 * (d % 2)) for d in ran...]
  transfers between devices with their start and end apart: 2 -> 3, of which waited for: 2 -> 2; matrix products, arithmetic and copies ran while one was open for 0% -> 0% of each run, Pallas kernels for 33% -> 42%
where the time goes in v2:
time: 41.9 us; the launch traced here: 41.5 us
  Pallas kernels  25.7 us (61%)
  starting transfers between devices  11.8 us (28%)
  waiting for transfers between devices  3.33 us (8%)
  between operations  0.68 us (2%)
    pallas_call x1, Pallas kernels, on_device(): call(prompt_kernel, (shape(prompt_x.shape, bf16), shape((KVH, count, HD),...  8.69 us
    all_to_all x1, starting transfers between devices, on_device(): lax.all_to_all(send, 'heads', split_axis=0, concat_axis=0, tiled=True)  7.1 us
    pallas_call x1, Pallas kernels, on_device(): call(state_kernel, (shape((prompts, width, NS), bf16), shape((2, SUB, LAN...  7.07 us
    pallas_call x1, Pallas kernels, on_device(): call(serve_kernel, shape((all_rows, HALF + max(LANES, width)), bf16), [hb...  5.95 us
    all_to_all x1, starting transfers between devices, on_device(): lax.all_to_all(back, 'heads', split_axis=0, concat_axis=0, tiled=True)  4.2 us
    pallas_call x1, Pallas kernels, on_device(): call(functools.partial(merge_kernel, width), (shape(step_x.shape, bf16),...  2.29 us
    all_to_all x1, waiting for transfers between devices, on_device(): lax.all_to_all(send, 'heads', split_axis=0, concat_axis=0, tiled=True)  1.98 us
    pallas_call x1, Pallas kernels, on_device(): call(functools.partial(pack_kernel, group, ways), shape((all_rows, HALF +...  1.7 us
  transfers between devices with their start and end apart: 3, of which 2 were waited for; matrix products, arithmetic and copies ran while one was open for 0% of the time, Pallas kernels for 42%

profile of v2, /device:TPU:0, one launch (start us, length us, event | category | flops | bytes accessed | tf_op | source)
XLA Modules:
  0.0 41.5 jit_solution(10697806936195081996)
XLA Ops:
  0.6 0.5 %collective-permute-start = (bf16[64,16,256]{2,1,0:T(8,128)(2,1)}, bf16[64,16,256]{2,1,0:T(8,128)(2,1)}, u32[]{:S(2)}, u32[]{:S(2)}) collective-permute-start(bf16[64,16,256]{2,1,0:T(8,128)(2,1)} %param.26), channel_id=1, source_target_pairs={{0,1},{1,0},{2,3},{3,2},{4,5},{5,4},{6,7},{7,6},{8,9},{9,8},{10,11... | collective-permute-start | bytes 1572872 | tf_op jit(solution)/shard_map/ppermute | solution.py:678
  1.1 1.7 %shard_map.184.send_any = bf16[128,768]{1,0:T(8,128)(2,1)} custom-call(bf16[3,2,8192]{2,1,0:T(2,128)(2,1)} %bitcast.21, bf16[3,2,1024]{2,1,0:T(2,128)(2,1)} %bitcast.22), custom_call_target="tpu_custom_call" | custom-call | bytes 524288 | tf_op jit(solution)/shard_map/pallas_call | solution.py:679
  2.9 7.1 %all-to-all-start = ((bf16[16,8,768]{2,1,0:T(8,128)(2,1)}), bf16[16,8,768]{2,1,0:T(8,128)(2,1)}, u32[]{:S(2)}, u32[]{:S(2)}) async-start(bf16[16,8,768]{2,1,0:T(8,128)(2,1)} %bitcast.18), calls=%async_computation | async-start | bytes 393216 | tf_op jit(solution)/shard_map/all_to_all | solution.py:693
  10.0 7.1 %shard_map.185 = (bf16[8,512,256]{2,1,0:T(8,128)(2,1)}, s32[2,8,128]{2,1,0:T(8,128)}, s32[128,128]{1,0:T(8,128)}, bf16[8,512,256]{2,1,0:T(8,128)(2,1)}) custom-call(f32[128]{0:T(128)} %rate_any.3, f32[128]{0:T(128)} %skip_any.3, s32[8]{0:T(128)} %len_any.3, s32[2,16]{1,0:T(2,128)} %bitcast.29, s32[8,128]{1,0:T(8,128)} %table_any.1, s32[32]{0:T(128)} %slot_any.1, ...), custom_call_target="tpu_custom_call" | custom-call | flops 1207959552 | bytes 6291456 | tf_op jit(solution)/shard_map/pallas_call | solution.py:706
  17.0 2.0 %all-to-all-done = bf16[16,8,768]{2,1,0:T(8,128)(2,1)} async-done(((bf16[16,8,768]{2,1,0:T(8,128)(2,1)}), bf16[16,8,768]{2,1,0:T(8,128)(2,1)}, u32[]{:S(2)}, u32[]{:S(2)}) %all-to-all-start) | async-done | bytes 196640 | tf_op jit(solution)/shard_map/all_to_all | solution.py:693
  19.0 0.0 collective-permute-done
  19.0 6.0 %shard_map.186.after_any = bf16[128,1024]{1,0:T(8,128)(2,1)} custom-call(bf16[128,768]{1,0:T(8,128)(2,1)} %bitcast.9.recv_any, bf16[1024,256]{1,0:T(8,128)(2,1)} %bitcast.19, bf16[1024,256]{1,0:T(8,128)(2,1)} %bitcast.11.other_any, s32[2,8,128]{2,1,0:T(8,128)} %get-tuple-element.14.tag_any, s32[128,128]{1,0:T(8,128)} %get-tuple-element.15.req_any, ...), custom_call_target="tpu_custom_call" | custom-call | flops 134217728 | bytes 4194304 | tf_op jit(solution)/shard_map/pallas_call | solution.py:734
  25.0 4.2 %all-to-all-start.1 = ((bf16[16,8,1024]{2,1,0:T(8,128)(2,1)}), bf16[16,8,1024]{2,1,0:T(8,128)(2,1)}, u32[]{:S(2)}, u32[]{:S(2)}) async-start(bf16[16,8,1024]{2,1,0:T(8,128)(2,1)} %bitcast.17), calls=%async_computation.1 | async-start | bytes 524288 | tf_op jit(solution)/shard_map/all_to_all | solution.py:758
  29.2 8.7 %shard_map.187 = (bf16[8,512,256]{2,1,0:T(8,128)(2,1)}, f32[8,64,128]{2,1,0:T(8,128)}, f32[8,64,128]{2,1,0:T(8,128)}, f32[8,8192]{1,0:T(8,128)}, f32[8,8192]{1,0:T(8,128)}) custom-call(f32[128]{0:T(128)} %rate_any.3, f32[128]{0:T(128)} %skip_any.3, s32[8]{0:T(128)} %len_any.3, bf16[8,8,256]{2,1,0:T(8,128)(2,1)} %dt_any.3, ...), custom_call_target="tpu_custom_call", output_to_operand_aliasing={{0}: (16, {})} | custom-call | flops 2013265920 | bytes 8388608 | tf_op jit(solution)/shard_map/pallas_call | solution.py:763
  37.9 1.4 %all-to-all-done.1 = bf16[16,8,1024]{2,1,0:T(8,128)(2,1)} async-done(((bf16[16,8,1024]{2,1,0:T(8,128)(2,1)}), bf16[16,8,1024]{2,1,0:T(8,128)(2,1)}, u32[]{:S(2)}, u32[]{:S(2)}) %all-to-all-start.1) | async-done | bytes 262176 | tf_op jit(solution)/shard_map/all_to_all | solution.py:758
  39.2 2.3 %shard_map.188 = (bf16[3,2,8192]{2,1,0:T(2,128)(2,1)}, bf16[3,2,8192]{2,1,0:T(2,128)(2,1)}) custom-call(bf16[128,1024]{1,0:T(8,128)(2,1)} %bitcast.14.back_any, f32[8,64,128]{2,1,0:T(8,128)} %get-tuple-element.19.own_any, f32[8,64,128]{2,1,0:T(8,128)} %get-tuple-element.20.ownsum_any, f32[8,8192]{1,0:T(8,128)} %get-tuple-element.21.fade_any, ...), custom_call_target="tpu_custom_call" | custom-call | bytes 2097152 | tf_op jit(solution)/shard_map/pallas_call | solution.py:820
Async XLA Ops:
  0.6 18.4 %collective-permute-start = (bf16[64,16,256]{2,1,0:T(8,128)(2,1)}, bf16[64,16,256]{2,1,0:T(8,128)(2,1)}, u32[]{:S(2)}, u32[]{:S(2)}) collective-permute-start(bf16[64,16,256]{2,1,0:T(8,128)(2,1)} %param.26), channel_id=1, source_target_pairs={{0,1},{1,0},{2,3},{3,2},{4,5},{5,4},{6,7},{7,6},{8,9},{9,8},{10,11... | collective-permute-start | bytes 1572872 | tf_op jit(solution)/shard_map/ppermute | solution.py:678
  2.9 16.2 %all-to-all-start = ((bf16[16,8,768]{2,1,0:T(8,128)(2,1)}), bf16[16,8,768]{2,1,0:T(8,128)(2,1)}, u32[]{:S(2)}, u32[]{:S(2)}) async-start(bf16[16,8,768]{2,1,0:T(8,128)(2,1)} %bitcast.18), calls=%async_computation | async-start | bytes 393216 | tf_op jit(solution)/shard_map/all_to_all | solution.py:693
  25.0 14.3 %all-to-all-start.1 = ((bf16[16,8,1024]{2,1,0:T(8,128)(2,1)}), bf16[16,8,1024]{2,1,0:T(8,128)(2,1)}, u32[]{:S(2)}, u32[]{:S(2)}) async-start(bf16[16,8,1024]{2,1,0:T(8,128)(2,1)} %bitcast.17), calls=%async_computation.1 | async-start | bytes 524288 | tf_op jit(solution)/shard_map/all_to_all | solution.py:758

commit v3 on v2

--- a/solution.py
+++ b/solution.py
@@ -21,8 +21,8 @@
 LOG2E = math.log2(math.e)
 SCORE = LOG2E / math.sqrt(HD)
 NONE = -1e30
-FLOOR = -1e29
-SUMS_ROW = 6
+PAIRS = 6
+MATCH = 32768.0
 EARLY = 2
 VMEM_LIMIT = 64 * 1024 * 1024
 
@@ -45,6 +45,19 @@
         held[k * rows : (k + 1) * rows, :] = source[k].astype(f32)
 
 
+def spare(blocks, taken):
+    return [(row, b) for row in range(PAIRS, SUB) for b in range(blocks)][taken : taken + PAIRS]
+
+
+def lift(value, slots):
+    row = iota(value.shape[:2] + (LANES,), 1)
+    found = jnp.zeros(row.shape, f32)
+    for pair, (at, b) in enumerate(slots):
+        one = value[:, at : at + 1, b * LANES : (b + 1) * LANES]
+        found = jnp.where(row == pair, jnp.broadcast_to(one, row.shape), found)
+    return found
+
+
 def fetches(pairs, sems):
     copies = [pltpu.make_async_copy(src, dst, sems.at[n]) for n, (src, dst) in enumerate(pairs)]
     for copy in copies:
@@ -52,20 +65,29 @@
     return copies
 
 
-def pack_kernel(group, ways, q_any, c_any, out_ref, q_ref, c_ref, q_held, c_held, sems):
+def pack_kernel(group, ways, q_any, c_any, out_ref, q_ref, c_ref, q_held, c_held, rest, sems):
     owners = out_ref.shape[0] // SUB
     for copy in fetches([(q_any, q_ref), (c_any, c_ref)], sems):
         copy.wait()
     stack_rows(q_ref, q_held)
     stack_rows(c_ref, c_held)
     span = 2 * HALF
+    slots = spare(HALF // LANES + 1, 0)
+    rest[...] = jnp.zeros_like(rest)
+    for e in range(c_ref.shape[2] // NS):
+        rest[e, :PAIRS, HALF:] = c_held[:PAIRS, e * NS : e * NS + LANES]
+        for pair, (row, b) in enumerate(slots):
+            rest[e, row : row + 1, b * LANES : (b + 1) * LANES] = c_held[
+                pair : pair + 1, e * NS + LANES : (e + 1) * NS
+            ]
+    real = iota((SUB, HALF), 0) < PAIRS
     for d in range(0, owners, 2):
         v, e = d // ways, (d * group) // HPG
-        low = q_held[:, v * span : v * span + HALF]
-        high = q_held[:, v * span + HALF : (v + 1) * span]
+        low = jnp.where(real, q_held[:, v * span : v * span + HALF], rest[e, :, :HALF])
+        high = jnp.where(real, q_held[:, v * span + HALF : (v + 1) * span], rest[e, :, :HALF])
         out_ref[d * SUB : (d + 2) * SUB, :HALF] = jnp.concatenate([low, high], axis=0).astype(bf16)
-        readout = c_held[:, e * NS : (e + 1) * NS]
-        out_ref[d * SUB : (d + 2) * SUB, HALF:] = jnp.concatenate([readout, readout], axis=0).astype(bf16)
+        end = rest[e, :, HALF:]
+        out_ref[d * SUB : (d + 2) * SUB, HALF:] = jnp.concatenate([end, end], axis=0).astype(bf16)
 
 
 def head_factors(first, dt_ref, rate_ref, skip_ref, len_ref, levels, w_in, w_out, w_skip, w_tail):
@@ -151,7 +173,8 @@
     b_any,
     c_any,
     state_any,
-    tag_ref,
+    mark_any,
+    hot_ref,
     req_ref,
     out_any,
     x_held,
@@ -164,6 +187,7 @@
     w_tail,
     masks,
     state_held,
+    mark_held,
     rate_ref,
     skip_ref,
     len_ref,
@@ -176,6 +200,7 @@
     c_sem,
     out_sem,
     state_sem,
+    mark_sem,
     sems,
 ):
     group, prompts, length = dt_ref.shape
@@ -223,23 +248,24 @@
     )
 
     spread = table_ref.shape[1] // owner_ref.shape[1]
-    key_page = iota((SUB, LANES), 0) * (LANES // PAGE) + iota((SUB, LANES), 1) // PAGE
-    key_offset = iota((SUB, LANES), 1) % PAGE
     per_head = table_ref.shape[1] // KVH
+    offset, lane = iota((PAGE, LANES), 0), iota((PAGE, LANES), 1)
     for n, holder in enumerate((me, me + 1 - 2 * lax.rem(me, 2))):
-        tag = jnp.full((SUB, LANES), -1, jnp.int32)
         for r in range(prompts):
             for page in range(spread):
                 entry = holder * spread + page
                 row = table_ref[r, entry] - holder * (prompts * spread)
                 begin = lax.rem(entry, per_head) * PAGE
-                inside = (key_page == row) & (key_offset < len_ref[r] - begin)
-                tag = jnp.where(inside, r, tag)
-        tag_ref[n] = tag
+                inside = (lane == r) & (offset < len_ref[r] - begin)
+                block = jnp.where(inside, MATCH, 0.0).astype(bf16)
+                mark_held[n, pl.ds(pl.multiple_of(row * PAGE, PAGE), PAGE), :] = block
+    mark_copy = pltpu.make_async_copy(mark_held, mark_any, mark_sem)
+    mark_copy.start()
 
     owners = owner_ref.shape[1]
     rows_dev = slot_ref.shape[0] // owners
     inner = iota((2 * SUB, LANES), 0)
+    lanes = iota((2 * SUB, LANES), 1)
 
     def fill(s, _):
         block = jnp.full((2 * SUB, LANES), -2, jnp.int32)
@@ -247,7 +273,9 @@
             for i in range(rows_dev):
                 target = owner_ref[slot_ref[(2 * s + n) * rows_dev + i], 2 * s + n]
                 block = jnp.where((inner // SUB == n) & (inner % rows_dev == i), target, block)
-        req_ref[pl.ds(pl.multiple_of(s * 2 * SUB, 2 * SUB), 2 * SUB), :] = block
+        place = pl.ds(pl.multiple_of(s * 2 * SUB, 2 * SUB), 2 * SUB)
+        req_ref[place, :] = block
+        hot_ref[place, :] = jnp.where(lanes == block, 1.0, 0.0).astype(bf16)
         return 0
 
     lax.fori_loop(0, owners // 2, fill, 0)
@@ -278,62 +306,81 @@
             out_copy(r).wait()
     for r in range(prompts):
         state_copy(r).wait()
+    mark_copy.wait()
 
 
 def serve_kernel(
     recv_any,
     pages_any,
     other_any,
-    tag_any,
+    mark_any,
+    hot_any,
     req_any,
     state_any,
     out_ref,
     recv_ref,
-    pages_ref,
-    tag_ref,
+    key_ref,
+    value_ref,
+    hot_ref,
     req_ref,
     state_ref,
-    bias,
+    query_ref,
+    score_ref,
     state_sem,
     sems,
 ):
-    marks = fetches([(tag_any, tag_ref), (req_any, req_ref)], sems.at[pl.ds(0, 2)])
-    smalls = fetches(
-        [(recv_any, recv_ref), (pages_any, pages_ref.at[0]), (other_any, pages_ref.at[1])],
-        sems.at[pl.ds(2, 3)],
-    )
-    states = fetches([(state_any.at[r], state_ref.at[r]) for r in range(state_any.shape[0])], state_sem)
-    for copy in marks:
+    rows = recv_ref.shape[0]
+    held = pages_any.shape[0]
+    prompts, width = state_ref.shape[0], state_ref.shape[1]
+    mine, other = pl.ds(0, held), pl.ds(held, held)
+    copies = fetches(
+        [
+            (recv_any, recv_ref),
+            (hot_any, hot_ref),
+            (pages_any.at[:, pl.ds(0, HD)], key_ref.at[mine, pl.ds(0, HD)]),
+            (other_any.at[:, pl.ds(0, HD)], key_ref.at[other, pl.ds(0, HD)]),
+            (mark_any.at[0], key_ref.at[mine, pl.ds(HD, LANES)]),
+            (mark_any.at[1], key_ref.at[other, pl.ds(HD, LANES)]),
+            (pages_any.at[:, pl.ds(HD, HD)], value_ref.at[mine]),
+            (other_any.at[:, pl.ds(HD, HD)], value_ref.at[other]),
+            (req_any, req_ref),
+        ],
+        sems,
+    )
+    states = fetches([(state_any.at[r], state_ref.at[r]) for r in range(prompts)], state_sem)
+    copies[0].wait()
+    copies[1].wait()
+    heads = HALF // HD
+    for g in range(heads):
+        query_ref[g * rows : (g + 1) * rows, :HD] = recv_ref[:, g * HD : (g + 1) * HD]
+        query_ref[g * rows : (g + 1) * rows, HD:] = hot_ref[...]
+    for copy in copies[2:6]:
         copy.wait()
-    rows = recv_ref.shape[0]
-    holders, keys = pages_ref.shape[0], pages_ref.shape[1]
-    prompts, width = state_ref.shape[0], state_ref.shape[1]
-    for n in range(holders):
-        tag = tag_ref[n]
-        for b in range(keys // LANES):
-            mine = jnp.broadcast_to(tag[b : b + 1, :], (rows, LANES))
-            bias[n, :, b * LANES : (b + 1) * LANES] = jnp.where(req_ref[...] == mine, 0.0, NONE)
-    for copy in smalls:
+    keys = key_ref.shape[0]
+    chunk = min(keys, 2 * NS)
+    widest = jnp.full((heads * rows, LANES), NONE, f32)
+    for k in range(0, keys, chunk):
+        scores = dot_nt(query_ref[...], key_ref[k : k + chunk, :])
+        score_ref[:, k : k + chunk] = scores
+        for b in range(0, chunk, LANES):
+            widest = jnp.maximum(widest, scores[:, b : b + LANES])
+    highest = jnp.max(widest, axis=1, keepdims=True)
+    for copy in copies[6:]:
         copy.wait()
+    total = jnp.zeros((heads * rows, LANES), f32)
+    value = jnp.zeros((heads * rows, HD), f32)
+    for k in range(0, keys, chunk):
+        weight = jnp.exp2((score_ref[:, k : k + chunk] - highest) * SCORE)
+        for b in range(0, chunk, LANES):
+            total = total + weight[:, b : b + LANES]
+        value = value + jnp.dot(weight.astype(bf16), value_ref[k : k + chunk, :], preferred_element_type=f32)
+    total = jnp.sum(total, axis=1, keepdims=True)
+    value = value / total
+    result = jnp.where(highest > 0.5 * MATCH, (highest - MATCH) * SCORE + jnp.log2(total), NONE)
     lane = iota((rows, LANES), 1)
     sums = jnp.zeros((rows, LANES), f32)
-    values = []
-    for g in range(HALF // HD):
-        query = recv_ref[:, g * HD : (g + 1) * HD]
-        scores = [dot_nt(query, pages_ref[n, :, :HD]) * SCORE + bias[n] for n in range(holders)]
-        highest = jnp.full((rows, 1), FLOOR, f32)
-        for one in scores:
-            highest = jnp.maximum(highest, jnp.max(one, axis=1, keepdims=True))
-        total = jnp.zeros((rows, 1), f32)
-        value = jnp.zeros((rows, HD), f32)
-        for n in range(holders):
-            weight = jnp.exp2(scores[n] - highest)
-            total = total + jnp.sum(weight, axis=1, keepdims=True)
-            value = value + jnp.dot(weight.astype(bf16), pages_ref[n, :, HD:], preferred_element_type=f32)
-        some = total > 0.0
-        safe = jnp.where(some, total, 1.0)
-        values.append(value / safe)
-        sums = jnp.where(lane % 4 == g, highest + jnp.log2(safe), sums)
+    for g in range(heads):
+        sums = jnp.where(lane % 4 == g, result[g * rows : (g + 1) * rows], sums)
     high = sums.astype(bf16).astype(f32)
     rest = sums - high
     middle = rest.astype(bf16).astype(f32)
@@ -342,12 +389,10 @@
     pair = iota((rows, LANES), 0) % SUB
     pieces = jnp.where((lane // 16 == pair) & (piece < 3), pieces, 0.0)
     packed = jnp.sum(pieces.reshape(rows // SUB, SUB, LANES), axis=1, keepdims=True)
-    packed = jnp.broadcast_to(packed, (rows // SUB, SUB, LANES)).reshape(rows, LANES)
-    values[0] = jnp.where(pair == SUMS_ROW, packed, values[0])
-    for g in range(HALF // HD):
-        out_ref[:, g * HD : (g + 1) * HD] = values[g].astype(bf16)
-
-    readout = recv_ref[:, HALF:].astype(f32)
+
+    given = recv_ref[...].astype(f32).reshape(rows // SUB, SUB, recv_ref.shape[1])
+    ending = lift(given, spare(heads + 1, 0))
+    readout = jnp.concatenate([given[..., HALF:], ending], axis=-1).reshape(rows, NS)
     target = jnp.concatenate([req_ref[...], req_ref[...]], axis=-1)
     found = jnp.zeros((rows, width), f32)
     for r in range(prompts):
@@ -356,7 +401,17 @@
         found = found + dot_nt(picked, state_ref[r])
     if width < LANES:
         found = jnp.concatenate([found, jnp.zeros((rows, LANES - width), f32)], axis=-1)
-    out_ref[:, HALF:] = found.astype(bf16)
+    blocks = [value[g * rows : (g + 1) * rows] for g in range(heads)]
+    blocks += [found[:, b : b + LANES] for b in range(0, found.shape[1], LANES)]
+    blocks = [one.reshape(rows // SUB, SUB, LANES) for one in blocks]
+    row = iota((rows // SUB, SUB, LANES), 1)
+    last = blocks.pop()
+    blocks[0] = jnp.where(row == PAIRS, jnp.broadcast_to(packed, row.shape), blocks[0])
+    for n, (at, b) in enumerate(spare(len(blocks), 1)):
+        one = jnp.broadcast_to(last[:, n : n + 1, :], row.shape)
+        blocks[b] = jnp.where(row == at, one, blocks[b])
+    for b, one in enumerate(blocks):
+        out_ref[:, b * LANES : (b + 1) * LANES] = one.reshape(rows, LANES).astype(bf16)
 
 
 def prompt_kernel(
@@ -580,8 +635,12 @@
     ways = owners // KVH
     steps, rows = mixer_ref.shape[0], mixer_ref.shape[1]
     for d in range(0, owners, 2):
-        found = back_ref[d * SUB : (d + 2) * SUB, HALF : HALF + width].astype(f32)
-        found = jnp.concatenate([found[:SUB], found[SUB:]], axis=-1)
+        block = back_ref[d * SUB : (d + 2) * SUB, :].astype(f32).reshape(2, SUB, back_ref.shape[1])
+        ending = lift(block, spare(back_ref.shape[1] // LANES, 1))
+        if back_ref.shape[1] > HALF:
+            ending = jnp.concatenate([block[..., HALF:], ending], axis=-1)
+        found = ending[..., :width]
+        found = jnp.concatenate([found[0], found[1]], axis=-1)
         columns = slice(d * width, (d + 2) * width)
         mixed[:, columns] = found * fade_ref[:, columns] + local_ref[:, columns]
     for k in range(steps):
@@ -592,7 +651,7 @@
         blocks, pieces = [], []
         for d in range(v * ways, (v + 1) * ways, 2):
             block = back_ref[d * SUB : (d + 2) * SUB, :HALF].astype(f32)
-            packed = block[:, :LANES].reshape(2, SUB, LANES)[:, SUMS_ROW : SUMS_ROW + 1, :]
+            packed = block[:, :LANES].reshape(2, SUB, LANES)[:, PAIRS : PAIRS + 1, :]
             blocks.append(block)
             pieces.append(jnp.where(mine, jnp.broadcast_to(packed, (2, SUB, LANES)), 0.0))
         for g in range(HALF // HD):
@@ -678,7 +737,7 @@
     other_pages = lax.ppermute(cache_pages, "heads", [(d, d + 1 - 2 * (d % 2)) for d in range(owners)])
     send = call(
         functools.partial(pack_kernel, group, ways),
-        shape((all_rows, HALF + NS), bf16),
+        shape((all_rows, HALF + LANES), bf16),
         [hbm, hbm],
         vmem,
         [
@@ -686,6 +745,7 @@
             like(vmem, step_c),
             vmem((SUB, queries.shape[2]), f32),
             vmem((SUB, step_c.shape[2]), f32),
+            vmem((step_c.shape[2] // NS, SUB, HALF + LANES), f32),
             sems(2),
         ],
         (0, 1 << 19),
@@ -703,20 +763,22 @@
     ]
     masks = vmem((levels, length, length), bf16)
     work = 2 * width * length * NS
-    states, tag, requests, early_out = call(
+    states, marks, hot, requests, early_out = call(
         state_kernel,
         (
             shape((prompts, width, NS), bf16),
-            shape((2, SUB, LANES), jnp.int32),
+            shape((2, keys, LANES), bf16),
+            shape((all_rows, LANES), bf16),
             shape((all_rows, LANES), jnp.int32),
             shape(prompt_x.shape, bf16),
         ),
         [hbm] * 10,
-        (hbm, vmem, vmem, hbm),
+        (hbm, hbm, vmem, vmem, hbm),
         block
-        + [vmem((prompts, group, length), f32), masks, vmem((prompts, width, NS), bf16)]
+        + [vmem((prompts, group, length), f32), masks]
+        + [vmem((prompts, width, NS), bf16), vmem((2, keys, LANES), bf16)]
         + [like(smem, one) for one in (decay_rate, skip_gain, lengths, owner_list, page_table, row_slot)]
-        + [like(vmem, prompt_dt), sem, sem, sem, sem, sem, sems(7)],
+        + [like(vmem, prompt_dt), sem, sem, sem, sem, sem, pltpu.SemaphoreType.DMA, sems(7)],
         (work * (prompts + 5 * EARLY), 6 << 20),
     )(
         decay_rate,
@@ -733,25 +795,28 @@
 
     back = call(
         serve_kernel,
-        shape((all_rows, HALF + max(LANES, width)), bf16),
-        [hbm] * 6,
+        shape((all_rows, HALF + max(LANES, width) - LANES), bf16),
+        [hbm] * 7,
         vmem,
         [
             like(vmem, recv),
-            vmem((2, keys, 2 * HD), bf16),
-            like(vmem, tag),
+            vmem((2 * keys, HD + LANES), bf16),
+            vmem((2 * keys, HD), bf16),
+            like(vmem, hot),
             like(vmem, requests),
             like(vmem, states),
-            vmem((2, all_rows, keys), f32),
+            vmem((HALF // HD * all_rows, HD + LANES), bf16),
+            vmem((HALF // HD * all_rows, 2 * keys), f32),
             sem,
-            sems(5),
+            sems(9),
         ],
         (8 * all_rows * keys * HD, 4 << 20),
     )(
         recv,
         cache_pages.reshape(keys, 2 * HD),
         other_pages.reshape(keys, 2 * HD),
-        tag,
+        marks,
+        hot,
         requests,
         states,
     )

time: 41.9 us -> 41.5 us (level)
  waiting for transfers between devices: 3.33 us -> 2.24 us
  starting transfers between devices: 11.8 us -> 12.3 us
    all_to_all x1, waiting for transfers between devices: 1.98 us -> 1.33 us  [on_device(): lax.all_to_all(send, 'heads', split_axis=0, concat_axis=0, tiled=True)]
    all_to_all x1, starting transfers between devices: 4.2 us -> 4.69 us  [on_device(): lax.all_to_all(back, 'heads', split_axis=0, concat_axis=0, tiled=True)]
    all_to_all x1, waiting for transfers between devices: 1.35 us -> 0.9 us  [on_device(): lax.all_to_all(back, 'heads', split_axis=0, concat_axis=0, tiled=True)]
  transfers between devices with their start and end apart: 3 -> 3, of which waited for: 2 -> 2; matrix products, arithmetic and copies ran while one was open for 0% -> 0% of each run, Pallas kernels for 42% -> 43%
where the time goes in v3:
time: 41.5 us; the launch traced here: 41.2 us
  Pallas kernels  25.9 us (62%)
  starting transfers between devices  12.3 us (30%)
  waiting for transfers between devices  2.24 us (5%)
  between operations  0.68 us (2%)
    pallas_call x1, Pallas kernels, on_device(): call(prompt_kernel, (shape(prompt_x.shape, bf16), shape((KVH, count, HD),...  8.67 us
    pallas_call x1, Pallas kernels, on_device(): call(state_kernel, (shape((prompts, width, NS), bf16), shape((2, keys, LA...  7.18 us
    all_to_all x1, starting transfers between devices, on_device(): lax.all_to_all(send, 'heads', split_axis=0, concat_axis=0, tiled=True)  7.1 us
    pallas_call x1, Pallas kernels, on_device(): call(serve_kernel, shape((all_rows, HALF + max(LANES, width) - LANES), bf...  6.03 us
    all_to_all x1, starting transfers between devices, on_device(): lax.all_to_all(back, 'heads', split_axis=0, concat_axis=0, tiled=True)  4.69 us
    pallas_call x1, Pallas kernels, on_device(): call(functools.partial(merge_kernel, width), (shape(step_x.shape, bf16),...  2.36 us
    pallas_call x1, Pallas kernels, on_device(): call(functools.partial(pack_kernel, group, ways), shape((all_rows, HALF +...  1.68 us
    all_to_all x1, waiting for transfers between devices, on_device(): lax.all_to_all(send, 'heads', split_axis=0, concat_axis=0, tiled=True)  1.33 us
  transfers between devices with their start and end apart: 3, of which 2 were waited for; matrix products, arithmetic and copies ran while one was open for 0% of the time, Pallas kernels for 43%

profile of v3, /device:TPU:0, one launch (start us, length us, event | category | flops | bytes accessed | tf_op | source)
XLA Modules:
  0.0 41.2 jit_solution(18036321546476442131)
XLA Ops:
  0.6 0.5 %collective-permute-start = (bf16[64,16,256]{2,1,0:T(8,128)(2,1)}, bf16[64,16,256]{2,1,0:T(8,128)(2,1)}, u32[]{:S(2)}, u32[]{:S(2)}) collective-permute-start(bf16[64,16,256]{2,1,0:T(8,128)(2,1)} %param.26), channel_id=1, source_target_pairs={{0,1},{1,0},{2,3},{3,2},{4,5},{5,4},{6,7},{7,6},{8,9},{9,8},{10,11... | collective-permute-start | bytes 1572872 | tf_op jit(solution)/shard_map/ppermute | solution.py:737
  1.1 1.7 %shard_map.184.send_any = bf16[128,640]{1,0:T(8,128)(2,1)} custom-call(bf16[3,2,8192]{2,1,0:T(2,128)(2,1)} %bitcast.21, bf16[3,2,1024]{2,1,0:T(2,128)(2,1)} %bitcast.22), custom_call_target="tpu_custom_call" | custom-call | bytes 524288 | tf_op jit(solution)/shard_map/pallas_call | solution.py:738
  2.8 7.1 %all-to-all-start = ((bf16[16,8,640]{2,1,0:T(8,128)(2,1)}), bf16[16,8,640]{2,1,0:T(8,128)(2,1)}, u32[]{:S(2)}, u32[]{:S(2)}) async-start(bf16[16,8,640]{2,1,0:T(8,128)(2,1)} %bitcast.18), calls=%async_computation | async-start | bytes 327680 | tf_op jit(solution)/shard_map/all_to_all | solution.py:753
  9.9 7.2 %shard_map.185 = (bf16[8,512,256]{2,1,0:T(8,128)(2,1)}, bf16[2,1024,128]{2,1,0:T(8,128)(2,1)}, bf16[128,128]{1,0:T(8,128)(2,1)}, s32[128,128]{1,0:T(8,128)}, bf16[8,512,256]{2,1,0:T(8,128)(2,1)}) custom-call(f32[128]{0:T(128)} %rate_any.3, f32[128]{0:T(128)} %skip_any.3, s32[8]{0:T(128)} %len_any.3, s32[2,16]{1,0:T(2,128)} %bitcast.29, s32[8,128]{1,0:T(8,128)} %table_any.1, ...), custom_call_target="tpu_custom_call" | custom-call | flops 1207959552 | bytes 6291456 | tf_op jit(solution)/shard_map/pallas_call | solution.py:766
  17.1 1.3 %all-to-all-done = bf16[16,8,640]{2,1,0:T(8,128)(2,1)} async-done(((bf16[16,8,640]{2,1,0:T(8,128)(2,1)}), bf16[16,8,640]{2,1,0:T(8,128)(2,1)}, u32[]{:S(2)}, u32[]{:S(2)}) %all-to-all-start) | async-done | bytes 163872 | tf_op jit(solution)/shard_map/all_to_all | solution.py:753
  18.5 0.0 collective-permute-done
  18.5 6.0 %shard_map.186.after_any = bf16[128,896]{1,0:T(8,128)(2,1)} custom-call(bf16[128,640]{1,0:T(8,128)(2,1)} %bitcast.9.recv_any, bf16[1024,256]{1,0:T(8,128)(2,1)} %bitcast.19, bf16[1024,256]{1,0:T(8,128)(2,1)} %bitcast.11.other_any, bf16[2,1024,128]{2,1,0:T(8,128)(2,1)} %get-tuple-element.15.mark_any, bf16[128,128]{1,0:T(8,128)(2,1)} %get-tuple-element.16.hot_any, ...), custom_call_target="tpu_custom_call" | custom-call | flops 134217728 | bytes 4194304 | tf_op jit(solution)/shard_map/pallas_call | solution.py:796
  24.5 4.7 %all-to-all-start.1 = ((bf16[16,8,896]{2,1,0:T(8,128)(2,1)}), bf16[16,8,896]{2,1,0:T(8,128)(2,1)}, u32[]{:S(2)}, u32[]{:S(2)}) async-start(bf16[16,8,896]{2,1,0:T(8,128)(2,1)} %bitcast.17), calls=%async_computation.1 | async-start | bytes 458752 | tf_op jit(solution)/shard_map/all_to_all | solution.py:823
  29.2 8.7 %shard_map.187 = (bf16[8,512,256]{2,1,0:T(8,128)(2,1)}, f32[8,64,128]{2,1,0:T(8,128)}, f32[8,64,128]{2,1,0:T(8,128)}, f32[8,8192]{1,0:T(8,128)}, f32[8,8192]{1,0:T(8,128)}) custom-call(f32[128]{0:T(128)} %rate_any.3, f32[128]{0:T(128)} %skip_any.3, s32[8]{0:T(128)} %len_any.3, bf16[8,8,256]{2,1,0:T(8,128)(2,1)} %dt_any.3, ...), custom_call_target="tpu_custom_call", output_to_operand_aliasing={{0}: (16, {})} | custom-call | flops 2013265920 | bytes 8388608 | tf_op jit(solution)/shard_map/pallas_call | solution.py:828
  37.9 0.9 %all-to-all-done.1 = bf16[16,8,896]{2,1,0:T(8,128)(2,1)} async-done(((bf16[16,8,896]{2,1,0:T(8,128)(2,1)}), bf16[16,8,896]{2,1,0:T(8,128)(2,1)}, u32[]{:S(2)}, u32[]{:S(2)}) %all-to-all-start.1) | async-done | bytes 229408 | tf_op jit(solution)/shard_map/all_to_all | solution.py:823
  38.8 2.4 %shard_map.188 = (bf16[3,2,8192]{2,1,0:T(2,128)(2,1)}, bf16[3,2,8192]{2,1,0:T(2,128)(2,1)}) custom-call(bf16[128,896]{1,0:T(8,128)(2,1)} %bitcast.14.back_any, f32[8,64,128]{2,1,0:T(8,128)} %get-tuple-element.21.own_any, f32[8,64,128]{2,1,0:T(8,128)} %get-tuple-element.22.ownsum_any, f32[8,8192]{1,0:T(8,128)} %get-tuple-element.23.fade_any, ...), custom_call_target="tpu_custom_call" | custom-call | bytes 2097152 | tf_op jit(solution)/shard_map/pallas_call | solution.py:885
Async XLA Ops:
  0.6 17.8 %collective-permute-start = (bf16[64,16,256]{2,1,0:T(8,128)(2,1)}, bf16[64,16,256]{2,1,0:T(8,128)(2,1)}, u32[]{:S(2)}, u32[]{:S(2)}) collective-permute-start(bf16[64,16,256]{2,1,0:T(8,128)(2,1)} %param.26), channel_id=1, source_target_pairs={{0,1},{1,0},{2,3},{3,2},{4,5},{5,4},{6,7},{7,6},{8,9},{9,8},{10,11... | collective-permute-start | bytes 1572872 | tf_op jit(solution)/shard_map/ppermute | solution.py:737
  2.8 15.6 %all-to-all-start = ((bf16[16,8,640]{2,1,0:T(8,128)(2,1)}), bf16[16,8,640]{2,1,0:T(8,128)(2,1)}, u32[]{:S(2)}, u32[]{:S(2)}) async-start(bf16[16,8,640]{2,1,0:T(8,128)(2,1)} %bitcast.18), calls=%async_computation | async-start | bytes 327680 | tf_op jit(solution)/shard_map/all_to_all | solution.py:753
  24.5 14.3 %all-to-all-start.1 = ((bf16[16,8,896]{2,1,0:T(8,128)(2,1)}), bf16[16,8,896]{2,1,0:T(8,128)(2,1)}, u32[]{:S(2)}, u32[]{:S(2)}) async-start(bf16[16,8,896]{2,1,0:T(8,128)(2,1)} %bitcast.17), calls=%async_computation.1 | async-start | bytes 458752 | tf_op jit(solution)/shard_map/all_to_all | solution.py:823

commit v4 on v3

--- a/solution.py
+++ b/solution.py
@@ -58,6 +58,30 @@
     return found
 
 
+def exchange(blocks):
+    if len(blocks) == 1:
+        return [lax.all_to_all(blocks[0], "heads", split_axis=0, concat_axis=0, tiled=True)]
+    count = len(blocks)
+    return [blocks[0]] + [
+        lax.ppermute(blocks[n], "heads", [(d, (d + n) % count) for d in range(count)]) for n in range(1, count)
+    ]
+
+
+def leave(held, outs):
+    if len(outs) == 1:
+        return [(held, outs[0])]
+    me = lax.axis_index("heads")
+    return [(held.at[lax.rem(me + n, len(outs))], out) for n, out in enumerate(outs)]
+
+
+def arrive(ins, held):
+    if len(ins) == 1:
+        return [(ins[0], held)]
+    me = lax.axis_index("heads")
+    count = len(ins)
+    return [(one, held.at[lax.rem(me + count - n, count)]) for n, one in enumerate(ins)]
+
+
 def fetches(pairs, sems):
     copies = [pltpu.make_async_copy(src, dst, sems.at[n]) for n, (src, dst) in enumerate(pairs)]
     for copy in copies:
@@ -65,8 +89,9 @@
     return copies
 
 
-def pack_kernel(group, ways, q_any, c_any, out_ref, q_ref, c_ref, q_held, c_held, rest, sems):
-    owners = out_ref.shape[0] // SUB
+def pack_kernel(group, ways, q_any, c_any, *refs):
+    *outs, held, q_ref, c_ref, q_held, c_held, rest, sems = refs
+    owners = held.shape[0]
     for copy in fetches([(q_any, q_ref), (c_any, c_ref)], sems):
         copy.wait()
     stack_rows(q_ref, q_held)
@@ -85,9 +110,11 @@
         v, e = d // ways, (d * group) // HPG
         low = jnp.where(real, q_held[:, v * span : v * span + HALF], rest[e, :, :HALF])
         high = jnp.where(real, q_held[:, v * span + HALF : (v + 1) * span], rest[e, :, :HALF])
-        out_ref[d * SUB : (d + 2) * SUB, :HALF] = jnp.concatenate([low, high], axis=0).astype(bf16)
-        end = rest[e, :, HALF:]
-        out_ref[d * SUB : (d + 2) * SUB, HALF:] = jnp.concatenate([end, end], axis=0).astype(bf16)
+        for n, one in enumerate((low, high)):
+            held[d + n, :, :HALF] = one.astype(bf16)
+            held[d + n, :, HALF:] = rest[e, :, HALF:].astype(bf16)
+    for copy in fetches(leave(held, outs), sems):
+        copy.wait()
 
 
 def head_factors(first, dt_ref, rate_ref, skip_ref, len_ref, levels, w_in, w_out, w_skip, w_tail):
@@ -309,33 +336,31 @@
     mark_copy.wait()
 
 
-def serve_kernel(
-    recv_any,
-    pages_any,
-    other_any,
-    mark_any,
-    hot_any,
-    req_any,
-    state_any,
-    out_ref,
-    recv_ref,
-    key_ref,
-    value_ref,
-    hot_ref,
-    req_ref,
-    state_ref,
-    query_ref,
-    score_ref,
-    state_sem,
-    sems,
-):
-    rows = recv_ref.shape[0]
+def serve_kernel(blocks_in, *refs):
+    recv_anys, refs = refs[:blocks_in], refs[blocks_in:]
+    pages_any, other_any, mark_any, hot_any, req_any, state_any, *refs = refs
+    outs, refs = refs[:blocks_in], refs[blocks_in:]
+    (
+        back_held,
+        recv_held,
+        key_ref,
+        value_ref,
+        hot_ref,
+        req_ref,
+        state_ref,
+        query_ref,
+        score_ref,
+        recv_sem,
+        state_sem,
+        sems,
+    ) = refs
+    rows = recv_held.shape[0] * SUB
     held = pages_any.shape[0]
     prompts, width = state_ref.shape[0], state_ref.shape[1]
     mine, other = pl.ds(0, held), pl.ds(held, held)
+    received = fetches(arrive(recv_anys, recv_held), recv_sem)
     copies = fetches(
         [
-            (recv_any, recv_ref),
             (hot_any, hot_ref),
             (pages_any.at[:, pl.ds(0, HD)], key_ref.at[mine, pl.ds(0, HD)]),
             (other_any.at[:, pl.ds(0, HD)], key_ref.at[other, pl.ds(0, HD)]),
@@ -348,13 +373,16 @@
         sems,
     )
     states = fetches([(state_any.at[r], state_ref.at[r]) for r in range(prompts)], state_sem)
+    for copy in received:
+        copy.wait()
     copies[0].wait()
-    copies[1].wait()
     heads = HALF // HD
+    given = recv_held[...].astype(f32)
     for g in range(heads):
-        query_ref[g * rows : (g + 1) * rows, :HD] = recv_ref[:, g * HD : (g + 1) * HD]
+        one = given[..., g * HD : (g + 1) * HD].reshape(rows, HD)
+        query_ref[g * rows : (g + 1) * rows, :HD] = one.astype(bf16)
         query_ref[g * rows : (g + 1) * rows, HD:] = hot_ref[...]
-    for copy in copies[2:6]:
+    for copy in copies[1:5]:
         copy.wait()
     keys = key_ref.shape[0]
     chunk = min(keys, 2 * NS)
@@ -365,7 +393,7 @@
         for b in range(0, chunk, LANES):
             widest = jnp.maximum(widest, scores[:, b : b + LANES])
     highest = jnp.max(widest, axis=1, keepdims=True)
-    for copy in copies[6:]:
+    for copy in copies[5:]:
         copy.wait()
     total = jnp.zeros((heads * rows, LANES), f32)
     value = jnp.zeros((heads * rows, HD), f32)
@@ -390,7 +418,6 @@
     pieces = jnp.where((lane // 16 == pair) & (piece < 3), pieces, 0.0)
     packed = jnp.sum(pieces.reshape(rows // SUB, SUB, LANES), axis=1, keepdims=True)
 
-    given = recv_ref[...].astype(f32).reshape(rows // SUB, SUB, recv_ref.shape[1])
     ending = lift(given, spare(heads + 1, 0))
     readout = jnp.concatenate([given[..., HALF:], ending], axis=-1).reshape(rows, NS)
     target = jnp.concatenate([req_ref[...], req_ref[...]], axis=-1)
@@ -411,7 +438,9 @@
         one = jnp.broadcast_to(last[:, n : n + 1, :], row.shape)
         blocks[b] = jnp.where(row == at, one, blocks[b])
     for b, one in enumerate(blocks):
-        out_ref[:, b * LANES : (b + 1) * LANES] = one.reshape(rows, LANES).astype(bf16)
+        back_held[:, :, b * LANES : (b + 1) * LANES] = one.astype(bf16)
+    for copy in fetches(leave(back_held, outs), recv_sem):
+        copy.wait()
 
 
 def prompt_kernel(
@@ -421,7 +450,7 @@
     dt_any,
     rates_any,
     skips_any,
-    send_any,
+    q_any,
     fresh_any,
     sx_any,
     sb_any,
@@ -446,6 +475,7 @@
     w_skip,
     masks,
     fresh_held,
+    q_held,
     c_rows,
     x_rows,
     rate_ref,
@@ -454,7 +484,7 @@
     dt_ref,
     rates_ref,
     skips_ref,
-    send_ref,
+    q_ref,
     fresh_ref,
     sx_ref,
     sb_ref,
@@ -475,7 +505,7 @@
             (len_any, len_ref),
             (rates_any, rates_ref),
             (skips_any, skips_ref),
-            (send_any, send_ref),
+            (q_any, q_ref),
             (fresh_any, fresh_ref),
             (sx_any, sx_ref),
             (sb_any, sb_ref),
@@ -519,15 +549,15 @@
         return 0
 
     lax.fori_loop(EARLY, prompts, one, 0, unroll=2)
-    own_attention(send_ref, fresh_ref, fresh_held, own_ref, ownsum_ref)
+    own_attention(q_ref, fresh_ref, q_held, fresh_held, own_ref, ownsum_ref)
     own_mixer(rates_ref, skips_ref, sx_ref, sb_ref, sc_ref, sdt_ref, c_rows, x_rows, fade_ref, local_ref)
     for r in range(EARLY, prompts):
         out_copy(r).wait()
 
 
-def own_attention(send_ref, fresh_ref, fresh_held, own_ref, ownsum_ref):
+def own_attention(q_ref, fresh_ref, q_held, fresh_held, own_ref, ownsum_ref):
     steps, rows = fresh_ref.shape[0], fresh_ref.shape[1]
-    ways = send_ref.shape[0] // SUB // KVH
+    stack_rows(q_ref, q_held)
     stack_rows(fresh_ref, fresh_held)
     count = HALF // HD * 2 * SUB
     pair = iota((count, SUB), 0) % SUB
@@ -535,8 +565,8 @@
     seen = (key % rows == pair % rows) & (key <= pair) & (key < rows * steps)
     seen = seen | ((pair >= rows * steps) & (key == 0))
     for v in range(KVH):
-        block = send_ref[v * ways * SUB : (v * ways + 2) * SUB]
-        query = jnp.concatenate([block[:, g * HD : (g + 1) * HD] for g in range(HALF // HD)], axis=0)
+        starts = [v * 2 * HALF + half + g for g in range(0, HALF, HD) for half in (0, HALF)]
+        query = jnp.concatenate([q_held[:, at : at + HD] for at in starts], axis=0).astype(bf16)
         keys = fresh_held[:, v * HD : (v + 1) * HD].astype(bf16)
         values = fresh_held[:, (KVH + v) * HD : (KVH + v + 1) * HD].astype(bf16)
         scores = jnp.where(seen, dot_nt(query, keys) * SCORE, NONE)
@@ -601,27 +631,13 @@
         local_ref[:, columns] = value
 
 
-def merge_kernel(
-    width,
-    back_any,
-    own_any,
-    ownsum_any,
-    fade_any,
-    local_any,
-    mixer_ref,
-    attention_ref,
-    back_ref,
-    own_ref,
-    ownsum_ref,
-    fade_ref,
-    local_ref,
-    mixed,
-    attended,
-    sems,
-):
-    copies = fetches(
+def merge_kernel(width, blocks_in, *refs):
+    back_anys, refs = refs[:blocks_in], refs[blocks_in:]
+    own_any, ownsum_any, fade_any, local_any, mixer_ref, attention_ref, *refs = refs
+    back_ref, own_ref, ownsum_ref, fade_ref, local_ref, mixed, attended, back_sem, sems = refs
+    copies = fetches(arrive(back_anys, back_ref), back_sem)
+    copies += fetches(
         [
-            (back_any, back_ref),
             (own_any, own_ref),
             (ownsum_any, ownsum_ref),
             (fade_any, fade_ref),
@@ -631,13 +647,13 @@
     )
     for copy in copies:
         copy.wait()
-    owners = back_ref.shape[0] // SUB
+    owners = back_ref.shape[0]
     ways = owners // KVH
     steps, rows = mixer_ref.shape[0], mixer_ref.shape[1]
     for d in range(0, owners, 2):
-        block = back_ref[d * SUB : (d + 2) * SUB, :].astype(f32).reshape(2, SUB, back_ref.shape[1])
-        ending = lift(block, spare(back_ref.shape[1] // LANES, 1))
-        if back_ref.shape[1] > HALF:
+        block = back_ref[d : d + 2].astype(f32)
+        ending = lift(block, spare(back_ref.shape[2] // LANES, 1))
+        if back_ref.shape[2] > HALF:
             ending = jnp.concatenate([block[..., HALF:], ending], axis=-1)
         found = ending[..., :width]
         found = jnp.concatenate([found[0], found[1]], axis=-1)
@@ -650,9 +666,9 @@
     for v in range(KVH):
         blocks, pieces = [], []
         for d in range(v * ways, (v + 1) * ways, 2):
-            block = back_ref[d * SUB : (d + 2) * SUB, :HALF].astype(f32)
-            packed = block[:, :LANES].reshape(2, SUB, LANES)[:, PAIRS : PAIRS + 1, :]
-            blocks.append(block)
+            block = back_ref[d : d + 2, :, :HALF].astype(f32)
+            packed = block[:, PAIRS : PAIRS + 1, :LANES]
+            blocks.append(block.reshape(2 * SUB, HALF))
             pieces.append(jnp.where(mine, jnp.broadcast_to(packed, (2, SUB, LANES)), 0.0))
         for g in range(HALF // HD):
             part = slice(g * 2 * SUB, (g + 1) * 2 * SUB)
@@ -735,22 +751,26 @@
         return pltpu.SemaphoreType.DMA((count,))
 
     other_pages = lax.ppermute(cache_pages, "heads", [(d, d + 1 - 2 * (d % 2)) for d in range(owners)])
+    parts = owners if owners <= 16 else 1
+    piece = (SUB,) if parts > 1 else (owners, SUB)
+    moved = sems(max(parts, 2))
     send = call(
         functools.partial(pack_kernel, group, ways),
-        shape((all_rows, HALF + LANES), bf16),
+        (shape(piece + (HALF + LANES,), bf16),) * parts,
         [hbm, hbm],
-        vmem,
+        (hbm,) * parts,
         [
+            vmem((owners, SUB, HALF + LANES), bf16),
             like(vmem, queries),
             like(vmem, step_c),
             vmem((SUB, queries.shape[2]), f32),
             vmem((SUB, step_c.shape[2]), f32),
             vmem((step_c.shape[2] // NS, SUB, HALF + LANES), f32),
-            sems(2),
+            moved,
         ],
         (0, 1 << 19),
     )(queries, step_c)
-    recv = lax.all_to_all(send, "heads", split_axis=0, concat_axis=0, tiled=True)
+    recv = exchange(send)
 
     block = [
         vmem((prompts, width, length), bf16),
@@ -793,13 +813,15 @@
         prompt_c,
     )
 
+    returns = HALF + max(LANES, width) - LANES
     back = call(
-        serve_kernel,
-        shape((all_rows, HALF + max(LANES, width) - LANES), bf16),
-        [hbm] * 7,
-        vmem,
+        functools.partial(serve_kernel, parts),
+        (shape(piece + (returns,), bf16),) * parts,
+        [hbm] * (parts + 6),
+        (hbm,) * parts,
         [
-            like(vmem, recv),
+            vmem((owners, SUB, returns), bf16),
+            vmem((owners, SUB, HALF + LANES), bf16),
             vmem((2 * keys, HD + LANES), bf16),
             vmem((2 * keys, HD), bf16),
             like(vmem, hot),
@@ -807,12 +829,13 @@
             like(vmem, states),
             vmem((HALF // HD * all_rows, HD + LANES), bf16),
             vmem((HALF // HD * all_rows, 2 * keys), f32),
+            moved,
             sem,
-            sems(9),
+            sems(8),
         ],
         (8 * all_rows * keys * HD, 4 << 20),
     )(
-        recv,
+        *recv,
         cache_pages.reshape(keys, 2 * HD),
         other_pages.reshape(keys, 2 * HD),
         marks,
@@ -820,7 +843,7 @@
         requests,
         states,
     )
-    returned = lax.all_to_all(back, "heads", split_axis=0, concat_axis=0, tiled=True)
+    returned = exchange(back)
 
     count = HALF // HD * 2 * SUB
     channels = step_x.shape[2]
@@ -840,6 +863,7 @@
         + [
             masks,
             vmem((SUB, fresh_cache.shape[2]), f32),
+            vmem((SUB, queries.shape[2]), f32),
             vmem((SUB, step_c.shape[2]), f32),
             vmem((steps, SUB, channels), f32),
             like(smem, decay_rate),
@@ -848,7 +872,7 @@
             like(vmem, prompt_dt),
             like(vmem, rates),
             like(vmem, skips),
-            like(vmem, send),
+            like(vmem, queries),
             like(vmem, fresh_cache),
             like(vmem, step_x),
             like(vmem, step_b),
@@ -869,7 +893,7 @@
         prompt_dt,
         rates,
         skips,
-        send,
+        queries,
         fresh_cache,
         step_x,
         step_b,
@@ -878,19 +902,20 @@
         prompt_x,
         prompt_b,
         prompt_c,
-        back,
+        back[0],
         early_out,
     )
 
     mixer_out, attention_out = call(
-        functools.partial(merge_kernel, width),
+        functools.partial(merge_kernel, width, parts),
         (shape(step_x.shape, bf16), shape(queries.shape, bf16)),
-        [hbm] * 5,
+        [hbm] * (parts + 4),
         (vmem, vmem),
-        [like(vmem, one) for one in (returned, own, own_sum, fade, local)]
-        + [vmem((SUB, channels), f32), vmem((SUB, queries.shape[2]), f32), sems(5)],
+        [vmem((owners, SUB, returns), bf16)]
+        + [like(vmem, one) for one in (own, own_sum, fade, local)]
+        + [vmem((SUB, channels), f32), vmem((SUB, queries.shape[2]), f32), moved, sems(4)],
         (0, 2 << 20),
-    )(returned, own, own_sum, fade, local)
+    )(*returned, own, own_sum, fade, local)
     return (prompt_out, jnp.swapaxes(mixer_out, 0, 1), jnp.swapaxes(attention_out, 0, 1))
 
 

time: 41.5 us -> 73 us (1.76)
  starting transfers between devices: 12.3 us -> 40.1 us
  waiting for transfers between devices: 2.24 us -> 5.23 us
  Pallas kernels: 25.9 us -> 26.7 us
    ppermute x0 -> x30, starting transfers between devices: none -> 39.6 us  [exchange(): lax.ppermute(blocks[n], 'heads', [(d, (d + n) % count) for d in range(cou...]
    all_to_all x2 -> x0, starting transfers between devices: 11.8 us -> none  [the longest x1 7.1 us: on_device(): lax.all_to_all(send, 'heads', split_axis=0, concat_axis=0, tiled=True)]
    ppermute x0 -> x30, waiting for transfers between devices: none -> 5.23 us  [exchange(): lax.ppermute(blocks[n], 'heads', [(d, (d + n) % count) for d in range(cou...]
    all_to_all x2 -> x0, waiting for transfers between devices: 2.24 us -> none  [the longest x1 1.33 us: on_device(): lax.all_to_all(send, 'heads', split_axis=0, concat_axis=0, tiled=True)]
    pallas_call x3, Pallas kernels: 10.1 us -> 10.9 us  [the longest x1 6.58 us: on_device(): call(functools.partial(serve_kernel, parts), (shape(piece + (returns,), b...]
  transfers between devices with their start and end apart: 3 -> 31, of which waited for: 2 -> 4; matrix products, arithmetic and copies ran while one was open for 0% -> 0% of each run, Pallas kernels for 43% -> 24%
where the time goes in v4:
time: 73 us; the launch traced here: 72.8 us
  starting transfers between devices  40.1 us (55%)
  Pallas kernels  26.7 us (37%)
  waiting for transfers between devices  5.23 us (7%)
  between operations  0.78 us (1%)
    ppermute x30, starting transfers between devices, exchange(): lax.ppermute(blocks[n], 'heads', [(d, (d + n) % count) for d in range(cou...  39.6 us
    pallas_call x1, Pallas kernels, on_device(): call(prompt_kernel, (shape(prompt_x.shape, bf16), shape((KVH, count, HD),...  8.63 us
    pallas_call x1, Pallas kernels, on_device(): call(state_kernel, (shape((prompts, width, NS), bf16), shape((2, keys, LA...  7.16 us
    pallas_call x1, Pallas kernels, on_device(): call(functools.partial(serve_kernel, parts), (shape(piece + (returns,), b...  6.58 us
    ppermute x30, waiting for transfers between devices, exchange(): lax.ppermute(blocks[n], 'heads', [(d, (d + n) % count) for d in range(cou...  5.23 us
    pallas_call x1, Pallas kernels, on_device(): call(functools.partial(merge_kernel, width, parts), (shape(step_x.shape,...  2.52 us
    pallas_call x1, Pallas kernels, on_device(): call(functools.partial(pack_kernel, group, ways), (shape(piece + (HALF +...  1.8 us
  transfers between devices with their start and end apart: 31, of which 4 were waited for; matrix products, arithmetic and copies ran while one was open for 0% of the time, Pallas kernels for 24%

profile of v4, /device:TPU:0, one launch (start us, length us, event | category | flops | bytes accessed | tf_op | source)
XLA Modules:
  0.0 72.8 jit_solution(13140520142173828466)
XLA Ops:
  1.1 1.8 %shard_map.184 = (bf16[8,640]{1,0:T(8,128)(2,1)}, bf16[8,640]{1,0:T(8,128)(2,1)}, bf16[8,640]{1,0:T(8,128)(2,1)}, bf16[8,640]{1,0:T(8,128)(2,1)}, bf16[8,640]{1,...) custom-call(bf16[3,2,8192]{2,1,0:T(2,128)(2,1)} %bitcast.14, ...), custom_call_target="tpu_custom_call" | custom-call | bytes 524288 | tf_op jit(solution)/shard_map/pallas_call | solution.py:757
  3.1 3.0 %collective-permute-start.1 = (bf16[8,640]{1,0:T(8,128)(2,1)}, bf16[8,640]{1,0:T(8,128)(2,1)}, u32[]{:S(2)}, u32[]{:S(2)}) collective-permute-start(bf16[8,640]{1,0:T(8,128)(2,1)} %get-tuple-element.49), channel_id=1, source_target_pairs={{0,2},{1,3},{2,4},{3,5},{4,6},{5,7},{6,8},{7,9},{8,10},{9,11},{10,... | collective-permute-start | bytes 30728 | tf_op jit(solution)/shard_map/ppermute | solution.py:66
  6.0 2.0 %collective-permute-start.2 = (bf16[8,640]{1,0:T(8,128)(2,1)}, bf16[8,640]{1,0:T(8,128)(2,1)}, u32[]{:S(2)}, u32[]{:S(2)}) collective-permute-start(bf16[8,640]{1,0:T(8,128)(2,1)} %get-tuple-element.50), channel_id=1, source_target_pairs={{0,3},{1,4},{2,5},{3,6},{4,7},{5,8},{6,9},{7,10},{8,11},{9,12},{10... | collective-permute-start | bytes 30728 | tf_op jit(solution)/shard_map/ppermute | solution.py:66
  8.0 1.6 %collective-permute-start.3 = (bf16[8,640]{1,0:T(8,128)(2,1)}, bf16[8,640]{1,0:T(8,128)(2,1)}, u32[]{:S(2)}, u32[]{:S(2)}) collective-permute-start(bf16[8,640]{1,0:T(8,128)(2,1)} %get-tuple-element.51), channel_id=1, source_target_pairs={{0,4},{1,5},{2,6},{3,7},{4,8},{5,9},{6,10},{7,11},{8,12},{9,13},{1... | collective-permute-start | bytes 30728 | tf_op jit(solution)/shard_map/ppermute | solution.py:66
  9.6 0.7 %collective-permute-done.refs_1_ = bf16[8,640]{1,0:T(8,128)(2,1)} collective-permute-done((bf16[8,640]{1,0:T(8,128)(2,1)}, bf16[8,640]{1,0:T(8,128)(2,1)}, u32[]{:S(2)}, u32[]{:S(2)}) %collective-permute-start) | collective-permute-done | bytes 10272 | tf_op jit(solution)/shard_map/ppermute | solution.py:66
  11.4 3.9 %collective-permute-start.6 = (bf16[8,640]{1,0:T(8,128)(2,1)}, bf16[8,640]{1,0:T(8,128)(2,1)}, u32[]{:S(2)}, u32[]{:S(2)}) collective-permute-start(bf16[8,640]{1,0:T(8,128)(2,1)} %get-tuple-element.54), channel_id=1, source_target_pairs={{0,7},{1,8},{2,9},{3,10},{4,11},{5,12},{6,13},{7,14},{8,15},{9,0},... | collective-permute-start | bytes 30728 | tf_op jit(solution)/shard_map/ppermute | solution.py:66
  16.9 1.5 %collective-permute-start.9 = (bf16[8,640]{1,0:T(8,128)(2,1)}, bf16[8,640]{1,0:T(8,128)(2,1)}, u32[]{:S(2)}, u32[]{:S(2)}) collective-permute-start(bf16[8,640]{1,0:T(8,128)(2,1)} %get-tuple-element.57), channel_id=1, source_target_pairs={{0,10},{1,11},{2,12},{3,13},{4,14},{5,15},{6,0},{7,1},{8,2},{9,3},... | collective-permute-start | bytes 30728 | tf_op jit(solution)/shard_map/ppermute | solution.py:66
  18.4 3.0 %collective-permute-start.10 = (bf16[8,640]{1,0:T(8,128)(2,1)}, bf16[8,640]{1,0:T(8,128)(2,1)}, u32[]{:S(2)}, u32[]{:S(2)}) collective-permute-start(bf16[8,640]{1,0:T(8,128)(2,1)} %get-tuple-element.58), channel_id=1, source_target_pairs={{0,11},{1,12},{2,13},{3,14},{4,15},{5,0},{6,1},{7,2},{8,3},{9,4},{... | collective-permute-start | bytes 30728 | tf_op jit(solution)/shard_map/ppermute | solution.py:66
  21.3 1.7 %collective-permute-start.11 = (bf16[8,640]{1,0:T(8,128)(2,1)}, bf16[8,640]{1,0:T(8,128)(2,1)}, u32[]{:S(2)}, u32[]{:S(2)}) collective-permute-start(bf16[8,640]{1,0:T(8,128)(2,1)} %get-tuple-element.59), channel_id=1, source_target_pairs={{0,12},{1,13},{2,14},{3,15},{4,0},{5,1},{6,2},{7,3},{8,4},{9,5},{1... | collective-permute-start | bytes 30728 | tf_op jit(solution)/shard_map/ppermute | solution.py:66
  23.0 2.0 %collective-permute-start.13 = (bf16[8,640]{1,0:T(8,128)(2,1)}, bf16[8,640]{1,0:T(8,128)(2,1)}, u32[]{:S(2)}, u32[]{:S(2)}) collective-permute-start(bf16[8,640]{1,0:T(8,128)(2,1)} %get-tuple-element.61), channel_id=1, source_target_pairs={{0,14},{1,15},{2,0},{3,1},{4,2},{5,3},{6,4},{7,5},{8,6},{9,7},{10,... | collective-permute-start | bytes 30728 | tf_op jit(solution)/shard_map/ppermute | solution.py:66
  25.0 1.8 %collective-permute-start.14 = (bf16[8,640]{1,0:T(8,128)(2,1)}, bf16[8,640]{1,0:T(8,128)(2,1)}, u32[]{:S(2)}, u32[]{:S(2)}) collective-permute-start(bf16[8,640]{1,0:T(8,128)(2,1)} %get-tuple-element.62), channel_id=1, source_target_pairs={{0,15},{1,0},{2,1},{3,2},{4,3},{5,4},{6,5},{7,6},{8,7},{9,8},{10,9... | collective-permute-start | bytes 30728 | tf_op jit(solution)/shard_map/ppermute | solution.py:66
  26.8 7.2 %shard_map.185 = (bf16[8,512,256]{2,1,0:T(8,128)(2,1)}, bf16[2,1024,128]{2,1,0:T(8,128)(2,1)}, bf16[128,128]{1,0:T(8,128)(2,1)}, s32[128,128]{1,0:T(8,128)}, bf16[8,512,256]{2,1,0:T(8,128)(2,1)}) custom-call(f32[128]{0:T(128)} %rate_any.3, f32[128]{0:T(128)} %skip_any.3, s32[8]{0:T(128)} %len_any.3, s32[2,16]{1,0:T(2,128)} %bitcast.24, s32[8,128]{1,0:T(8,128)} %table_any.1, ...), custom_call_target="tpu_custom_call" | custom-call | flops 1207959552 | bytes 6291456 | tf_op jit(solution)/shard_map/pallas_call | solution.py:786
  34.0 6.6 %shard_map.186 = (bf16[8,896]{1,0:T(8,128)(2,1)}, bf16[8,896]{1,0:T(8,128)(2,1)}, bf16[8,896]{1,0:T(8,128)(2,1)}, bf16[8,896]{1,0:T(8,128)(2,1)}, bf16[8,896]{1,...) custom-call(bf16[8,640]{1,0:T(8,128)(2,1)} %get-tuple-element.47.ref, ...), custom_call_target="tpu_custom_call" | custom-call | flops 134217728 | bytes 4194304 | tf_op jit(solution)/shard_map/pallas_call | solution.py:817
  40.7 1.3 %collective-permute-start.17 = (bf16[8,896]{1,0:T(8,128)(2,1)}, bf16[8,896]{1,0:T(8,128)(2,1)}, u32[]{:S(2)}, u32[]{:S(2)}) collective-permute-start(bf16[8,896]{1,0:T(8,128)(2,1)} %get-tuple-element.71), channel_id=1, source_target_pairs={{0,2},{1,3},{2,4},{3,5},{4,6},{5,7},{6,8},{7,9},{8,10},{9,11},{10,... | collective-permute-start | bytes 43016 | tf_op jit(solution)/shard_map/ppermute | solution.py:66
  42.0 1.1 %collective-permute-start.18 = (bf16[8,896]{1,0:T(8,128)(2,1)}, bf16[8,896]{1,0:T(8,128)(2,1)}, u32[]{:S(2)}, u32[]{:S(2)}) collective-permute-start(bf16[8,896]{1,0:T(8,128)(2,1)} %get-tuple-element.72), channel_id=1, source_target_pairs={{0,3},{1,4},{2,5},{3,6},{4,7},{5,8},{6,9},{7,10},{8,11},{9,12},{10... | collective-permute-start | bytes 43016 | tf_op jit(solution)/shard_map/ppermute | solution.py:66
  43.6 3.2 %collective-permute-done.16.refs_1_ = bf16[8,896]{1,0:T(8,128)(2,1)} collective-permute-done((bf16[8,896]{1,0:T(8,128)(2,1)}, bf16[8,896]{1,0:T(8,128)(2,1)}, u32[]{:S(2)}, u32[]{:S(2)}) %collective-permute-start.16) | collective-permute-done | bytes 14368 | tf_op jit(solution)/shard_map/ppermute | solution.py:66
  47.5 2.0 %collective-permute-start.22 = (bf16[8,896]{1,0:T(8,128)(2,1)}, bf16[8,896]{1,0:T(8,128)(2,1)}, u32[]{:S(2)}, u32[]{:S(2)}) collective-permute-start(bf16[8,896]{1,0:T(8,128)(2,1)} %get-tuple-element.76), channel_id=1, source_target_pairs={{0,7},{1,8},{2,9},{3,10},{4,11},{5,12},{6,13},{7,14},{8,15},{9,0},... | collective-permute-start | bytes 43016 | tf_op jit(solution)/shard_map/ppermute | solution.py:66
  49.5 2.3 %collective-permute-start.23 = (bf16[8,896]{1,0:T(8,128)(2,1)}, bf16[8,896]{1,0:T(8,128)(2,1)}, u32[]{:S(2)}, u32[]{:S(2)}) collective-permute-start(bf16[8,896]{1,0:T(8,128)(2,1)} %get-tuple-element.77), channel_id=1, source_target_pairs={{0,8},{1,9},{2,10},{3,11},{4,12},{5,13},{6,14},{7,15},{8,0},{9,1},... | collective-permute-start | bytes 43016 | tf_op jit(solution)/shard_map/ppermute | solution.py:66
  51.9 1.6 %collective-permute-start.25 = (bf16[8,896]{1,0:T(8,128)(2,1)}, bf16[8,896]{1,0:T(8,128)(2,1)}, u32[]{:S(2)}, u32[]{:S(2)}) collective-permute-start(bf16[8,896]{1,0:T(8,128)(2,1)} %get-tuple-element.79), channel_id=1, source_target_pairs={{0,10},{1,11},{2,12},{3,13},{4,14},{5,15},{6,0},{7,1},{8,2},{9,3},... | collective-permute-start | bytes 43016 | tf_op jit(solution)/shard_map/ppermute | solution.py:66
  53.5 4.1 %collective-permute-start.26 = (bf16[8,896]{1,0:T(8,128)(2,1)}, bf16[8,896]{1,0:T(8,128)(2,1)}, u32[]{:S(2)}, u32[]{:S(2)}) collective-permute-start(bf16[8,896]{1,0:T(8,128)(2,1)} %get-tuple-element.80), channel_id=1, source_target_pairs={{0,11},{1,12},{2,13},{3,14},{4,15},{5,0},{6,1},{7,2},{8,3},{9,4},{... | collective-permute-start | bytes 43016 | tf_op jit(solution)/shard_map/ppermute | solution.py:66
  58.2 2.3 %collective-permute-start.29 = (bf16[8,896]{1,0:T(8,128)(2,1)}, bf16[8,896]{1,0:T(8,128)(2,1)}, u32[]{:S(2)}, u32[]{:S(2)}) collective-permute-start(bf16[8,896]{1,0:T(8,128)(2,1)} %get-tuple-element.83), channel_id=1, source_target_pairs={{0,14},{1,15},{2,0},{3,1},{4,2},{5,3},{6,4},{7,5},{8,6},{9,7},{10,... | collective-permute-start | bytes 43016 | tf_op jit(solution)/shard_map/ppermute | solution.py:66
  60.5 1.1 %collective-permute-start.30 = (bf16[8,896]{1,0:T(8,128)(2,1)}, bf16[8,896]{1,0:T(8,128)(2,1)}, u32[]{:S(2)}, u32[]{:S(2)}) collective-permute-start(bf16[8,896]{1,0:T(8,128)(2,1)} %get-tuple-element.84), channel_id=1, source_target_pairs={{0,15},{1,0},{2,1},{3,2},{4,3},{5,4},{6,5},{7,6},{8,7},{9,8},{10,9... | collective-permute-start | bytes 43016 | tf_op jit(solution)/shard_map/ppermute | solution.py:66
  61.6 8.6 %shard_map.187 = (bf16[8,512,256]{2,1,0:T(8,128)(2,1)}, f32[8,64,128]{2,1,0:T(8,128)}, f32[8,64,128]{2,1,0:T(8,128)}, f32[8,8192]{1,0:T(8,128)}, f32[8,8192]{1,0:T(8,128)}) custom-call(f32[128]{0:T(128)} %rate_any.3, f32[128]{0:T(128)} %skip_any.3, s32[8]{0:T(128)} %len_any.3, bf16[8,8,256]{2,1,0:T(8,128)(2,1)} %dt_any.3, ...), custom_call_target="tpu_custom_call", output_to_operand_aliasing={{0}: (16, {})} | custom-call | flops 2013265920 | bytes 8388608 | tf_op jit(solution)/shard_map/pallas_call | solution.py:851
  70.3 2.5 %shard_map.188 = (bf16[3,2,8192]{2,1,0:T(2,128)(2,1)}, bf16[3,2,8192]{2,1,0:T(2,128)(2,1)}) custom-call(bf16[8,896]{1,0:T(8,128)(2,1)} %get-tuple-element.67.after_any.refs_0_, bf16[8,896]{1,0:T(8,128)(2,1)} %collective-permute-done.16.refs_1_, bf16[8,896]{1,0:T(8,128)(2,1)} %collective-permute-done.17.refs_2_, ...), custom_call_target="tpu_custom_call" | custom-call | bytes 2097152 | tf_op jit(solution)/shard_map/pallas_call | solution.py:909
  (43 shorter events, 5.2 us)
Async XLA Ops:
  0.6 33.4 %collective-permute-start.15 = (bf16[64,16,256]{2,1,0:T(8,128)(2,1)}, bf16[64,16,256]{2,1,0:T(8,128)(2,1)}, u32[]{:S(2)}, u32[]{:S(2)}) collective-permute-start(bf16[64,16,256]{2,1,0:T(8,128)(2,1)} %param.26), channel_id=1, source_target_pairs={{0,1},{1,0},{2,3},{3,2},{4,5},{5,4},{6,7},{7,6},{8,9},{9,8},{10,11... | collective-permute-start | bytes 1572872 | tf_op jit(solution)/shard_map/ppermute | solution.py:753
  3.0 7.4 %collective-permute-start = (bf16[8,640]{1,0:T(8,128)(2,1)}, bf16[8,640]{1,0:T(8,128)(2,1)}, u32[]{:S(2)}, u32[]{:S(2)}) collective-permute-start(bf16[8,640]{1,0:T(8,128)(2,1)} %get-tuple-element.48), channel_id=1, source_target_pairs={{0,1},{1,2},{2,3},{3,4},{4,5},{5,6},{6,7},{7,8},{8,9},{9,10},{10,1... | collective-permute-start | bytes 30728 | tf_op jit(solution)/shard_map/ppermute | solution.py:66
  3.1 8.0 %collective-permute-start.1 = (bf16[8,640]{1,0:T(8,128)(2,1)}, bf16[8,640]{1,0:T(8,128)(2,1)}, u32[]{:S(2)}, u32[]{:S(2)}) collective-permute-start(bf16[8,640]{1,0:T(8,128)(2,1)} %get-tuple-element.49), channel_id=1, source_target_pairs={{0,2},{1,3},{2,4},{3,5},{4,6},{5,7},{6,8},{7,9},{8,10},{9,11},{10,... | collective-permute-start | bytes 30728 | tf_op jit(solution)/shard_map/ppermute | solution.py:66
  8.0 7.3 %collective-permute-start.3 = (bf16[8,640]{1,0:T(8,128)(2,1)}, bf16[8,640]{1,0:T(8,128)(2,1)}, u32[]{:S(2)}, u32[]{:S(2)}) collective-permute-start(bf16[8,640]{1,0:T(8,128)(2,1)} %get-tuple-element.51), channel_id=1, source_target_pairs={{0,4},{1,5},{2,6},{3,7},{4,8},{5,9},{6,10},{7,11},{8,12},{9,13},{1... | collective-permute-start | bytes 30728 | tf_op jit(solution)/shard_map/ppermute | solution.py:66
  11.4 7.0 %collective-permute-start.6 = (bf16[8,640]{1,0:T(8,128)(2,1)}, bf16[8,640]{1,0:T(8,128)(2,1)}, u32[]{:S(2)}, u32[]{:S(2)}) collective-permute-start(bf16[8,640]{1,0:T(8,128)(2,1)} %get-tuple-element.54), channel_id=1, source_target_pairs={{0,7},{1,8},{2,9},{3,10},{4,11},{5,12},{6,13},{7,14},{8,15},{9,0},... | collective-permute-start | bytes 30728 | tf_op jit(solution)/shard_map/ppermute | solution.py:66
  15.7 7.4 %collective-permute-start.8 = (bf16[8,640]{1,0:T(8,128)(2,1)}, bf16[8,640]{1,0:T(8,128)(2,1)}, u32[]{:S(2)}, u32[]{:S(2)}) collective-permute-start(bf16[8,640]{1,0:T(8,128)(2,1)} %get-tuple-element.56), channel_id=1, source_target_pairs={{0,9},{1,10},{2,11},{3,12},{4,13},{5,14},{6,15},{7,0},{8,1},{9,2},... | collective-permute-start | bytes 30728 | tf_op jit(solution)/shard_map/ppermute | solution.py:66
  18.4 6.6 %collective-permute-start.10 = (bf16[8,640]{1,0:T(8,128)(2,1)}, bf16[8,640]{1,0:T(8,128)(2,1)}, u32[]{:S(2)}, u32[]{:S(2)}) collective-permute-start(bf16[8,640]{1,0:T(8,128)(2,1)} %get-tuple-element.58), channel_id=1, source_target_pairs={{0,11},{1,12},{2,13},{3,14},{4,15},{5,0},{6,1},{7,2},{8,3},{9,4},{... | collective-permute-start | bytes 30728 | tf_op jit(solution)/shard_map/ppermute | solution.py:66
  21.3 12.7 %collective-permute-start.11 = (bf16[8,640]{1,0:T(8,128)(2,1)}, bf16[8,640]{1,0:T(8,128)(2,1)}, u32[]{:S(2)}, u32[]{:S(2)}) collective-permute-start(bf16[8,640]{1,0:T(8,128)(2,1)} %get-tuple-element.59), channel_id=1, source_target_pairs={{0,12},{1,13},{2,14},{3,15},{4,0},{5,1},{6,2},{7,3},{8,4},{9,5},{1... | collective-permute-start | bytes 30728 | tf_op jit(solution)/shard_map/ppermute | solution.py:66
  23.0 11.0 %collective-permute-start.12 = (bf16[8,640]{1,0:T(8,128)(2,1)}, bf16[8,640]{1,0:T(8,128)(2,1)}, u32[]{:S(2)}, u32[]{:S(2)}) collective-permute-start(bf16[8,640]{1,0:T(8,128)(2,1)} %get-tuple-element.60), channel_id=1, source_target_pairs={{0,13},{1,14},{2,15},{3,0},{4,1},{5,2},{6,3},{7,4},{8,5},{9,6},{10... | collective-permute-start | bytes 30728 | tf_op jit(solution)/shard_map/ppermute | solution.py:66
  23.0 11.0 %collective-permute-start.13 = (bf16[8,640]{1,0:T(8,128)(2,1)}, bf16[8,640]{1,0:T(8,128)(2,1)}, u32[]{:S(2)}, u32[]{:S(2)}) collective-permute-start(bf16[8,640]{1,0:T(8,128)(2,1)} %get-tuple-element.61), channel_id=1, source_target_pairs={{0,14},{1,15},{2,0},{3,1},{4,2},{5,3},{6,4},{7,5},{8,6},{9,7},{10,... | collective-permute-start | bytes 30728 | tf_op jit(solution)/shard_map/ppermute | solution.py:66
  25.0 9.0 %collective-permute-start.14 = (bf16[8,640]{1,0:T(8,128)(2,1)}, bf16[8,640]{1,0:T(8,128)(2,1)}, u32[]{:S(2)}, u32[]{:S(2)}) collective-permute-start(bf16[8,640]{1,0:T(8,128)(2,1)} %get-tuple-element.62), channel_id=1, source_target_pairs={{0,15},{1,0},{2,1},{3,2},{4,3},{5,4},{6,5},{7,6},{8,7},{9,8},{10,9... | collective-permute-start | bytes 30728 | tf_op jit(solution)/shard_map/ppermute | solution.py:66
  40.7 6.8 %collective-permute-start.17 = (bf16[8,896]{1,0:T(8,128)(2,1)}, bf16[8,896]{1,0:T(8,128)(2,1)}, u32[]{:S(2)}, u32[]{:S(2)}) collective-permute-start(bf16[8,896]{1,0:T(8,128)(2,1)} %get-tuple-element.71), channel_id=1, source_target_pairs={{0,2},{1,3},{2,4},{3,5},{4,6},{5,7},{6,8},{7,9},{8,10},{9,11},{10,... | collective-permute-start | bytes 43016 | tf_op jit(solution)/shard_map/ppermute | solution.py:66
  42.0 7.5 %collective-permute-start.18 = (bf16[8,896]{1,0:T(8,128)(2,1)}, bf16[8,896]{1,0:T(8,128)(2,1)}, u32[]{:S(2)}, u32[]{:S(2)}) collective-permute-start(bf16[8,896]{1,0:T(8,128)(2,1)} %get-tuple-element.72), channel_id=1, source_target_pairs={{0,3},{1,4},{2,5},{3,6},{4,7},{5,8},{6,9},{7,10},{8,11},{9,12},{10... | collective-permute-start | bytes 43016 | tf_op jit(solution)/shard_map/ppermute | solution.py:66
  43.0 8.8 %collective-permute-start.19 = (bf16[8,896]{1,0:T(8,128)(2,1)}, bf16[8,896]{1,0:T(8,128)(2,1)}, u32[]{:S(2)}, u32[]{:S(2)}) collective-permute-start(bf16[8,896]{1,0:T(8,128)(2,1)} %get-tuple-element.73), channel_id=1, source_target_pairs={{0,4},{1,5},{2,6},{3,7},{4,8},{5,9},{6,10},{7,11},{8,12},{9,13},{1... | collective-permute-start | bytes 43016 | tf_op jit(solution)/shard_map/ppermute | solution.py:66
  43.3 8.6 %collective-permute-start.20 = (bf16[8,896]{1,0:T(8,128)(2,1)}, bf16[8,896]{1,0:T(8,128)(2,1)}, u32[]{:S(2)}, u32[]{:S(2)}) collective-permute-start(bf16[8,896]{1,0:T(8,128)(2,1)} %get-tuple-element.74), channel_id=1, source_target_pairs={{0,5},{1,6},{2,7},{3,8},{4,9},{5,10},{6,11},{7,12},{8,13},{9,14},{... | collective-permute-start | bytes 43016 | tf_op jit(solution)/shard_map/ppermute | solution.py:66
  46.8 6.6 %collective-permute-start.21 = (bf16[8,896]{1,0:T(8,128)(2,1)}, bf16[8,896]{1,0:T(8,128)(2,1)}, u32[]{:S(2)}, u32[]{:S(2)}) collective-permute-start(bf16[8,896]{1,0:T(8,128)(2,1)} %get-tuple-element.75), channel_id=1, source_target_pairs={{0,6},{1,7},{2,8},{3,9},{4,10},{5,11},{6,12},{7,13},{8,14},{9,15},... | collective-permute-start | bytes 43016 | tf_op jit(solution)/shard_map/ppermute | solution.py:66
  47.5 10.1 %collective-permute-start.22 = (bf16[8,896]{1,0:T(8,128)(2,1)}, bf16[8,896]{1,0:T(8,128)(2,1)}, u32[]{:S(2)}, u32[]{:S(2)}) collective-permute-start(bf16[8,896]{1,0:T(8,128)(2,1)} %get-tuple-element.76), channel_id=1, source_target_pairs={{0,7},{1,8},{2,9},{3,10},{4,11},{5,12},{6,13},{7,14},{8,15},{9,0},... | collective-permute-start | bytes 43016 | tf_op jit(solution)/shard_map/ppermute | solution.py:66
  49.5 8.1 %collective-permute-start.23 = (bf16[8,896]{1,0:T(8,128)(2,1)}, bf16[8,896]{1,0:T(8,128)(2,1)}, u32[]{:S(2)}, u32[]{:S(2)}) collective-permute-start(bf16[8,896]{1,0:T(8,128)(2,1)} %get-tuple-element.77), channel_id=1, source_target_pairs={{0,8},{1,9},{2,10},{3,11},{4,12},{5,13},{6,14},{7,15},{8,0},{9,1},... | collective-permute-start | bytes 43016 | tf_op jit(solution)/shard_map/ppermute | solution.py:66
  51.9 8.6 %collective-permute-start.25 = (bf16[8,896]{1,0:T(8,128)(2,1)}, bf16[8,896]{1,0:T(8,128)(2,1)}, u32[]{:S(2)}, u32[]{:S(2)}) collective-permute-start(bf16[8,896]{1,0:T(8,128)(2,1)} %get-tuple-element.79), channel_id=1, source_target_pairs={{0,10},{1,11},{2,12},{3,13},{4,14},{5,15},{6,0},{7,1},{8,2},{9,3},... | collective-permute-start | bytes 43016 | tf_op jit(solution)/shard_map/ppermute | solution.py:66
  53.5 16.8 %collective-permute-start.26 = (bf16[8,896]{1,0:T(8,128)(2,1)}, bf16[8,896]{1,0:T(8,128)(2,1)}, u32[]{:S(2)}, u32[]{:S(2)}) collective-permute-start(bf16[8,896]{1,0:T(8,128)(2,1)} %get-tuple-element.80), channel_id=1, source_target_pairs={{0,11},{1,12},{2,13},{3,14},{4,15},{5,0},{6,1},{7,2},{8,3},{9,4},{... | collective-permute-start | bytes 43016 | tf_op jit(solution)/shard_map/ppermute | solution.py:66
  57.6 12.7 %collective-permute-start.27 = (bf16[8,896]{1,0:T(8,128)(2,1)}, bf16[8,896]{1,0:T(8,128)(2,1)}, u32[]{:S(2)}, u32[]{:S(2)}) collective-permute-start(bf16[8,896]{1,0:T(8,128)(2,1)} %get-tuple-element.81), channel_id=1, source_target_pairs={{0,12},{1,13},{2,14},{3,15},{4,0},{5,1},{6,2},{7,3},{8,4},{9,5},{1... | collective-permute-start | bytes 43016 | tf_op jit(solution)/shard_map/ppermute | solution.py:66
  57.6 12.7 %collective-permute-start.28 = (bf16[8,896]{1,0:T(8,128)(2,1)}, bf16[8,896]{1,0:T(8,128)(2,1)}, u32[]{:S(2)}, u32[]{:S(2)}) collective-permute-start(bf16[8,896]{1,0:T(8,128)(2,1)} %get-tuple-element.82), channel_id=1, source_target_pairs={{0,13},{1,14},{2,15},{3,0},{4,1},{5,2},{6,3},{7,4},{8,5},{9,6},{10... | collective-permute-start | bytes 43016 | tf_op jit(solution)/shard_map/ppermute | solution.py:66
  58.2 12.0 %collective-permute-start.29 = (bf16[8,896]{1,0:T(8,128)(2,1)}, bf16[8,896]{1,0:T(8,128)(2,1)}, u32[]{:S(2)}, u32[]{:S(2)}) collective-permute-start(bf16[8,896]{1,0:T(8,128)(2,1)} %get-tuple-element.83), channel_id=1, source_target_pairs={{0,14},{1,15},{2,0},{3,1},{4,2},{5,3},{6,4},{7,5},{8,6},{9,7},{10,... | collective-permute-start | bytes 43016 | tf_op jit(solution)/shard_map/ppermute | solution.py:66
  60.5 9.8 %collective-permute-start.30 = (bf16[8,896]{1,0:T(8,128)(2,1)}, bf16[8,896]{1,0:T(8,128)(2,1)}, u32[]{:S(2)}, u32[]{:S(2)}) collective-permute-start(bf16[8,896]{1,0:T(8,128)(2,1)} %get-tuple-element.84), channel_id=1, source_target_pairs={{0,15},{1,0},{2,1},{3,2},{4,3},{5,4},{6,5},{7,6},{8,7},{9,8},{10,9... | collective-permute-start | bytes 43016 | tf_op jit(solution)/shard_map/ppermute | solution.py:66
  (7 other events, 41.2 us)

commit v5 on v3

--- a/solution.py
+++ b/solution.py
@@ -23,6 +23,7 @@
 NONE = -1e30
 PAIRS = 6
 MATCH = 32768.0
+AHEAD = 2
 EARLY = 2
 VMEM_LIMIT = 64 * 1024 * 1024
 
@@ -58,8 +59,8 @@
     return found
 
 
-def fetches(pairs, sems):
-    copies = [pltpu.make_async_copy(src, dst, sems.at[n]) for n, (src, dst) in enumerate(pairs)]
+def fetches(pairs, sems, first=0):
+    copies = [pltpu.make_async_copy(src, dst, sems.at[first + n]) for n, (src, dst) in enumerate(pairs)]
     for copy in copies:
         copy.start()
     return copies
@@ -90,7 +91,18 @@
         out_ref[d * SUB : (d + 2) * SUB, HALF:] = jnp.concatenate([end, end], axis=0).astype(bf16)
 
 
-def head_factors(first, dt_ref, rate_ref, skip_ref, len_ref, levels, w_in, w_out, w_skip, w_tail):
+def sign_tables(signs, tail):
+    length = signs.shape[-1]
+    j = iota((length, length), 0)
+    i = iota((length, length), 1)
+    for l, n in enumerate(LEVELS):
+        middle = (i // (2 * n)) * (2 * n) + (n - 1)
+        signs[l] = (jnp.where(j <= i, 1.0, 0.0) - jnp.where(j <= middle, 1.0, 0.0)).astype(bf16)
+    if tail:
+        signs[len(LEVELS)] = jnp.where(j > i, 1.0, 0.0).astype(bf16)
+
+
+def head_factors(first, dt_ref, rate_ref, skip_ref, len_ref, signs, w_in, w_out, w_skip, w_tail):
     group, prompts, length = dt_ref.shape
     row = iota((prompts, length), 0)
     lens = jnp.zeros((prompts, length), jnp.int32)
@@ -99,23 +111,16 @@
     valid = iota((prompts, length), 1) < lens
     moved = [jnp.where(valid, dt_ref[h].astype(f32), 0.0) for h in range(group)]
     every = jnp.concatenate(moved, axis=0).astype(bf16)
-    j = iota((length, length), 0)
-    i = iota((length, length), 1)
     rates = [rate_ref[first + h] * LOG2E for h in range(group)]
     if w_tail is not None:
-        after = jnp.where(j > i, 1.0, 0.0).astype(bf16)
-        total = jnp.dot(every, after, preferred_element_type=f32)
+        total = jnp.dot(every, signs[len(LEVELS)], preferred_element_type=f32)
         for h in range(group):
             part = total[h * prompts : (h + 1) * prompts]
             w_tail[:, h, :] = jnp.exp2(-(rates[h] * part)) * moved[h]
-    if not levels:
-        return
     for h in range(group):
         w_skip[:, h, :] = jnp.where(valid, skip_ref[first + h], 0.0)
-    for l, n in enumerate(levels):
-        middle = (i // (2 * n)) * (2 * n) + (n - 1)
-        signs = (jnp.where(j <= i, 1.0, 0.0) - jnp.where(j <= middle, 1.0, 0.0)).astype(bf16)
-        total = jnp.dot(every, signs, preferred_element_type=f32)
+    for l, n in enumerate(LEVELS):
+        total = jnp.dot(every, signs[l], preferred_element_type=f32)
         for h in range(group):
             gap = rates[h] * total[h * prompts : (h + 1) * prompts]
             if n == LEVELS[-1]:
@@ -174,8 +179,8 @@
     c_any,
     state_any,
     mark_any,
-    hot_ref,
-    req_ref,
+    hot_any,
+    req_any,
     out_any,
     x_held,
     b_held,
@@ -184,10 +189,13 @@
     w_in,
     w_out,
     w_skip,
+    masks,
+    signs,
     w_tail,
-    masks,
     state_held,
     mark_held,
+    hot_held,
+    req_held,
     rate_ref,
     skip_ref,
     len_ref,
@@ -200,7 +208,6 @@
     c_sem,
     out_sem,
     state_sem,
-    mark_sem,
     sems,
 ):
     group, prompts, length = dt_ref.shape
@@ -235,17 +242,35 @@
     def state_copy(r):
         return pltpu.make_async_copy(state_held.at[r], state_any.at[r], state_sem.at[r])
 
-    for r in range(prompts):
+    def ask(r):
         x_copy(r).start()
         b_copy(r).start()
+
+    for r in range(AHEAD):
+        ask(r)
+    sign_tables(signs, True)
+    level_masks(masks)
+    for copy in smalls:
+        copy.wait()
+    head_factors(first, dt_ref, rate_ref, skip_ref, len_ref, signs, w_in, w_out, w_skip, w_tail)
+
+    def one(r, _):
+        @pl.when(r + AHEAD < prompts)
+        def _():
+            ask(r + AHEAD)
+
+        x_copy(r).wait()
+        b_copy(r).wait()
+        width = x_held.shape[1]
+        inputs = x_held[r].astype(f32).reshape(group, HP, length)
+        scaled = (inputs * w_tail[r][:, None, :]).astype(bf16).reshape(width, length)
+        state_held[r] = jnp.dot(scaled, b_held[r], preferred_element_type=f32).astype(bf16)
+        state_copy(r).start()
+        return 0
+
+    lax.fori_loop(0, prompts, one, 0, unroll=2)
     for r in range(EARLY):
         c_copy(r).start()
-    for copy in smalls:
-        copy.wait()
-
-    head_factors(
-        first, dt_ref, rate_ref, skip_ref, len_ref, LEVELS if EARLY else (), w_in, w_out, w_skip, w_tail
-    )
 
     spread = table_ref.shape[1] // owner_ref.shape[1]
     per_head = table_ref.shape[1] // KVH
@@ -259,8 +284,6 @@
                 inside = (lane == r) & (offset < len_ref[r] - begin)
                 block = jnp.where(inside, MATCH, 0.0).astype(bf16)
                 mark_held[n, pl.ds(pl.multiple_of(row * PAGE, PAGE), PAGE), :] = block
-    mark_copy = pltpu.make_async_copy(mark_held, mark_any, mark_sem)
-    mark_copy.start()
 
     owners = owner_ref.shape[1]
     rows_dev = slot_ref.shape[0] // owners
@@ -274,39 +297,26 @@
                 target = owner_ref[slot_ref[(2 * s + n) * rows_dev + i], 2 * s + n]
                 block = jnp.where((inner // SUB == n) & (inner % rows_dev == i), target, block)
         place = pl.ds(pl.multiple_of(s * 2 * SUB, 2 * SUB), 2 * SUB)
-        req_ref[place, :] = block
-        hot_ref[place, :] = jnp.where(lanes == block, 1.0, 0.0).astype(bf16)
+        req_held[place, :] = block
+        hot_held[place, :] = jnp.where(lanes == block, 1.0, 0.0).astype(bf16)
         return 0
 
     lax.fori_loop(0, owners // 2, fill, 0)
-
-    def one(r, _):
-        x_copy(r).wait()
-        b_copy(r).wait()
-        width = x_held.shape[1]
-        inputs = x_held[r].astype(f32).reshape(group, HP, length)
-        scaled = (inputs * w_tail[r][:, None, :]).astype(bf16).reshape(width, length)
-        state_held[r] = jnp.dot(scaled, b_held[r], preferred_element_type=f32).astype(bf16)
-        state_copy(r).start()
+    marks = fetches([(mark_held, mark_any), (hot_held, hot_any), (req_held, req_any)], sems)
+
+    def early(r, _):
+        c_copy(r).wait()
+        prompt_result(r, x_held, b_held, c_held, w_in, w_out, w_skip, masks, out_held)
+        out_copy(r).start()
         return 0
 
-    lax.fori_loop(0, prompts, one, 0, unroll=2)
-
-    if EARLY:
-        level_masks(masks)
-
-        def early(r, _):
-            c_copy(r).wait()
-            prompt_result(r, x_held, b_held, c_held, w_in, w_out, w_skip, masks, out_held)
-            out_copy(r).start()
-            return 0
-
-        lax.fori_loop(0, EARLY, early, 0, unroll=2)
-        for r in range(EARLY):
-            out_copy(r).wait()
+    lax.fori_loop(0, EARLY, early, 0, unroll=2)
+    for copy in marks:
+        copy.wait()
     for r in range(prompts):
         state_copy(r).wait()
-    mark_copy.wait()
+    for r in range(EARLY):
+        out_copy(r).wait()
 
 
 def serve_kernel(
@@ -341,21 +351,27 @@
             (other_any.at[:, pl.ds(0, HD)], key_ref.at[other, pl.ds(0, HD)]),
             (mark_any.at[0], key_ref.at[mine, pl.ds(HD, LANES)]),
             (mark_any.at[1], key_ref.at[other, pl.ds(HD, LANES)]),
-            (pages_any.at[:, pl.ds(HD, HD)], value_ref.at[mine]),
-            (other_any.at[:, pl.ds(HD, HD)], value_ref.at[other]),
-            (req_any, req_ref),
         ],
         sems,
     )
-    states = fetches([(state_any.at[r], state_ref.at[r]) for r in range(prompts)], state_sem)
     copies[0].wait()
     copies[1].wait()
     heads = HALF // HD
     for g in range(heads):
         query_ref[g * rows : (g + 1) * rows, :HD] = recv_ref[:, g * HD : (g + 1) * HD]
         query_ref[g * rows : (g + 1) * rows, HD:] = hot_ref[...]
-    for copy in copies[2:6]:
+    for copy in copies[2:]:
         copy.wait()
+    copies = fetches(
+        [
+            (pages_any.at[:, pl.ds(HD, HD)], value_ref.at[mine]),
+            (other_any.at[:, pl.ds(HD, HD)], value_ref.at[other]),
+            (req_any, req_ref),
+        ],
+        sems,
+        len(copies),
+    )
+    states = fetches([(state_any.at[r], state_ref.at[r]) for r in range(prompts)], state_sem)
     keys = key_ref.shape[0]
     chunk = min(keys, 2 * NS)
     widest = jnp.full((heads * rows, LANES), NONE, f32)
@@ -365,7 +381,7 @@
         for b in range(0, chunk, LANES):
             widest = jnp.maximum(widest, scores[:, b : b + LANES])
     highest = jnp.max(widest, axis=1, keepdims=True)
-    for copy in copies[6:]:
+    for copy in copies:
         copy.wait()
     total = jnp.zeros((heads * rows, LANES), f32)
     value = jnp.zeros((heads * rows, HD), f32)
@@ -433,10 +449,10 @@
     after_any,
     early_any,
     out_any,
-    own_ref,
-    ownsum_ref,
-    fade_ref,
-    local_ref,
+    own_any,
+    ownsum_any,
+    fade_any,
+    local_any,
     x_held,
     b_held,
     c_held,
@@ -445,6 +461,11 @@
     w_out,
     w_skip,
     masks,
+    signs,
+    own_ref,
+    ownsum_ref,
+    fade_ref,
+    local_ref,
     fresh_held,
     c_rows,
     x_rows,
@@ -500,17 +521,29 @@
     def out_copy(r):
         return pltpu.make_async_copy(out_held.at[r], out_any.at[r], out_sem.at[r])
 
-    for r in range(EARLY, prompts):
+    def ask(r):
         x_copy(r).start()
         b_copy(r).start()
         c_copy(r).start()
+
+    for r in range(EARLY, min(EARLY + AHEAD, prompts)):
+        ask(r)
+    sign_tables(signs, False)
+    level_masks(masks)
     for copy in smalls:
         copy.wait()
-
-    head_factors(first, dt_ref, rate_ref, skip_ref, len_ref, LEVELS, w_in, w_out, w_skip, None)
-    level_masks(masks)
+    head_factors(first, dt_ref, rate_ref, skip_ref, len_ref, signs, w_in, w_out, w_skip, None)
+    own_attention(send_ref, fresh_ref, fresh_held, own_ref, ownsum_ref)
+    own_mixer(rates_ref, skips_ref, sx_ref, sb_ref, sc_ref, sdt_ref, c_rows, x_rows, fade_ref, local_ref)
+    outs = fetches(
+        [(own_ref, own_any), (ownsum_ref, ownsum_any), (fade_ref, fade_any), (local_ref, local_any)], sems
+    )
 
     def one(r, _):
+        @pl.when(r + AHEAD < prompts)
+        def _():
+            ask(r + AHEAD)
+
         x_copy(r).wait()
         b_copy(r).wait()
         c_copy(r).wait()
@@ -519,8 +552,8 @@
         return 0
 
     lax.fori_loop(EARLY, prompts, one, 0, unroll=2)
-    own_attention(send_ref, fresh_ref, fresh_held, own_ref, ownsum_ref)
-    own_mixer(rates_ref, skips_ref, sx_ref, sb_ref, sc_ref, sdt_ref, c_rows, x_rows, fade_ref, local_ref)
+    for copy in outs:
+        copy.wait()
     for r in range(EARLY, prompts):
         out_copy(r).wait()
 
@@ -608,8 +641,8 @@
     ownsum_any,
     fade_any,
     local_any,
-    mixer_ref,
-    attention_ref,
+    mixer_any,
+    attention_any,
     back_ref,
     own_ref,
     ownsum_ref,
@@ -617,18 +650,12 @@
     local_ref,
     mixed,
     attended,
+    mixer_ref,
+    attention_ref,
     sems,
 ):
-    copies = fetches(
-        [
-            (back_any, back_ref),
-            (own_any, own_ref),
-            (ownsum_any, ownsum_ref),
-            (fade_any, fade_ref),
-            (local_any, local_ref),
-        ],
-        sems,
-    )
+    copies = fetches([(back_any, back_ref), (fade_any, fade_ref), (local_any, local_ref)], sems)
+    rest = fetches([(own_any, own_ref), (ownsum_any, ownsum_ref)], sems, len(copies))
     for copy in copies:
         copy.wait()
     owners = back_ref.shape[0] // SUB
@@ -645,6 +672,9 @@
         mixed[:, columns] = found * fade_ref[:, columns] + local_ref[:, columns]
     for k in range(steps):
         mixer_ref[k] = mixed[k * rows : (k + 1) * rows, :].astype(bf16)
+    outs = fetches([(mixer_ref, mixer_any)], sems)
+    for copy in rest:
+        copy.wait()
     lane = iota((2, SUB, LANES), 2)
     mine = (lane // 16 == iota((2, SUB, LANES), 1)) & (lane % 16 < 12)
     for v in range(KVH):
@@ -675,6 +705,9 @@
             attended[:, start + HALF : start + HALF + HD] = value[SUB:]
     for k in range(steps):
         attention_ref[k] = attended[k * rows : (k + 1) * rows, :].astype(bf16)
+    outs += fetches([(attention_ref, attention_any)], sems, 1)
+    for copy in outs:
+        copy.wait()
 
 
 def call(kernel, out_shape, in_spaces, out_spaces, scratch, cost, aliases=None):
@@ -761,7 +794,7 @@
         vmem((levels, prompts, group, length), f32),
         vmem((prompts, group, length), f32),
     ]
-    masks = vmem((levels, length, length), bf16)
+    tables = [vmem((levels, length, length), bf16), vmem((levels + 1, length, length), bf16)]
     work = 2 * width * length * NS
     states, marks, hot, requests, early_out = call(
         state_kernel,
@@ -773,12 +806,13 @@
             shape(prompt_x.shape, bf16),
         ),
         [hbm] * 10,
-        (hbm, hbm, vmem, vmem, hbm),
+        (hbm,) * 5,
         block
-        + [vmem((prompts, group, length), f32), masks]
-        + [vmem((prompts, width, NS), bf16), vmem((2, keys, LANES), bf16)]
+        + tables
+        + [vmem((prompts, group, length), f32), vmem((prompts, width, NS), bf16)]
+        + [vmem((2, keys, LANES), bf16), vmem((all_rows, LANES), bf16), vmem((all_rows, LANES), jnp.int32)]
         + [like(smem, one) for one in (decay_rate, skip_gain, lengths, owner_list, page_table, row_slot)]
-        + [like(vmem, prompt_dt), sem, sem, sem, sem, sem, pltpu.SemaphoreType.DMA, sems(7)],
+        + [like(vmem, prompt_dt), sem, sem, sem, sem, sem, sems(7)],
         (work * (prompts + 5 * EARLY), 6 << 20),
     )(
         decay_rate,
@@ -835,10 +869,14 @@
             shape((SUB, channels), f32),
         ),
         [hbm] * 17,
-        (hbm, vmem, vmem, vmem, vmem),
+        (hbm,) * 5,
         block
+        + tables
         + [
-            masks,
+            vmem((KVH, count, HD), f32),
+            vmem((KVH, count, HD), f32),
+            vmem((SUB, channels), f32),
+            vmem((SUB, channels), f32),
             vmem((SUB, fresh_cache.shape[2]), f32),
             vmem((SUB, step_c.shape[2]), f32),
             vmem((steps, SUB, channels), f32),
@@ -886,9 +924,10 @@
         functools.partial(merge_kernel, width),
         (shape(step_x.shape, bf16), shape(queries.shape, bf16)),
         [hbm] * 5,
-        (vmem, vmem),
+        (hbm, hbm),
         [like(vmem, one) for one in (returned, own, own_sum, fade, local)]
-        + [vmem((SUB, channels), f32), vmem((SUB, queries.shape[2]), f32), sems(5)],
+        + [vmem((SUB, channels), f32), vmem((SUB, queries.shape[2]), f32)]
+        + [like(vmem, step_x), like(vmem, queries), sems(5)],
         (0, 2 << 20),
     )(returned, own, own_sum, fade, local)
     return (prompt_out, jnp.swapaxes(mixer_out, 0, 1), jnp.swapaxes(attention_out, 0, 1))

time: 41.5 us -> 43.1 us (1.039)
  starting transfers between devices: 12.3 us -> 13.4 us
    all_to_all x1, waiting for transfers between devices: 0.9 us -> 2.38 us  [on_device(): lax.all_to_all(back, 'heads', split_axis=0, concat_axis=0, tiled=True)]
    pallas_call x1, Pallas kernels: 8.67 us -> 7.19 us  [on_device(): call(prompt_kernel, (shape(prompt_x.shape, bf16), shape((KVH, count, HD),...]
    all_to_all x1, starting transfers between devices: 4.69 us -> 5.76 us  [on_device(): lax.all_to_all(back, 'heads', split_axis=0, concat_axis=0, tiled=True)]
    all_to_all x1, waiting for transfers between devices: 1.33 us -> 0.27 us  [on_device(): lax.all_to_all(send, 'heads', split_axis=0, concat_axis=0, tiled=True)]
    pallas_call x1, Pallas kernels: 7.18 us -> 8.24 us  [on_device(): call(state_kernel, (shape((prompts, width, NS), bf16), shape((2, keys, LA...]
  transfers between devices with their start and end apart: 3 -> 3, of which waited for: 2 -> 2; matrix products, arithmetic and copies ran while one was open for 0% -> 0% of each run, Pallas kernels for 43% -> 40%
where the time goes in v5:
time: 43.1 us; the launch traced here: 42.5 us
  Pallas kernels  25.8 us (60%)
  starting transfers between devices  13.4 us (31%)
  waiting for transfers between devices  2.65 us (6%)
  between operations  0.68 us (2%)
    pallas_call x1, Pallas kernels, on_device(): call(state_kernel, (shape((prompts, width, NS), bf16), shape((2, keys, LA...  8.24 us
    pallas_call x1, Pallas kernels, on_device(): call(prompt_kernel, (shape(prompt_x.shape, bf16), shape((KVH, count, HD),...  7.19 us
    all_to_all x1, starting transfers between devices, on_device(): lax.all_to_all(send, 'heads', split_axis=0, concat_axis=0, tiled=True)  7.1 us
    pallas_call x1, Pallas kernels, on_device(): call(serve_kernel, shape((all_rows, HALF + max(LANES, width) - LANES), bf...  6.45 us
    all_to_all x1, starting transfers between devices, on_device(): lax.all_to_all(back, 'heads', split_axis=0, concat_axis=0, tiled=True)  5.76 us
    all_to_all x1, waiting for transfers between devices, on_device(): lax.all_to_all(back, 'heads', split_axis=0, concat_axis=0, tiled=True)  2.38 us
    pallas_call x1, Pallas kernels, on_device(): call(functools.partial(merge_kernel, width), (shape(step_x.shape, bf16),...  2.26 us
    pallas_call x1, Pallas kernels, on_device(): call(functools.partial(pack_kernel, group, ways), shape((all_rows, HALF +...  1.68 us
  transfers between devices with their start and end apart: 3, of which 2 were waited for; matrix products, arithmetic and copies ran while one was open for 0% of the time, Pallas kernels for 40%

profile of v5, /device:TPU:0, one launch (start us, length us, event | category | flops | bytes accessed | tf_op | source)
XLA Modules:
  0.0 42.5 jit_solution(487170647402676430)
XLA Ops:
  0.6 0.5 %collective-permute-start = (bf16[64,16,256]{2,1,0:T(8,128)(2,1)}, bf16[64,16,256]{2,1,0:T(8,128)(2,1)}, u32[]{:S(2)}, u32[]{:S(2)}) collective-permute-start(bf16[64,16,256]{2,1,0:T(8,128)(2,1)} %param.26), channel_id=1, source_target_pairs={{0,1},{1,0},{2,3},{3,2},{4,5},{5,4},{6,7},{7,6},{8,9},{9,8},{10,11... | collective-permute-start | bytes 1572872 | tf_op jit(solution)/shard_map/ppermute | solution.py:770
  1.1 1.7 %shard_map.184.send_any = bf16[128,640]{1,0:T(8,128)(2,1)} custom-call(bf16[3,2,8192]{2,1,0:T(2,128)(2,1)} %bitcast.21, bf16[3,2,1024]{2,1,0:T(2,128)(2,1)} %bitcast.22), custom_call_target="tpu_custom_call" | custom-call | bytes 524288 | tf_op jit(solution)/shard_map/pallas_call | solution.py:771
  2.8 7.1 %all-to-all-start = ((bf16[16,8,640]{2,1,0:T(8,128)(2,1)}), bf16[16,8,640]{2,1,0:T(8,128)(2,1)}, u32[]{:S(2)}, u32[]{:S(2)}) async-start(bf16[16,8,640]{2,1,0:T(8,128)(2,1)} %bitcast.18), calls=%async_computation | async-start | bytes 327680 | tf_op jit(solution)/shard_map/all_to_all | solution.py:786
  9.9 8.2 %shard_map.185 = (bf16[8,512,256]{2,1,0:T(8,128)(2,1)}, bf16[2,1024,128]{2,1,0:T(8,128)(2,1)}, bf16[128,128]{1,0:T(8,128)(2,1)}, s32[128,128]{1,0:T(8,128)}, bf16[8,512,256]{2,1,0:T(8,128)(2,1)}) custom-call(f32[128]{0:T(128)} %rate_any.3, f32[128]{0:T(128)} %skip_any.3, s32[8]{0:T(128)} %len_any.3, s32[2,16]{1,0:T(2,128)} %bitcast.29, s32[8,128]{1,0:T(8,128)} %table_any.1, ...), custom_call_target="tpu_custom_call" | custom-call | flops 1207959552 | bytes 6291456 | tf_op jit(solution)/shard_map/pallas_call | solution.py:799
  18.2 0.3 all-to-all-done
  18.5 0.0 collective-permute-done
  18.5 6.5 %shard_map.186.after_any = bf16[128,896]{1,0:T(8,128)(2,1)} custom-call(bf16[128,640]{1,0:T(8,128)(2,1)} %bitcast.9.recv_any, bf16[1024,256]{1,0:T(8,128)(2,1)} %bitcast.19, bf16[1024,256]{1,0:T(8,128)(2,1)} %bitcast.11.other_any, bf16[2,1024,128]{2,1,0:T(8,128)(2,1)} %get-tuple-element.15.mark_any, bf16[128,128]{1,0:T(8,128)(2,1)} %get-tuple-element.16.hot_any, ...), custom_call_target="tpu_custom_call" | custom-call | flops 134217728 | bytes 4194304 | tf_op jit(solution)/shard_map/pallas_call | solution.py:830
  24.9 5.8 %all-to-all-start.1 = ((bf16[16,8,896]{2,1,0:T(8,128)(2,1)}), bf16[16,8,896]{2,1,0:T(8,128)(2,1)}, u32[]{:S(2)}, u32[]{:S(2)}) async-start(bf16[16,8,896]{2,1,0:T(8,128)(2,1)} %bitcast.17), calls=%async_computation.1 | async-start | bytes 458752 | tf_op jit(solution)/shard_map/all_to_all | solution.py:857
  30.7 7.2 %shard_map.187 = (bf16[8,512,256]{2,1,0:T(8,128)(2,1)}, f32[8,64,128]{2,1,0:T(8,128)}, f32[8,64,128]{2,1,0:T(8,128)}, f32[8,8192]{1,0:T(8,128)}, f32[8,8192]{1,0:T(8,128)}) custom-call(f32[128]{0:T(128)} %rate_any.3, f32[128]{0:T(128)} %skip_any.3, s32[8]{0:T(128)} %len_any.3, bf16[8,8,256]{2,1,0:T(8,128)(2,1)} %dt_any.3, ...), custom_call_target="tpu_custom_call", output_to_operand_aliasing={{0}: (16, {})} | custom-call | flops 2013265920 | bytes 8388608 | tf_op jit(solution)/shard_map/pallas_call | solution.py:862
  37.9 2.4 %all-to-all-done.1 = bf16[16,8,896]{2,1,0:T(8,128)(2,1)} async-done(((bf16[16,8,896]{2,1,0:T(8,128)(2,1)}), bf16[16,8,896]{2,1,0:T(8,128)(2,1)}, u32[]{:S(2)}, u32[]{:S(2)}) %all-to-all-start.1) | async-done | bytes 229408 | tf_op jit(solution)/shard_map/all_to_all | solution.py:857
  40.3 2.3 %shard_map.188 = (bf16[3,2,8192]{2,1,0:T(2,128)(2,1)}, bf16[3,2,8192]{2,1,0:T(2,128)(2,1)}) custom-call(bf16[128,896]{1,0:T(8,128)(2,1)} %bitcast.14.back_any, f32[8,64,128]{2,1,0:T(8,128)} %get-tuple-element.21.own_any, f32[8,64,128]{2,1,0:T(8,128)} %get-tuple-element.22.ownsum_any, f32[8,8192]{1,0:T(8,128)} %get-tuple-element.23.fade_any, ...), custom_call_target="tpu_custom_call" | custom-call | bytes 2097152 | tf_op jit(solution)/shard_map/pallas_call | solution.py:923
Async XLA Ops:
  0.6 17.8 %collective-permute-start = (bf16[64,16,256]{2,1,0:T(8,128)(2,1)}, bf16[64,16,256]{2,1,0:T(8,128)(2,1)}, u32[]{:S(2)}, u32[]{:S(2)}) collective-permute-start(bf16[64,16,256]{2,1,0:T(8,128)(2,1)} %param.26), channel_id=1, source_target_pairs={{0,1},{1,0},{2,3},{3,2},{4,5},{5,4},{6,7},{7,6},{8,9},{9,8},{10,11... | collective-permute-start | bytes 1572872 | tf_op jit(solution)/shard_map/ppermute | solution.py:770
  2.8 15.6 %all-to-all-start = ((bf16[16,8,640]{2,1,0:T(8,128)(2,1)}), bf16[16,8,640]{2,1,0:T(8,128)(2,1)}, u32[]{:S(2)}, u32[]{:S(2)}) async-start(bf16[16,8,640]{2,1,0:T(8,128)(2,1)} %bitcast.18), calls=%async_computation | async-start | bytes 327680 | tf_op jit(solution)/shard_map/all_to_all | solution.py:786
  24.9 15.3 %all-to-all-start.1 = ((bf16[16,8,896]{2,1,0:T(8,128)(2,1)}), bf16[16,8,896]{2,1,0:T(8,128)(2,1)}, u32[]{:S(2)}, u32[]{:S(2)}) async-start(bf16[16,8,896]{2,1,0:T(8,128)(2,1)} %bitcast.17), calls=%async_computation.1 | async-start | bytes 458752 | tf_op jit(solution)/shard_map/all_to_all | solution.py:857

commit v6 on v5

--- a/solution.py
+++ b/solution.py
@@ -66,29 +66,41 @@
     return copies
 
 
-def pack_kernel(group, ways, q_any, c_any, out_ref, q_ref, c_ref, q_held, c_held, rest, sems):
-    owners = out_ref.shape[0] // SUB
-    for copy in fetches([(q_any, q_ref), (c_any, c_ref)], sems):
-        copy.wait()
-    stack_rows(q_ref, q_held)
-    stack_rows(c_ref, c_held)
-    span = 2 * HALF
+def pack_kernel(
+    group, ways, q_any, q_other, c_any, c_other, out_any, out_held, q_ref, c_ref, q_held, c_held, rest, sems
+):
+    chips = out_held.shape[0] // (2 * SUB)
+    core = lax.rem(lax.axis_index("heads"), 2)
+    copies = fetches(
+        [(c_any, c_ref.at[0]), (c_other, c_ref.at[1]), (q_any, q_ref.at[0]), (q_other, q_ref.at[1])], sems
+    )
     slots = spare(HALF // LANES + 1, 0)
     rest[...] = jnp.zeros_like(rest)
-    for e in range(c_ref.shape[2] // NS):
-        rest[e, :PAIRS, HALF:] = c_held[:PAIRS, e * NS : e * NS + LANES]
-        for pair, (row, b) in enumerate(slots):
-            rest[e, row : row + 1, b * LANES : (b + 1) * LANES] = c_held[
-                pair : pair + 1, e * NS + LANES : (e + 1) * NS
-            ]
+    for n in range(2):
+        copies[n].wait()
+        stack_rows(c_ref.at[n], c_held.at[n])
+        for e in range(c_ref.shape[3] // NS):
+            rest[n, e, :PAIRS, HALF:] = c_held[n, :PAIRS, e * NS : e * NS + LANES]
+            for pair, (row, b) in enumerate(slots):
+                rest[n, e, row : row + 1, b * LANES : (b + 1) * LANES] = c_held[
+                    n, pair : pair + 1, e * NS + LANES : (e + 1) * NS
+                ]
     real = iota((SUB, HALF), 0) < PAIRS
-    for d in range(0, owners, 2):
-        v, e = d // ways, (d * group) // HPG
-        low = jnp.where(real, q_held[:, v * span : v * span + HALF], rest[e, :, :HALF])
-        high = jnp.where(real, q_held[:, v * span + HALF : (v + 1) * span], rest[e, :, :HALF])
-        out_ref[d * SUB : (d + 2) * SUB, :HALF] = jnp.concatenate([low, high], axis=0).astype(bf16)
-        end = rest[e, :, HALF:]
-        out_ref[d * SUB : (d + 2) * SUB, HALF:] = jnp.concatenate([end, end], axis=0).astype(bf16)
+    for n in range(2):
+        copies[2 + n].wait()
+        stack_rows(q_ref.at[n], q_held.at[n])
+    for chip in range(chips):
+        v, e = 2 * chip // ways, (2 * chip * group) // HPG
+        begin = pl.multiple_of(v * 2 * HALF + core * HALF, HALF)
+        blocks = [jnp.where(real, q_held[n, :, pl.ds(begin, HALF)], rest[n, e, :, :HALF]) for n in range(2)]
+        ends = [rest[n, e, :, HALF:] for n in range(2)]
+        place = slice(chip * 2 * SUB, (chip + 1) * 2 * SUB)
+        for columns, (mine, other) in ((slice(0, HALF), blocks), (slice(HALF, HALF + LANES), ends)):
+            low = jnp.where(core == 0, mine, other)
+            high = jnp.where(core == 0, other, mine)
+            out_held[place, columns] = jnp.concatenate([low, high], axis=0).astype(bf16)
+    for copy in fetches([(out_held, out_any)], sems):
+        copy.wait()
 
 
 def sign_tables(signs, tail):
@@ -246,7 +258,7 @@
         x_copy(r).start()
         b_copy(r).start()
 
-    for r in range(AHEAD):
+    for r in range(prompts):
         ask(r)
     sign_tables(signs, True)
     level_masks(masks)
@@ -255,10 +267,6 @@
     head_factors(first, dt_ref, rate_ref, skip_ref, len_ref, signs, w_in, w_out, w_skip, w_tail)
 
     def one(r, _):
-        @pl.when(r + AHEAD < prompts)
-        def _():
-            ask(r + AHEAD)
-
         x_copy(r).wait()
         b_copy(r).wait()
         width = x_held.shape[1]
@@ -351,27 +359,21 @@
             (other_any.at[:, pl.ds(0, HD)], key_ref.at[other, pl.ds(0, HD)]),
             (mark_any.at[0], key_ref.at[mine, pl.ds(HD, LANES)]),
             (mark_any.at[1], key_ref.at[other, pl.ds(HD, LANES)]),
+            (pages_any.at[:, pl.ds(HD, HD)], value_ref.at[mine]),
+            (other_any.at[:, pl.ds(HD, HD)], value_ref.at[other]),
+            (req_any, req_ref),
         ],
         sems,
     )
+    states = fetches([(state_any.at[r], state_ref.at[r]) for r in range(prompts)], state_sem)
     copies[0].wait()
     copies[1].wait()
     heads = HALF // HD
     for g in range(heads):
         query_ref[g * rows : (g + 1) * rows, :HD] = recv_ref[:, g * HD : (g + 1) * HD]
         query_ref[g * rows : (g + 1) * rows, HD:] = hot_ref[...]
-    for copy in copies[2:]:
+    for copy in copies[2:6]:
         copy.wait()
-    copies = fetches(
-        [
-            (pages_any.at[:, pl.ds(HD, HD)], value_ref.at[mine]),
-            (other_any.at[:, pl.ds(HD, HD)], value_ref.at[other]),
-            (req_any, req_ref),
-        ],
-        sems,
-        len(copies),
-    )
-    states = fetches([(state_any.at[r], state_ref.at[r]) for r in range(prompts)], state_sem)
     keys = key_ref.shape[0]
     chunk = min(keys, 2 * NS)
     widest = jnp.full((heads * rows, LANES), NONE, f32)
@@ -381,7 +383,7 @@
         for b in range(0, chunk, LANES):
             widest = jnp.maximum(widest, scores[:, b : b + LANES])
     highest = jnp.max(widest, axis=1, keepdims=True)
-    for copy in copies:
+    for copy in copies[6:]:
         copy.wait()
     total = jnp.zeros((heads * rows, LANES), f32)
     value = jnp.zeros((heads * rows, HD), f32)
@@ -437,7 +439,7 @@
     dt_any,
     rates_any,
     skips_any,
-    send_any,
+    q_any,
     fresh_any,
     sx_any,
     sb_any,
@@ -467,6 +469,7 @@
     fade_ref,
     local_ref,
     fresh_held,
+    q_held,
     c_rows,
     x_rows,
     rate_ref,
@@ -475,7 +478,7 @@
     dt_ref,
     rates_ref,
     skips_ref,
-    send_ref,
+    q_ref,
     fresh_ref,
     sx_ref,
     sb_ref,
@@ -496,7 +499,7 @@
             (len_any, len_ref),
             (rates_any, rates_ref),
             (skips_any, skips_ref),
-            (send_any, send_ref),
+            (q_any, q_ref),
             (fresh_any, fresh_ref),
             (sx_any, sx_ref),
             (sb_any, sb_ref),
@@ -533,7 +536,7 @@
     for copy in smalls:
         copy.wait()
     head_factors(first, dt_ref, rate_ref, skip_ref, len_ref, signs, w_in, w_out, w_skip, None)
-    own_attention(send_ref, fresh_ref, fresh_held, own_ref, ownsum_ref)
+    own_attention(q_ref, fresh_ref, q_held, fresh_held, own_ref, ownsum_ref)
     own_mixer(rates_ref, skips_ref, sx_ref, sb_ref, sc_ref, sdt_ref, c_rows, x_rows, fade_ref, local_ref)
     outs = fetches(
         [(own_ref, own_any), (ownsum_ref, ownsum_any), (fade_ref, fade_any), (local_ref, local_any)], sems
@@ -558,9 +561,9 @@
         out_copy(r).wait()
 
 
-def own_attention(send_ref, fresh_ref, fresh_held, own_ref, ownsum_ref):
+def own_attention(q_ref, fresh_ref, q_held, fresh_held, own_ref, ownsum_ref):
     steps, rows = fresh_ref.shape[0], fresh_ref.shape[1]
-    ways = send_ref.shape[0] // SUB // KVH
+    stack_rows(q_ref, q_held)
     stack_rows(fresh_ref, fresh_held)
     count = HALF // HD * 2 * SUB
     pair = iota((count, SUB), 0) % SUB
@@ -568,8 +571,8 @@
     seen = (key % rows == pair % rows) & (key <= pair) & (key < rows * steps)
     seen = seen | ((pair >= rows * steps) & (key == 0))
     for v in range(KVH):
-        block = send_ref[v * ways * SUB : (v * ways + 2) * SUB]
-        query = jnp.concatenate([block[:, g * HD : (g + 1) * HD] for g in range(HALF // HD)], axis=0)
+        starts = [v * 2 * HALF + half + g for g in range(0, HALF, HD) for half in (0, HALF)]
+        query = jnp.concatenate([q_held[:, at : at + HD] for at in starts], axis=0).astype(bf16)
         keys = fresh_held[:, v * HD : (v + 1) * HD].astype(bf16)
         values = fresh_held[:, (KVH + v) * HD : (KVH + v + 1) * HD].astype(bf16)
         scores = jnp.where(seen, dot_nt(query, keys) * SCORE, NONE)
@@ -767,23 +770,30 @@
     def sems(count):
         return pltpu.SemaphoreType.DMA((count,))
 
-    other_pages = lax.ppermute(cache_pages, "heads", [(d, d + 1 - 2 * (d % 2)) for d in range(owners)])
+    across = [(d, d + 1 - 2 * (d % 2)) for d in range(owners)]
+    same_core = [list(range(n, owners, 2)) for n in range(2)]
+    other_queries = lax.ppermute(queries, "heads", across)
+    other_c = lax.ppermute(step_c, "heads", across)
+    other_pages = lax.ppermute(cache_pages, "heads", across)
     send = call(
         functools.partial(pack_kernel, group, ways),
         shape((all_rows, HALF + LANES), bf16),
-        [hbm, hbm],
-        vmem,
+        [hbm] * 4,
+        hbm,
         [
-            like(vmem, queries),
-            like(vmem, step_c),
-            vmem((SUB, queries.shape[2]), f32),
-            vmem((SUB, step_c.shape[2]), f32),
-            vmem((step_c.shape[2] // NS, SUB, HALF + LANES), f32),
-            sems(2),
+            vmem((all_rows, HALF + LANES), bf16),
+            vmem((2,) + queries.shape, bf16),
+            vmem((2,) + step_c.shape, bf16),
+            vmem((2, SUB, queries.shape[2]), f32),
+            vmem((2, SUB, step_c.shape[2]), f32),
+            vmem((2, step_c.shape[2] // NS, SUB, HALF + LANES), f32),
+            sems(4),
         ],
         (0, 1 << 19),
-    )(queries, step_c)
-    recv = lax.all_to_all(send, "heads", split_axis=0, concat_axis=0, tiled=True)
+    )(queries, other_queries, step_c, other_c)
+    recv = lax.all_to_all(
+        send, "heads", split_axis=0, concat_axis=0, tiled=True, axis_index_groups=same_core
+    )
 
     block = [
         vmem((prompts, width, length), bf16),
@@ -878,6 +888,7 @@
             vmem((SUB, channels), f32),
             vmem((SUB, channels), f32),
             vmem((SUB, fresh_cache.shape[2]), f32),
+            vmem((SUB, queries.shape[2]), f32),
             vmem((SUB, step_c.shape[2]), f32),
             vmem((steps, SUB, channels), f32),
             like(smem, decay_rate),
@@ -886,7 +897,7 @@
             like(vmem, prompt_dt),
             like(vmem, rates),
             like(vmem, skips),
-            like(vmem, send),
+            like(vmem, queries),
             like(vmem, fresh_cache),
             like(vmem, step_x),
             like(vmem, step_b),
@@ -907,7 +918,7 @@
         prompt_dt,
         rates,
         skips,
-        send,
+        queries,
         fresh_cache,
         step_x,
         step_b,

time: 43.1 us -> 44 us (1.021)
  waiting for transfers between devices: 2.65 us -> 4.49 us
  Pallas kernels: 25.8 us -> 24.6 us
    ppermute x1 -> x3, waiting for transfers between devices: 0.01 us -> 1.53 us  [the longest x1 1.53 us: on_device(): other_c = lax.ppermute(step_c, 'heads', across)]
    pallas_call x1, Pallas kernels: 8.24 us -> 7.28 us  [on_device(): call(state_kernel, (shape((prompts, width, NS), bf16), shape((2, keys, LA...]
    ppermute x1 -> x3, starting transfers between devices: 0.52 us -> 1.03 us  [the longest x1 0.52 us: on_device(): other_pages = lax.ppermute(cache_pages, 'heads', across)]
  transfers between devices with their start and end apart: 3 -> 5, of which waited for: 2 -> 3; matrix products, arithmetic and copies ran while one was open for 0% -> 0% of each run, Pallas kernels for 40% -> 37%
where the time goes in v6:
time: 44 us; the launch traced here: 43.6 us
  Pallas kernels  24.6 us (56%)
  starting transfers between devices  13.8 us (31%)
  waiting for transfers between devices  4.49 us (10%)
  between operations  0.67 us (2%)
    pallas_call x1, Pallas kernels, on_device(): call(state_kernel, (shape((prompts, width, NS), bf16), shape((2, keys, LA...  7.28 us
    all_to_all x1, starting transfers between devices, on_device(): lax.all_to_all(send, 'heads', split_axis=0, concat_axis=0, tiled=True, ax...  7.21 us
    pallas_call x1, Pallas kernels, on_device(): call(prompt_kernel, (shape(prompt_x.shape, bf16), shape((KVH, count, HD),...  7.19 us
    pallas_call x1, Pallas kernels, on_device(): call(serve_kernel, shape((all_rows, HALF + max(LANES, width) - LANES), bf...  6.03 us
    all_to_all x1, starting transfers between devices, on_device(): lax.all_to_all(back, 'heads', split_axis=0, concat_axis=0, tiled=True)  5.6 us
    all_to_all x1, waiting for transfers between devices, on_device(): lax.all_to_all(back, 'heads', split_axis=0, concat_axis=0, tiled=True)  2.38 us
    pallas_call x1, Pallas kernels, on_device(): call(functools.partial(merge_kernel, width), (shape(step_x.shape, bf16),...  2.26 us
    pallas_call x1, Pallas kernels, on_device(): call(functools.partial(pack_kernel, group, ways), shape((all_rows, HALF +...  1.79 us
  transfers between devices with their start and end apart: 5, of which 3 were waited for; matrix products, arithmetic and copies ran while one was open for 0% of the time, Pallas kernels for 37%

profile of v6, /device:TPU:0, one launch (start us, length us, event | category | flops | bytes accessed | tf_op | source)
XLA Modules:
  0.0 43.6 jit_solution(14720590730963580596)
XLA Ops:
  0.6 0.5 %collective-permute-start.2 = (bf16[64,16,256]{2,1,0:T(8,128)(2,1)}, bf16[64,16,256]{2,1,0:T(8,128)(2,1)}, u32[]{:S(2)}, u32[]{:S(2)}) collective-permute-start(bf16[64,16,256]{2,1,0:T(8,128)(2,1)} %param.26), channel_id=1, source_target_pairs={{0,1},{1,0},{2,3},{3,2},{4,5},{5,4},{6,7},{7,6},{8,9},{9,8},{10,11... | collective-permute-start | bytes 1572872 | tf_op jit(solution)/shard_map/ppermute | solution.py:777
  1.1 0.1 collective-permute-start
  1.2 0.4 collective-permute-start.1
  1.7 1.5 %collective-permute-done.1.c_other = bf16[3,2,1024]{2,1,0:T(2,128)(2,1)} collective-permute-done((bf16[3,2,1024]{2,1,0:T(2,128)(2,1)}, bf16[3,2,1024]{2,1,0:T(2,128)(2,1)}, u32[]{:S(2)}, u32[]{:S(2)}) %collective-permute-start.1) | collective-permute-done | bytes 12320 | tf_op jit(solution)/shard_map/ppermute | solution.py:776
  3.2 0.0 collective-permute-done.q_other
  3.2 1.8 %shard_map.184 = bf16[128,640]{1,0:T(8,128)(2,1)} custom-call(bf16[3,2,8192]{2,1,0:T(2,128)(2,1)} %bitcast.21, bf16[3,2,8192]{2,1,0:T(2,128)(2,1)} %collective-permute-done.q_other, bf16[3,2,1024]{2,1,0:T(2,128)(2,1)} %bitcast.25, bf16[3,2,1024]{2,1,0:T(2,128)(2,1)} %collective-permute-done.1.c_other), custom_call_target="tpu_custom_call" | custom-call | bytes 524288 | tf_op jit(solution)/shard_map/pallas_call | solution.py:778
  5.0 7.2 %all-to-all-start = ((bf16[8,16,640]{2,1,0:T(8,128)(2,1)}), bf16[8,16,640]{2,1,0:T(8,128)(2,1)}, u32[]{:S(2)}, u32[]{:S(2)}) async-start(bf16[8,16,640]{2,1,0:T(8,128)(2,1)} %bitcast.18), calls=%async_computation | async-start | bytes 327680 | tf_op jit(solution)/shard_map/all_to_all | solution.py:794
  12.2 7.3 %shard_map.185 = (bf16[8,512,256]{2,1,0:T(8,128)(2,1)}, bf16[2,1024,128]{2,1,0:T(8,128)(2,1)}, bf16[128,128]{1,0:T(8,128)(2,1)}, s32[128,128]{1,0:T(8,128)}, bf16[8,512,256]{2,1,0:T(8,128)(2,1)}) custom-call(f32[128]{0:T(128)} %rate_any.3, f32[128]{0:T(128)} %skip_any.3, s32[8]{0:T(128)} %len_any.3, s32[2,16]{1,0:T(2,128)} %bitcast.32, s32[8,128]{1,0:T(8,128)} %table_any.1, ...), custom_call_target="tpu_custom_call" | custom-call | flops 1207959552 | bytes 6291456 | tf_op jit(solution)/shard_map/pallas_call | solution.py:809
  19.5 0.6 %all-to-all-done = bf16[8,16,640]{2,1,0:T(8,128)(2,1)} async-done(((bf16[8,16,640]{2,1,0:T(8,128)(2,1)}), bf16[8,16,640]{2,1,0:T(8,128)(2,1)}, u32[]{:S(2)}, u32[]{:S(2)}) %all-to-all-start) | async-done | bytes 163872 | tf_op jit(solution)/shard_map/all_to_all | solution.py:794
  20.1 0.0 collective-permute-done.2
  20.1 6.0 %shard_map.186.after_any = bf16[128,896]{1,0:T(8,128)(2,1)} custom-call(bf16[128,640]{1,0:T(8,128)(2,1)} %bitcast.9.recv_any, bf16[1024,256]{1,0:T(8,128)(2,1)} %bitcast.19, bf16[1024,256]{1,0:T(8,128)(2,1)} %bitcast.11.other_any, bf16[2,1024,128]{2,1,0:T(8,128)(2,1)} %get-tuple-element.15.mark_any, bf16[128,128]{1,0:T(8,128)(2,1)} %get-tuple-element.16.hot_any, ...), custom_call_target="tpu_custom_call" | custom-call | flops 134217728 | bytes 4194304 | tf_op jit(solution)/shard_map/pallas_call | solution.py:840
  26.1 5.6 %all-to-all-start.1 = ((bf16[16,8,896]{2,1,0:T(8,128)(2,1)}), bf16[16,8,896]{2,1,0:T(8,128)(2,1)}, u32[]{:S(2)}, u32[]{:S(2)}) async-start(bf16[16,8,896]{2,1,0:T(8,128)(2,1)} %bitcast.17), calls=%async_computation.1 | async-start | bytes 458752 | tf_op jit(solution)/shard_map/all_to_all | solution.py:867
  31.7 7.2 %shard_map.187 = (bf16[8,512,256]{2,1,0:T(8,128)(2,1)}, f32[8,64,128]{2,1,0:T(8,128)}, f32[8,64,128]{2,1,0:T(8,128)}, f32[8,8192]{1,0:T(8,128)}, f32[8,8192]{1,0:T(8,128)}) custom-call(f32[128]{0:T(128)} %rate_any.3, f32[128]{0:T(128)} %skip_any.3, s32[8]{0:T(128)} %len_any.3, bf16[8,8,256]{2,1,0:T(8,128)(2,1)} %dt_any.3, ...), custom_call_target="tpu_custom_call", output_to_operand_aliasing={{0}: (16, {})} | custom-call | flops 2013265920 | bytes 8388608 | tf_op jit(solution)/shard_map/pallas_call | solution.py:872
  38.9 2.4 %all-to-all-done.1 = bf16[16,8,896]{2,1,0:T(8,128)(2,1)} async-done(((bf16[16,8,896]{2,1,0:T(8,128)(2,1)}), bf16[16,8,896]{2,1,0:T(8,128)(2,1)}, u32[]{:S(2)}, u32[]{:S(2)}) %all-to-all-start.1) | async-done | bytes 229408 | tf_op jit(solution)/shard_map/all_to_all | solution.py:867
  41.3 2.3 %shard_map.188 = (bf16[3,2,8192]{2,1,0:T(2,128)(2,1)}, bf16[3,2,8192]{2,1,0:T(2,128)(2,1)}) custom-call(bf16[128,896]{1,0:T(8,128)(2,1)} %bitcast.14.back_any, f32[8,64,128]{2,1,0:T(8,128)} %get-tuple-element.21.own_any, f32[8,64,128]{2,1,0:T(8,128)} %get-tuple-element.22.ownsum_any, f32[8,8192]{1,0:T(8,128)} %get-tuple-element.23.fade_any, ...), custom_call_target="tpu_custom_call" | custom-call | bytes 2097152 | tf_op jit(solution)/shard_map/pallas_call | solution.py:934
Async XLA Ops:
  0.6 19.4 %collective-permute-start.2 = (bf16[64,16,256]{2,1,0:T(8,128)(2,1)}, bf16[64,16,256]{2,1,0:T(8,128)(2,1)}, u32[]{:S(2)}, u32[]{:S(2)}) collective-permute-start(bf16[64,16,256]{2,1,0:T(8,128)(2,1)} %param.26), channel_id=1, source_target_pairs={{0,1},{1,0},{2,3},{3,2},{4,5},{5,4},{6,7},{7,6},{8,9},{9,8},{10,11... | collective-permute-start | bytes 1572872 | tf_op jit(solution)/shard_map/ppermute | solution.py:777
  1.1 2.0 %collective-permute-start = (bf16[3,2,8192]{2,1,0:T(2,128)(2,1)}, bf16[3,2,8192]{2,1,0:T(2,128)(2,1)}, u32[]{:S(2)}, u32[]{:S(2)}) collective-permute-start(bf16[3,2,8192]{2,1,0:T(2,128)(2,1)} %bitcast.20), channel_id=1, source_target_pairs={{0,1},{1,0},{2,3},{3,2},{4,5},{5,4},{6,7},{7,6},{8,9},{9,8},{10,11... | collective-permute-start | bytes 294920 | tf_op jit(solution)/shard_map/ppermute | solution.py:775
  1.2 2.0 %collective-permute-start.1 = (bf16[3,2,1024]{2,1,0:T(2,128)(2,1)}, bf16[3,2,1024]{2,1,0:T(2,128)(2,1)}, u32[]{:S(2)}, u32[]{:S(2)}) collective-permute-start(bf16[3,2,1024]{2,1,0:T(2,128)(2,1)} %bitcast.24), channel_id=1, source_target_pairs={{0,1},{1,0},{2,3},{3,2},{4,5},{5,4},{6,7},{7,6},{8,9},{9,8},{10,11... | collective-permute-start | bytes 36872 | tf_op jit(solution)/shard_map/ppermute | solution.py:776
  5.0 15.1 %all-to-all-start = ((bf16[8,16,640]{2,1,0:T(8,128)(2,1)}), bf16[8,16,640]{2,1,0:T(8,128)(2,1)}, u32[]{:S(2)}, u32[]{:S(2)}) async-start(bf16[8,16,640]{2,1,0:T(8,128)(2,1)} %bitcast.18), calls=%async_computation | async-start | bytes 327680 | tf_op jit(solution)/shard_map/all_to_all | solution.py:794
  26.1 15.2 %all-to-all-start.1 = ((bf16[16,8,896]{2,1,0:T(8,128)(2,1)}), bf16[16,8,896]{2,1,0:T(8,128)(2,1)}, u32[]{:S(2)}, u32[]{:S(2)}) async-start(bf16[16,8,896]{2,1,0:T(8,128)(2,1)} %bitcast.17), calls=%async_computation.1 | async-start | bytes 458752 | tf_op jit(solution)/shard_map/all_to_all | solution.py:867

commit v7 on v5

--- a/solution.py
+++ b/solution.py
@@ -14,6 +14,7 @@
 KVH = 8
 HD = 128
 PAGE = 16
+PAGES = 16
 LANES = 128
 SUB = 8
 HALF = 512
@@ -21,8 +22,9 @@
 LOG2E = math.log2(math.e)
 SCORE = LOG2E / math.sqrt(HD)
 NONE = -1e30
+FLOOR = -1e29
 PAIRS = 6
-MATCH = 32768.0
+LENGTH_BITS = 10
 AHEAD = 2
 EARLY = 2
 VMEM_LIMIT = 64 * 1024 * 1024
@@ -177,10 +179,12 @@
     x_any,
     b_any,
     c_any,
+    pages_any,
+    other_any,
     state_any,
-    mark_any,
-    hot_any,
-    req_any,
+    key_any,
+    value_any,
+    code_any,
     out_any,
     x_held,
     b_held,
@@ -193,9 +197,10 @@
     signs,
     w_tail,
     state_held,
-    mark_held,
-    hot_held,
-    req_held,
+    pages_held,
+    key_held,
+    value_held,
+    code_held,
     rate_ref,
     skip_ref,
     len_ref,
@@ -224,6 +229,7 @@
         sems,
     )
     me = lax.axis_index("heads")
+    core = lax.rem(me, 2)
     first = me * group
     column = pl.multiple_of((first // HPG) * NS, NS)
 
@@ -246,7 +252,8 @@
         x_copy(r).start()
         b_copy(r).start()
 
-    for r in range(AHEAD):
+    pages = fetches([(pages_any, pages_held.at[core]), (other_any, pages_held.at[1 - core])], sems, len(smalls))
+    for r in range(prompts):
         ask(r)
     sign_tables(signs, True)
     level_masks(masks)
@@ -255,10 +262,6 @@
     head_factors(first, dt_ref, rate_ref, skip_ref, len_ref, signs, w_in, w_out, w_skip, w_tail)
 
     def one(r, _):
-        @pl.when(r + AHEAD < prompts)
-        def _():
-            ask(r + AHEAD)
-
         x_copy(r).wait()
         b_copy(r).wait()
         width = x_held.shape[1]
@@ -273,36 +276,36 @@
         c_copy(r).start()
 
     spread = table_ref.shape[1] // owner_ref.shape[1]
-    per_head = table_ref.shape[1] // KVH
-    offset, lane = iota((PAGE, LANES), 0), iota((PAGE, LANES), 1)
-    for n, holder in enumerate((me, me + 1 - 2 * lax.rem(me, 2))):
+    for copy in pages:
+        copy.wait()
+    for n in range(2):
         for r in range(prompts):
             for page in range(spread):
-                entry = holder * spread + page
-                row = table_ref[r, entry] - holder * (prompts * spread)
-                begin = lax.rem(entry, per_head) * PAGE
-                inside = (lane == r) & (offset < len_ref[r] - begin)
-                block = jnp.where(inside, MATCH, 0.0).astype(bf16)
-                mark_held[n, pl.ds(pl.multiple_of(row * PAGE, PAGE), PAGE), :] = block
+                holder = me - core + n
+                row = table_ref[r, holder * spread + page] - holder * (prompts * spread)
+                block = pages_held[n, row]
+                place = pl.ds((n * spread + page) * PAGE, PAGE)
+                columns = pl.ds(r % 2 * HD, HD)
+                key_held[r // 2, place, columns] = block[:, :HD]
+                value_held[r // 2, place, columns] = block[:, HD:]
 
     owners = owner_ref.shape[1]
     rows_dev = slot_ref.shape[0] // owners
     inner = iota((2 * SUB, LANES), 0)
-    lanes = iota((2 * SUB, LANES), 1)
 
     def fill(s, _):
-        block = jnp.full((2 * SUB, LANES), -2, jnp.int32)
+        block = jnp.zeros((2 * SUB, LANES), jnp.int32)
         for n in range(2):
             for i in range(rows_dev):
                 target = owner_ref[slot_ref[(2 * s + n) * rows_dev + i], 2 * s + n]
-                block = jnp.where((inner // SUB == n) & (inner % rows_dev == i), target, block)
+                code = target * (1 << LENGTH_BITS) + len_ref[target]
+                block = jnp.where((inner // SUB == n) & (inner % rows_dev == i), code, block)
         place = pl.ds(pl.multiple_of(s * 2 * SUB, 2 * SUB), 2 * SUB)
-        req_held[place, :] = block
-        hot_held[place, :] = jnp.where(lanes == block, 1.0, 0.0).astype(bf16)
+        code_held[place, :] = block
         return 0
 
     lax.fori_loop(0, owners // 2, fill, 0)
-    marks = fetches([(mark_held, mark_any), (hot_held, hot_any), (req_held, req_any)], sems)
+    marks = fetches([(key_held, key_any), (value_held, value_any), (code_held, code_any)], sems)
 
     def early(r, _):
         c_copy(r).wait()
@@ -321,78 +324,62 @@
 
 def serve_kernel(
     recv_any,
-    pages_any,
-    other_any,
-    mark_any,
-    hot_any,
-    req_any,
+    key_any,
+    value_any,
+    code_any,
     state_any,
     out_ref,
     recv_ref,
     key_ref,
     value_ref,
-    hot_ref,
-    req_ref,
+    code_ref,
     state_ref,
     query_ref,
-    score_ref,
     state_sem,
     sems,
 ):
     rows = recv_ref.shape[0]
-    held = pages_any.shape[0]
     prompts, width = state_ref.shape[0], state_ref.shape[1]
-    mine, other = pl.ds(0, held), pl.ds(held, held)
     copies = fetches(
-        [
-            (recv_any, recv_ref),
-            (hot_any, hot_ref),
-            (pages_any.at[:, pl.ds(0, HD)], key_ref.at[mine, pl.ds(0, HD)]),
-            (other_any.at[:, pl.ds(0, HD)], key_ref.at[other, pl.ds(0, HD)]),
-            (mark_any.at[0], key_ref.at[mine, pl.ds(HD, LANES)]),
-            (mark_any.at[1], key_ref.at[other, pl.ds(HD, LANES)]),
-        ],
-        sems,
-    )
+        [(recv_any, recv_ref), (code_any, code_ref), (key_any, key_ref), (value_any, value_ref)], sems
+    )
+    states = fetches([(state_any.at[r], state_ref.at[r]) for r in range(prompts)], state_sem)
+    heads = HALF // HD
+    keys = key_ref.shape[1]
+    chips = keys // PAGE
+    begin = lax.rem(lax.axis_index("heads") // 2 * chips, PAGES) * PAGE
     copies[0].wait()
     copies[1].wait()
-    heads = HALF // HD
-    for g in range(heads):
-        query_ref[g * rows : (g + 1) * rows, :HD] = recv_ref[:, g * HD : (g + 1) * HD]
-        query_ref[g * rows : (g + 1) * rows, HD:] = hot_ref[...]
-    for copy in copies[2:]:
-        copy.wait()
-    copies = fetches(
-        [
-            (pages_any.at[:, pl.ds(HD, HD)], value_ref.at[mine]),
-            (other_any.at[:, pl.ds(HD, HD)], value_ref.at[other]),
-            (req_any, req_ref),
-        ],
-        sems,
-        len(copies),
-    )
-    states = fetches([(state_any.at[r], state_ref.at[r]) for r in range(prompts)], state_sem)
-    keys = key_ref.shape[0]
-    chunk = min(keys, 2 * NS)
-    widest = jnp.full((heads * rows, LANES), NONE, f32)
-    for k in range(0, keys, chunk):
-        scores = dot_nt(query_ref[...], key_ref[k : k + chunk, :])
-        score_ref[:, k : k + chunk] = scores
-        for b in range(0, chunk, LANES):
-            widest = jnp.maximum(widest, scores[:, b : b + LANES])
-    highest = jnp.max(widest, axis=1, keepdims=True)
-    for copy in copies:
-        copy.wait()
-    total = jnp.zeros((heads * rows, LANES), f32)
+    code = code_ref[...]
+    target = code >> LENGTH_BITS
+    lengths = code & ((1 << LENGTH_BITS) - 1)
+    for r in range(prompts):
+        for g in range(heads):
+            query = recv_ref[:, g * HD : (g + 1) * HD].astype(f32)
+            query_ref[r // 2, g * rows : (g + 1) * rows, r % 2 * HD : (r % 2 + 1) * HD] = jnp.where(
+                target == r, query, 0.0
+            ).astype(bf16)
+    copies[2].wait()
+    scores = jnp.zeros((heads * rows, keys), f32)
+    for pair in range(prompts // 2):
+        scores = scores + dot_nt(query_ref[pair], key_ref[pair])
+    seen = jnp.concatenate([lengths[:, :1]] * heads, axis=0) > iota((heads * rows, keys), 1) + begin
+    scores = jnp.where(seen, scores * SCORE, NONE)
+    highest = jnp.maximum(jnp.max(scores, axis=1, keepdims=True), FLOOR)
+    weight = jnp.exp2(scores - highest)
+    total = jnp.sum(weight, axis=1, keepdims=True)
+    some = total > 0.0
+    safe = jnp.where(some, total, 1.0)
+    result = jnp.where(some, highest + jnp.log2(safe), NONE)
+    weight = weight.astype(bf16)
+    copies[3].wait()
+    targets = jnp.concatenate([target] * heads, axis=0)
     value = jnp.zeros((heads * rows, HD), f32)
-    for k in range(0, keys, chunk):
-        weight = jnp.exp2((score_ref[:, k : k + chunk] - highest) * SCORE)
-        for b in range(0, chunk, LANES):
-            total = total + weight[:, b : b + LANES]
-        value = value + jnp.dot(weight.astype(bf16), value_ref[k : k + chunk, :], preferred_element_type=f32)
-    total = jnp.sum(total, axis=1, keepdims=True)
-    value = value / total
-    result = jnp.where(highest > 0.5 * MATCH, (highest - MATCH) * SCORE + jnp.log2(total), NONE)
+    for pair in range(prompts // 2):
+        both = jnp.dot(weight, value_ref[pair], preferred_element_type=f32)
+        for n in range(2):
+            value = jnp.where(targets == 2 * pair + n, both[:, n * HD : (n + 1) * HD], value)
+    value = value / safe
     lane = iota((rows, LANES), 1)
     sums = jnp.zeros((rows, LANES), f32)
     for g in range(heads):
@@ -409,7 +396,7 @@
     given = recv_ref[...].astype(f32).reshape(rows // SUB, SUB, recv_ref.shape[1])
     ending = lift(given, spare(heads + 1, 0))
     readout = jnp.concatenate([given[..., HALF:], ending], axis=-1).reshape(rows, NS)
-    target = jnp.concatenate([req_ref[...], req_ref[...]], axis=-1)
+    target = jnp.concatenate([target, target], axis=-1)
     found = jnp.zeros((rows, width), f32)
     for r in range(prompts):
         picked = jnp.where(target == r, readout, 0.0).astype(bf16)
@@ -750,6 +737,7 @@
     group, prompts, length = prompt_dt.shape
     width = prompt_x.shape[1]
     keys = cache_pages.shape[0] * PAGE
+    span = 2 * keys // prompts
     steps = step_x.shape[1]
     all_rows = owners * SUB
     shape = jax.ShapeDtypeStruct
@@ -796,23 +784,25 @@
     ]
     tables = [vmem((levels, length, length), bf16), vmem((levels + 1, length, length), bf16)]
     work = 2 * width * length * NS
-    states, marks, hot, requests, early_out = call(
+    states, sorted_keys, sorted_values, codes, early_out = call(
         state_kernel,
         (
             shape((prompts, width, NS), bf16),
-            shape((2, keys, LANES), bf16),
-            shape((all_rows, LANES), bf16),
+            shape((prompts // 2, span, 2 * HD), bf16),
+            shape((prompts // 2, span, 2 * HD), bf16),
             shape((all_rows, LANES), jnp.int32),
             shape(prompt_x.shape, bf16),
         ),
-        [hbm] * 10,
+        [hbm] * 12,
         (hbm,) * 5,
         block
         + tables
         + [vmem((prompts, group, length), f32), vmem((prompts, width, NS), bf16)]
-        + [vmem((2, keys, LANES), bf16), vmem((all_rows, LANES), bf16), vmem((all_rows, LANES), jnp.int32)]
+        + [vmem((2,) + cache_pages.shape, bf16)]
+        + [vmem((prompts // 2, span, 2 * HD), bf16)] * 2
+        + [vmem((all_rows, LANES), jnp.int32)]
         + [like(smem, one) for one in (decay_rate, skip_gain, lengths, owner_list, page_table, row_slot)]
-        + [like(vmem, prompt_dt), sem, sem, sem, sem, sem, sems(7)],
+        + [like(vmem, prompt_dt), sem, sem, sem, sem, sem, sems(9)],
         (work * (prompts + 5 * EARLY), 6 << 20),
     )(
         decay_rate,
@@ -825,35 +815,19 @@
         prompt_x,
         prompt_b,
         prompt_c,
+        cache_pages,
+        other_pages,
     )
 
     back = call(
         serve_kernel,
         shape((all_rows, HALF + max(LANES, width) - LANES), bf16),
-        [hbm] * 7,
+        [hbm] * 5,
         vmem,
-        [
-            like(vmem, recv),
-            vmem((2 * keys, HD + LANES), bf16),
-            vmem((2 * keys, HD), bf16),
-            like(vmem, hot),
-            like(vmem, requests),
-            like(vmem, states),
-            vmem((HALF // HD * all_rows, HD + LANES), bf16),
-            vmem((HALF // HD * all_rows, 2 * keys), f32),
-            sem,
-            sems(9),
-        ],
+        [like(vmem, one) for one in (recv, sorted_keys, sorted_values, codes, states)]
+        + [vmem((prompts // 2, HALF // HD * all_rows, 2 * HD), bf16), sem, sems(4)],
         (8 * all_rows * keys * HD, 4 << 20),
-    )(
-        recv,
-        cache_pages.reshape(keys, 2 * HD),
-        other_pages.reshape(keys, 2 * HD),
-        marks,
-        hot,
-        requests,
-        states,
-    )
+    )(recv, sorted_keys, sorted_values, codes, states)
     returned = lax.all_to_all(back, "heads", split_axis=0, concat_axis=0, tiled=True)
 
     count = HALF // HD * 2 * SUB

time: 43.1 us -> 40 us (0.928)
  Pallas kernels: 25.8 us -> 22.9 us
  waiting for transfers between devices: 2.65 us -> 4.17 us
  starting transfers between devices: 13.4 us -> 11.9 us
    pallas_call x1, Pallas kernels: 8.24 us -> 6.71 us  [on_device(): call(state_kernel, (shape((prompts, width, NS), bf16), shape((prompts //...]
    all_to_all x1, starting transfers between devices: 5.76 us -> 4.23 us  [on_device(): lax.all_to_all(back, 'heads', split_axis=0, concat_axis=0, tiled=True)]
    all_to_all x1, waiting for transfers between devices: 0.27 us -> 1.8 us  [on_device(): lax.all_to_all(send, 'heads', split_axis=0, concat_axis=0, tiled=True)]
    pallas_call x1, Pallas kernels: 6.45 us -> 5.01 us  [on_device(): call(serve_kernel, shape((all_rows, HALF + max(LANES, width) - LANES), bf...]
  transfers between devices with their start and end apart: 3 -> 3, of which waited for: 2 -> 2; matrix products, arithmetic and copies ran while one was open for 0% -> 0% of each run, Pallas kernels for 40% -> 39%
where the time goes in v7:
time: 40 us; the launch traced here: 39.6 us
  Pallas kernels  22.9 us (57%)
  starting transfers between devices  11.9 us (30%)
  waiting for transfers between devices  4.17 us (10%)
  between operations  0.69 us (2%)
    pallas_call x1, Pallas kernels, on_device(): call(prompt_kernel, (shape(prompt_x.shape, bf16), shape((KVH, count, HD),...  7.2 us
    all_to_all x1, starting transfers between devices, on_device(): lax.all_to_all(send, 'heads', split_axis=0, concat_axis=0, tiled=True)  7.1 us
    pallas_call x1, Pallas kernels, on_device(): call(state_kernel, (shape((prompts, width, NS), bf16), shape((prompts //...  6.71 us
    pallas_call x1, Pallas kernels, on_device(): call(serve_kernel, shape((all_rows, HALF + max(LANES, width) - LANES), bf...  5.01 us
    all_to_all x1, starting transfers between devices, on_device(): lax.all_to_all(back, 'heads', split_axis=0, concat_axis=0, tiled=True)  4.23 us
    all_to_all x1, waiting for transfers between devices, on_device(): lax.all_to_all(back, 'heads', split_axis=0, concat_axis=0, tiled=True)  2.37 us
    pallas_call x1, Pallas kernels, on_device(): call(functools.partial(merge_kernel, width), (shape(step_x.shape, bf16),...  2.26 us
    all_to_all x1, waiting for transfers between devices, on_device(): lax.all_to_all(send, 'heads', split_axis=0, concat_axis=0, tiled=True)  1.8 us
  transfers between devices with their start and end apart: 3, of which 2 were waited for; matrix products, arithmetic and copies ran while one was open for 0% of the time, Pallas kernels for 39%

profile of v7, /device:TPU:0, one launch (start us, length us, event | category | flops | bytes accessed | tf_op | source)
XLA Modules:
  0.0 39.6 jit_solution(17451331027093955648)
XLA Ops:
  0.6 0.5 %collective-permute-start = (bf16[64,16,256]{2,1,0:T(8,128)(2,1)}, bf16[64,16,256]{2,1,0:T(8,128)(2,1)}, u32[]{:S(2)}, u32[]{:S(2)}) collective-permute-start(bf16[64,16,256]{2,1,0:T(8,128)(2,1)} %pages_any.1), channel_id=1, source_target_pairs={{0,1},{1,0},{2,3},{3,2},{4,5},{5,4},{6,7},{7,6},{8,9},{9,8},{10,11... | collective-permute-start | bytes 1572872 | tf_op jit(solution)/shard_map/ppermute | solution.py:758
  1.1 1.7 %shard_map.184.send_any = bf16[128,640]{1,0:T(8,128)(2,1)} custom-call(bf16[3,2,8192]{2,1,0:T(2,128)(2,1)} %bitcast.18, bf16[3,2,1024]{2,1,0:T(2,128)(2,1)} %bitcast.19), custom_call_target="tpu_custom_call" | custom-call | bytes 524288 | tf_op jit(solution)/shard_map/pallas_call | solution.py:759
  2.8 7.1 %all-to-all-start = ((bf16[16,8,640]{2,1,0:T(8,128)(2,1)}), bf16[16,8,640]{2,1,0:T(8,128)(2,1)}, u32[]{:S(2)}, u32[]{:S(2)}) async-start(bf16[16,8,640]{2,1,0:T(8,128)(2,1)} %bitcast.16), calls=%async_computation | async-start | bytes 327680 | tf_op jit(solution)/shard_map/all_to_all | solution.py:774
  9.9 0.0 collective-permute-done.other_any
  10.0 6.7 %shard_map.185 = (bf16[8,512,256]{2,1,0:T(8,128)(2,1)}, bf16[4,256,256]{2,1,0:T(8,128)(2,1)}, bf16[4,256,256]{2,1,0:T(8,128)(2,1)}, s32[128,128]{1,0:T(8,128)}, bf16[8,512,256]{2,1,0:T(8,128)(2,1)}) custom-call(f32[128]{0:T(128)} %rate_any.3, f32[128]{0:T(128)} %skip_any.3, s32[8]{0:T(128)} %len_any.3, s32[2,16]{1,0:T(2,128)} %bitcast.26, ...), custom_call_target="tpu_custom_call" | custom-call | flops 1207959552 | bytes 6291456 | tf_op jit(solution)/shard_map/pallas_call | solution.py:787
  16.7 1.8 %all-to-all-done = bf16[16,8,640]{2,1,0:T(8,128)(2,1)} async-done(((bf16[16,8,640]{2,1,0:T(8,128)(2,1)}), bf16[16,8,640]{2,1,0:T(8,128)(2,1)}, u32[]{:S(2)}, u32[]{:S(2)}) %all-to-all-start) | async-done | bytes 163872 | tf_op jit(solution)/shard_map/all_to_all | solution.py:774
  18.5 5.0 %shard_map.186.after_any = bf16[128,896]{1,0:T(8,128)(2,1)} custom-call(bf16[128,640]{1,0:T(8,128)(2,1)} %bitcast.9.recv_any, bf16[4,256,256]{2,1,0:T(8,128)(2,1)} %get-tuple-element.15.key_any, bf16[4,256,256]{2,1,0:T(8,128)(2,1)} %get-tuple-element.16.value_any, s32[128,128]{1,0:T(8,128)} %get-tuple-element.17.code_any, ...), custom_call_target="tpu_custom_call" | custom-call | flops 134217728 | bytes 4194304 | tf_op jit(solution)/shard_map/pallas_call | solution.py:822
  23.5 4.2 %all-to-all-start.1 = ((bf16[16,8,896]{2,1,0:T(8,128)(2,1)}), bf16[16,8,896]{2,1,0:T(8,128)(2,1)}, u32[]{:S(2)}, u32[]{:S(2)}) async-start(bf16[16,8,896]{2,1,0:T(8,128)(2,1)} %bitcast.15), calls=%async_computation.1 | async-start | bytes 458752 | tf_op jit(solution)/shard_map/all_to_all | solution.py:831
  27.7 7.2 %shard_map.187 = (bf16[8,512,256]{2,1,0:T(8,128)(2,1)}, f32[8,64,128]{2,1,0:T(8,128)}, f32[8,64,128]{2,1,0:T(8,128)}, f32[8,8192]{1,0:T(8,128)}, f32[8,8192]{1,0:T(8,128)}) custom-call(f32[128]{0:T(128)} %rate_any.3, f32[128]{0:T(128)} %skip_any.3, s32[8]{0:T(128)} %len_any.3, bf16[8,8,256]{2,1,0:T(8,128)(2,1)} %dt_any.3, ...), custom_call_target="tpu_custom_call", output_to_operand_aliasing={{0}: (16, {})} | custom-call | flops 2013265920 | bytes 8388608 | tf_op jit(solution)/shard_map/pallas_call | solution.py:836
  34.9 2.4 %all-to-all-done.1 = bf16[16,8,896]{2,1,0:T(8,128)(2,1)} async-done(((bf16[16,8,896]{2,1,0:T(8,128)(2,1)}), bf16[16,8,896]{2,1,0:T(8,128)(2,1)}, u32[]{:S(2)}, u32[]{:S(2)}) %all-to-all-start.1) | async-done | bytes 229408 | tf_op jit(solution)/shard_map/all_to_all | solution.py:831
  37.3 2.3 %shard_map.188 = (bf16[3,2,8192]{2,1,0:T(2,128)(2,1)}, bf16[3,2,8192]{2,1,0:T(2,128)(2,1)}) custom-call(bf16[128,896]{1,0:T(8,128)(2,1)} %bitcast.12.back_any, f32[8,64,128]{2,1,0:T(8,128)} %get-tuple-element.21.own_any, f32[8,64,128]{2,1,0:T(8,128)} %get-tuple-element.22.ownsum_any, f32[8,8192]{1,0:T(8,128)} %get-tuple-element.23.fade_any, ...), custom_call_target="tpu_custom_call" | custom-call | bytes 2097152 | tf_op jit(solution)/shard_map/pallas_call | solution.py:897
Async XLA Ops:
  0.6 9.3 %collective-permute-start = (bf16[64,16,256]{2,1,0:T(8,128)(2,1)}, bf16[64,16,256]{2,1,0:T(8,128)(2,1)}, u32[]{:S(2)}, u32[]{:S(2)}) collective-permute-start(bf16[64,16,256]{2,1,0:T(8,128)(2,1)} %pages_any.1), channel_id=1, source_target_pairs={{0,1},{1,0},{2,3},{3,2},{4,5},{5,4},{6,7},{7,6},{8,9},{9,8},{10,11... | collective-permute-start | bytes 1572872 | tf_op jit(solution)/shard_map/ppermute | solution.py:758
  2.8 15.6 %all-to-all-start = ((bf16[16,8,640]{2,1,0:T(8,128)(2,1)}), bf16[16,8,640]{2,1,0:T(8,128)(2,1)}, u32[]{:S(2)}, u32[]{:S(2)}) async-start(bf16[16,8,640]{2,1,0:T(8,128)(2,1)} %bitcast.16), calls=%async_computation | async-start | bytes 327680 | tf_op jit(solution)/shard_map/all_to_all | solution.py:774
  23.5 13.8 %all-to-all-start.1 = ((bf16[16,8,896]{2,1,0:T(8,128)(2,1)}), bf16[16,8,896]{2,1,0:T(8,128)(2,1)}, u32[]{:S(2)}, u32[]{:S(2)}) async-start(bf16[16,8,896]{2,1,0:T(8,128)(2,1)} %bitcast.15), calls=%async_computation.1 | async-start | bytes 458752 | tf_op jit(solution)/shard_map/all_to_all | solution.py:831

commit v8 on v7

--- a/solution.py
+++ b/solution.py
@@ -37,6 +37,11 @@
     return lax.broadcasted_iota(jnp.int32, shape, dim)
 
 
+def exchange_order(owners):
+    bits = (owners - 1).bit_length()
+    return [int(format(owners - 1 - rank, f"0{bits}b")[::-1], 2) for rank in range(owners)]
+
+
 def dot_nt(left, right):
     return lax.dot_general(left, right, (((1,), (1,)), ((), ())), preferred_element_type=f32)
 
@@ -84,13 +89,16 @@
                 pair : pair + 1, e * NS + LANES : (e + 1) * NS
             ]
     real = iota((SUB, HALF), 0) < PAIRS
-    for d in range(0, owners, 2):
-        v, e = d // ways, (d * group) // HPG
-        low = jnp.where(real, q_held[:, v * span : v * span + HALF], rest[e, :, :HALF])
-        high = jnp.where(real, q_held[:, v * span + HALF : (v + 1) * span], rest[e, :, :HALF])
-        out_ref[d * SUB : (d + 2) * SUB, :HALF] = jnp.concatenate([low, high], axis=0).astype(bf16)
-        end = rest[e, :, HALF:]
-        out_ref[d * SUB : (d + 2) * SUB, HALF:] = jnp.concatenate([end, end], axis=0).astype(bf16)
+    order = exchange_order(owners)
+    for rank in range(0, owners, 2):
+        blocks, ends = [], []
+        for d in order[rank : rank + 2]:
+            begin, e = d // ways * span + d % 2 * HALF, (d * group) // HPG
+            blocks.append(jnp.where(real, q_held[:, begin : begin + HALF], rest[e, :, :HALF]))
+            ends.append(rest[e, :, HALF:])
+        place = slice(rank * SUB, (rank + 2) * SUB)
+        out_ref[place, :HALF] = jnp.concatenate(blocks, axis=0).astype(bf16)
+        out_ref[place, HALF:] = jnp.concatenate(ends, axis=0).astype(bf16)
 
 
 def sign_tables(signs, tail):
@@ -293,18 +301,16 @@
     rows_dev = slot_ref.shape[0] // owners
     inner = iota((2 * SUB, LANES), 0)
 
-    def fill(s, _):
+    order = exchange_order(owners)
+    for rank in range(0, owners, 2):
         block = jnp.zeros((2 * SUB, LANES), jnp.int32)
         for n in range(2):
+            s = order[rank + n]
             for i in range(rows_dev):
-                target = owner_ref[slot_ref[(2 * s + n) * rows_dev + i], 2 * s + n]
+                target = owner_ref[slot_ref[s * rows_dev + i], s]
                 code = target * (1 << LENGTH_BITS) + len_ref[target]
                 block = jnp.where((inner // SUB == n) & (inner % rows_dev == i), code, block)
-        place = pl.ds(pl.multiple_of(s * 2 * SUB, 2 * SUB), 2 * SUB)
-        code_held[place, :] = block
-        return 0
-
-    lax.fori_loop(0, owners // 2, fill, 0)
+        code_held[rank * SUB : (rank + 2) * SUB, :] = block
     marks = fetches([(key_held, key_any), (value_held, value_any), (code_held, code_any)], sems)
 
     def early(r, _):
@@ -547,7 +553,9 @@
 
 def own_attention(send_ref, fresh_ref, fresh_held, own_ref, ownsum_ref):
     steps, rows = fresh_ref.shape[0], fresh_ref.shape[1]
-    ways = send_ref.shape[0] // SUB // KVH
+    owners = send_ref.shape[0]
+    order = exchange_order(owners)
+    ways = owners // KVH
     stack_rows(fresh_ref, fresh_held)
     count = HALF // HD * 2 * SUB
     pair = iota((count, SUB), 0) % SUB
@@ -555,8 +563,9 @@
     seen = (key % rows == pair % rows) & (key <= pair) & (key < rows * steps)
     seen = seen | ((pair >= rows * steps) & (key == 0))
     for v in range(KVH):
-        block = send_ref[v * ways * SUB : (v * ways + 2) * SUB]
-        query = jnp.concatenate([block[:, g * HD : (g + 1) * HD] for g in range(HALF // HD)], axis=0)
+        halves = [send_ref[order.index(v * ways + n), :, :HALF].astype(f32) for n in range(2)]
+        parts = [half[:, g * HD : (g + 1) * HD] for g in range(HALF // HD) for half in halves]
+        query = jnp.concatenate(parts, axis=0).astype(bf16)
         keys = fresh_held[:, v * HD : (v + 1) * HD].astype(bf16)
         values = fresh_held[:, (KVH + v) * HD : (KVH + v + 1) * HD].astype(bf16)
         scores = jnp.where(seen, dot_nt(query, keys) * SCORE, NONE)
@@ -645,13 +654,14 @@
     rest = fetches([(own_any, own_ref), (ownsum_any, ownsum_ref)], sems, len(copies))
     for copy in copies:
         copy.wait()
-    owners = back_ref.shape[0] // SUB
+    owners = back_ref.shape[0]
     ways = owners // KVH
+    order = exchange_order(owners)
     steps, rows = mixer_ref.shape[0], mixer_ref.shape[1]
     for d in range(0, owners, 2):
-        block = back_ref[d * SUB : (d + 2) * SUB, :].astype(f32).reshape(2, SUB, back_ref.shape[1])
-        ending = lift(block, spare(back_ref.shape[1] // LANES, 1))
-        if back_ref.shape[1] > HALF:
+        block = jnp.stack([back_ref[order.index(d + n)].astype(f32) for n in range(2)])
+        ending = lift(block, spare(back_ref.shape[2] // LANES, 1))
+        if back_ref.shape[2] > HALF:
             ending = jnp.concatenate([block[..., HALF:], ending], axis=-1)
         found = ending[..., :width]
         found = jnp.concatenate([found[0], found[1]], axis=-1)
@@ -667,9 +677,9 @@
     for v in range(KVH):
         blocks, pieces = [], []
         for d in range(v * ways, (v + 1) * ways, 2):
-            block = back_ref[d * SUB : (d + 2) * SUB, :HALF].astype(f32)
-            packed = block[:, :LANES].reshape(2, SUB, LANES)[:, PAIRS : PAIRS + 1, :]
-            blocks.append(block)
+            block = jnp.stack([back_ref[order.index(d + n), :, :HALF].astype(f32) for n in range(2)])
+            packed = block[:, PAIRS : PAIRS + 1, :LANES]
+            blocks.append(block.reshape(2 * SUB, HALF))
             pieces.append(jnp.where(mine, jnp.broadcast_to(packed, (2, SUB, LANES)), 0.0))
         for g in range(HALF // HD):
             part = slice(g * 2 * SUB, (g + 1) * 2 * SUB)
@@ -771,7 +781,10 @@
         ],
         (0, 1 << 19),
     )(queries, step_c)
-    recv = lax.all_to_all(send, "heads", split_axis=0, concat_axis=0, tiled=True)
+    order = [exchange_order(owners)]
+    recv = lax.all_to_all(
+        send, "heads", split_axis=0, concat_axis=0, tiled=True, axis_index_groups=order
+    )
 
     block = [
         vmem((prompts, width, length), bf16),
@@ -828,7 +841,9 @@
         + [vmem((prompts // 2, HALF // HD * all_rows, 2 * HD), bf16), sem, sems(4)],
         (8 * all_rows * keys * HD, 4 << 20),
     )(recv, sorted_keys, sorted_values, codes, states)
-    returned = lax.all_to_all(back, "heads", split_axis=0, concat_axis=0, tiled=True)
+    returned = lax.all_to_all(
+        back, "heads", split_axis=0, concat_axis=0, tiled=True, axis_index_groups=order
+    ).reshape(owners, SUB, back.shape[1])
 
     count = HALF // HD * 2 * SUB
     channels = step_x.shape[2]
@@ -860,7 +875,7 @@
             like(vmem, prompt_dt),
             like(vmem, rates),
             like(vmem, skips),
-            like(vmem, send),
+            vmem((owners, SUB, HALF + LANES), bf16),
             like(vmem, fresh_cache),
             like(vmem, step_x),
             like(vmem, step_b),
@@ -881,7 +896,7 @@
         prompt_dt,
         rates,
         skips,
-        send,
+        send.reshape(owners, SUB, HALF + LANES),
         fresh_cache,
         step_x,
         step_b,

time: 40 us -> 39.9 us (level)
  waiting for transfers between devices: 4.17 us -> 0.01 us
  starting transfers between devices: 11.9 us -> 16 us
    all_to_all x2, waiting for transfers between devices: 4.17 us -> 0.01 us  [the longest x1 0.01 us: on_device(): lax.all_to_all(send, 'heads', split_axis=0, concat_axis=0, tiled=True, ax...]
    all_to_all x2, starting transfers between devices: 11.3 us -> 15.5 us  [the longest x1 9.67 us: on_device(): lax.all_to_all(send, 'heads', split_axis=0, concat_axis=0, tiled=True, ax...]
  transfers between devices with their start and end apart: 3 -> 3, of which waited for: 2 -> 0; matrix products, arithmetic and copies ran while one was open for 0% -> 0% of each run, Pallas kernels for 39% -> 39%
where the time goes in v8:
time: 39.9 us; the launch traced here: 39.5 us
  Pallas kernels  22.8 us (57%)
  starting transfers between devices  16 us (40%)
  between operations  0.68 us (2%)
    all_to_all x1, starting transfers between devices, on_device(): lax.all_to_all(send, 'heads', split_axis=0, concat_axis=0, tiled=True, ax...  9.67 us
    pallas_call x1, Pallas kernels, on_device(): call(prompt_kernel, (shape(prompt_x.shape, bf16), shape((KVH, count, HD),...  7.18 us
    pallas_call x1, Pallas kernels, on_device(): call(state_kernel, (shape((prompts, width, NS), bf16), shape((prompts //...  6.7 us
    all_to_all x1, starting transfers between devices, on_device(): lax.all_to_all(back, 'heads', split_axis=0, concat_axis=0, tiled=True, ax...  5.78 us
    pallas_call x1, Pallas kernels, on_device(): call(serve_kernel, shape((all_rows, HALF + max(LANES, width) - LANES), bf...  5.01 us
    pallas_call x1, Pallas kernels, on_device(): call(functools.partial(merge_kernel, width), (shape(step_x.shape, bf16),...  2.26 us
    pallas_call x1, Pallas kernels, on_device(): call(functools.partial(pack_kernel, group, ways), shape((all_rows, HALF +...  1.68 us
  transfers between devices with their start and end apart: 3, of which 0 were waited for; matrix products, arithmetic and copies ran while one was open for 0% of the time, Pallas kernels for 39%

profile of v8, /device:TPU:0, one launch (start us, length us, event | category | flops | bytes accessed | tf_op | source)
XLA Modules:
  0.0 39.5 jit_solution(828391028105826480)
XLA Ops:
  0.6 0.5 %collective-permute-start = (bf16[64,16,256]{2,1,0:T(8,128)(2,1)}, bf16[64,16,256]{2,1,0:T(8,128)(2,1)}, u32[]{:S(2)}, u32[]{:S(2)}) collective-permute-start(bf16[64,16,256]{2,1,0:T(8,128)(2,1)} %pages_any.1), channel_id=1, source_target_pairs={{0,1},{1,0},{2,3},{3,2},{4,5},{5,4},{6,7},{7,6},{8,9},{9,8},{10,11... | collective-permute-start | bytes 1572872 | tf_op jit(solution)/shard_map/ppermute | solution.py:768
  1.1 1.7 %shard_map.184 = bf16[128,640]{1,0:T(8,128)(2,1)} custom-call(bf16[3,2,8192]{2,1,0:T(2,128)(2,1)} %bitcast.18, bf16[3,2,1024]{2,1,0:T(2,128)(2,1)} %bitcast.19), custom_call_target="tpu_custom_call" | custom-call | bytes 524288 | tf_op jit(solution)/shard_map/pallas_call | solution.py:769
  2.8 9.7 %all-to-all-start = ((bf16[16,8,640]{2,1,0:T(8,128)(2,1)}), bf16[16,8,640]{2,1,0:T(8,128)(2,1)}, u32[]{:S(2)}, u32[]{:S(2)}) async-start(bf16[16,8,640]{2,1,0:T(8,128)(2,1)} %bitcast.15), calls=%async_computation | async-start | bytes 327680 | tf_op jit(solution)/shard_map/all_to_all | solution.py:785
  12.5 0.0 collective-permute-done.other_any
  12.5 6.7 %shard_map.185 = (bf16[8,512,256]{2,1,0:T(8,128)(2,1)}, bf16[4,256,256]{2,1,0:T(8,128)(2,1)}, bf16[4,256,256]{2,1,0:T(8,128)(2,1)}, s32[128,128]{1,0:T(8,128)}, bf16[8,512,256]{2,1,0:T(8,128)(2,1)}) custom-call(f32[128]{0:T(128)} %rate_any.3, f32[128]{0:T(128)} %skip_any.3, s32[8]{0:T(128)} %len_any.3, s32[2,16]{1,0:T(2,128)} %bitcast.26, ...), custom_call_target="tpu_custom_call" | custom-call | flops 1207959552 | bytes 6291456 | tf_op jit(solution)/shard_map/pallas_call | solution.py:800
  19.2 0.0 all-to-all-done
  19.2 5.0 %shard_map.186.after_any = bf16[128,896]{1,0:T(8,128)(2,1)} custom-call(bf16[128,640]{1,0:T(8,128)(2,1)} %bitcast.9.recv_any, bf16[4,256,256]{2,1,0:T(8,128)(2,1)} %get-tuple-element.15.key_any, bf16[4,256,256]{2,1,0:T(8,128)(2,1)} %get-tuple-element.16.value_any, s32[128,128]{1,0:T(8,128)} %get-tuple-element.17.code_any, ...), custom_call_target="tpu_custom_call" | custom-call | flops 134217728 | bytes 4194304 | tf_op jit(solution)/shard_map/pallas_call | solution.py:835
  24.3 5.8 %all-to-all-start.1 = ((bf16[16,8,896]{2,1,0:T(8,128)(2,1)}), bf16[16,8,896]{2,1,0:T(8,128)(2,1)}, u32[]{:S(2)}, u32[]{:S(2)}) async-start(bf16[16,8,896]{2,1,0:T(8,128)(2,1)} %bitcast.14), calls=%async_computation.1 | async-start | bytes 458752 | tf_op jit(solution)/shard_map/all_to_all | solution.py:844
  30.0 7.2 %shard_map.187 = (bf16[8,512,256]{2,1,0:T(8,128)(2,1)}, f32[8,64,128]{2,1,0:T(8,128)}, f32[8,64,128]{2,1,0:T(8,128)}, f32[8,8192]{1,0:T(8,128)}, f32[8,8192]{1,0:T(8,128)}) custom-call(f32[128]{0:T(128)} %rate_any.3, f32[128]{0:T(128)} %skip_any.3, s32[8]{0:T(128)} %len_any.3, bf16[8,8,256]{2,1,0:T(8,128)(2,1)} %dt_any.3, ...), custom_call_target="tpu_custom_call", output_to_operand_aliasing={{0}: (16, {})} | custom-call | flops 2013265920 | bytes 8388608 | tf_op jit(solution)/shard_map/pallas_call | solution.py:851
  37.2 0.0 all-to-all-done.1.back_any
  37.2 2.3 %shard_map.188 = (bf16[3,2,8192]{2,1,0:T(2,128)(2,1)}, bf16[3,2,8192]{2,1,0:T(2,128)(2,1)}) custom-call(bf16[16,8,896]{2,1,0:T(8,128)(2,1)} %all-to-all-done.1.back_any, f32[8,64,128]{2,1,0:T(8,128)} %get-tuple-element.21.own_any, f32[8,64,128]{2,1,0:T(8,128)} %get-tuple-element.22.ownsum_any, f32[8,8192]{1,0:T(8,128)} %get-tuple-element.23.fade_any, ...), custom_call_target="tpu_custom_call" | custom-call | bytes 2097152 | tf_op jit(solution)/shard_map/pallas_call | solution.py:912
Async XLA Ops:
  0.6 11.9 %collective-permute-start = (bf16[64,16,256]{2,1,0:T(8,128)(2,1)}, bf16[64,16,256]{2,1,0:T(8,128)(2,1)}, u32[]{:S(2)}, u32[]{:S(2)}) collective-permute-start(bf16[64,16,256]{2,1,0:T(8,128)(2,1)} %pages_any.1), channel_id=1, source_target_pairs={{0,1},{1,0},{2,3},{3,2},{4,5},{5,4},{6,7},{7,6},{8,9},{9,8},{10,11... | collective-permute-start | bytes 1572872 | tf_op jit(solution)/shard_map/ppermute | solution.py:768
  2.8 16.4 %all-to-all-start = ((bf16[16,8,640]{2,1,0:T(8,128)(2,1)}), bf16[16,8,640]{2,1,0:T(8,128)(2,1)}, u32[]{:S(2)}, u32[]{:S(2)}) async-start(bf16[16,8,640]{2,1,0:T(8,128)(2,1)} %bitcast.15), calls=%async_computation | async-start | bytes 327680 | tf_op jit(solution)/shard_map/all_to_all | solution.py:785
  24.3 13.0 %all-to-all-start.1 = ((bf16[16,8,896]{2,1,0:T(8,128)(2,1)}), bf16[16,8,896]{2,1,0:T(8,128)(2,1)}, u32[]{:S(2)}, u32[]{:S(2)}) async-start(bf16[16,8,896]{2,1,0:T(8,128)(2,1)} %bitcast.14), calls=%async_computation.1 | async-start | bytes 458752 | tf_op jit(solution)/shard_map/all_to_all | solution.py:844

commit v9 on v8

--- a/solution.py
+++ b/solution.py
@@ -38,8 +38,8 @@
 
 
 def exchange_order(owners):
-    bits = (owners - 1).bit_length()
-    return [int(format(owners - 1 - rank, f"0{bits}b")[::-1], 2) for rank in range(owners)]
+    middle = owners // 4
+    return [middle] + [d for d in range(owners) if d != middle]
 
 
 def dot_nt(left, right):

time: 39.9 us -> 37.9 us (0.950)
  starting transfers between devices: 16 us -> 13.2 us
  waiting for transfers between devices: 0.01 us -> 0.8 us
    all_to_all x1, starting transfers between devices: 9.67 us -> 7.53 us  [on_device(): lax.all_to_all(send, 'heads', split_axis=0, concat_axis=0, tiled=True, ax...]
    all_to_all x1, waiting for transfers between devices: 0.01 us -> 0.78 us  [on_device(): lax.all_to_all(back, 'heads', split_axis=0, concat_axis=0, tiled=True, ax...]
    all_to_all x1, starting transfers between devices: 5.78 us -> 5.13 us  [on_device(): lax.all_to_all(back, 'heads', split_axis=0, concat_axis=0, tiled=True, ax...]
  transfers between devices with their start and end apart: 3 -> 3, of which waited for: 0 -> 1; matrix products, arithmetic and copies ran while one was open for 0% -> 0% of each run, Pallas kernels for 39% -> 42%
where the time goes in v9:
time: 37.9 us; the launch traced here: 37.5 us
  Pallas kernels  22.8 us (60%)
  starting transfers between devices  13.2 us (35%)
  waiting for transfers between devices  0.8 us (2%)
  between operations  0.67 us (2%)
    all_to_all x1, starting transfers between devices, on_device(): lax.all_to_all(send, 'heads', split_axis=0, concat_axis=0, tiled=True, ax...  7.53 us
    pallas_call x1, Pallas kernels, on_device(): call(prompt_kernel, (shape(prompt_x.shape, bf16), shape((KVH, count, HD),...  7.18 us
    pallas_call x1, Pallas kernels, on_device(): call(state_kernel, (shape((prompts, width, NS), bf16), shape((prompts //...  6.71 us
    all_to_all x1, starting transfers between devices, on_device(): lax.all_to_all(back, 'heads', split_axis=0, concat_axis=0, tiled=True, ax...  5.13 us
    pallas_call x1, Pallas kernels, on_device(): call(serve_kernel, shape((all_rows, HALF + max(LANES, width) - LANES), bf...  5.01 us
    pallas_call x1, Pallas kernels, on_device(): call(functools.partial(merge_kernel, width), (shape(step_x.shape, bf16),...  2.26 us
    pallas_call x1, Pallas kernels, on_device(): call(functools.partial(pack_kernel, group, ways), shape((all_rows, HALF +...  1.68 us
    all_to_all x1, waiting for transfers between devices, on_device(): lax.all_to_all(back, 'heads', split_axis=0, concat_axis=0, tiled=True, ax...  0.78 us
  transfers between devices with their start and end apart: 3, of which 1 were waited for; matrix products, arithmetic and copies ran while one was open for 0% of the time, Pallas kernels for 42%

profile of v9, /device:TPU:0, one launch (start us, length us, event | category | flops | bytes accessed | tf_op | source)
XLA Modules:
  0.0 37.5 jit_solution(9044639712329074718)
XLA Ops:
  0.6 0.5 %collective-permute-start = (bf16[64,16,256]{2,1,0:T(8,128)(2,1)}, bf16[64,16,256]{2,1,0:T(8,128)(2,1)}, u32[]{:S(2)}, u32[]{:S(2)}) collective-permute-start(bf16[64,16,256]{2,1,0:T(8,128)(2,1)} %pages_any.1), channel_id=1, source_target_pairs={{0,1},{1,0},{2,3},{3,2},{4,5},{5,4},{6,7},{7,6},{8,9},{9,8},{10,11... | collective-permute-start | bytes 1572872 | tf_op jit(solution)/shard_map/ppermute | solution.py:768
  1.1 1.7 %shard_map.184 = bf16[128,640]{1,0:T(8,128)(2,1)} custom-call(bf16[3,2,8192]{2,1,0:T(2,128)(2,1)} %bitcast.18, bf16[3,2,1024]{2,1,0:T(2,128)(2,1)} %bitcast.19), custom_call_target="tpu_custom_call" | custom-call | bytes 524288 | tf_op jit(solution)/shard_map/pallas_call | solution.py:769
  2.8 7.5 %all-to-all-start = ((bf16[16,8,640]{2,1,0:T(8,128)(2,1)}), bf16[16,8,640]{2,1,0:T(8,128)(2,1)}, u32[]{:S(2)}, u32[]{:S(2)}) async-start(bf16[16,8,640]{2,1,0:T(8,128)(2,1)} %bitcast.15), calls=%async_computation | async-start | bytes 327680 | tf_op jit(solution)/shard_map/all_to_all | solution.py:785
  10.4 0.0 collective-permute-done.other_any
  10.4 6.7 %shard_map.185 = (bf16[8,512,256]{2,1,0:T(8,128)(2,1)}, bf16[4,256,256]{2,1,0:T(8,128)(2,1)}, bf16[4,256,256]{2,1,0:T(8,128)(2,1)}, s32[128,128]{1,0:T(8,128)}, bf16[8,512,256]{2,1,0:T(8,128)(2,1)}) custom-call(f32[128]{0:T(128)} %rate_any.3, f32[128]{0:T(128)} %skip_any.3, s32[8]{0:T(128)} %len_any.3, s32[2,16]{1,0:T(2,128)} %bitcast.26, ...), custom_call_target="tpu_custom_call" | custom-call | flops 1207959552 | bytes 6291456 | tf_op jit(solution)/shard_map/pallas_call | solution.py:800
  17.1 0.0 all-to-all-done
  17.1 5.0 %shard_map.186.after_any = bf16[128,896]{1,0:T(8,128)(2,1)} custom-call(bf16[128,640]{1,0:T(8,128)(2,1)} %bitcast.9.recv_any, bf16[4,256,256]{2,1,0:T(8,128)(2,1)} %get-tuple-element.15.key_any, bf16[4,256,256]{2,1,0:T(8,128)(2,1)} %get-tuple-element.16.value_any, s32[128,128]{1,0:T(8,128)} %get-tuple-element.17.code_any, ...), custom_call_target="tpu_custom_call" | custom-call | flops 134217728 | bytes 4194304 | tf_op jit(solution)/shard_map/pallas_call | solution.py:835
  22.1 5.1 %all-to-all-start.1 = ((bf16[16,8,896]{2,1,0:T(8,128)(2,1)}), bf16[16,8,896]{2,1,0:T(8,128)(2,1)}, u32[]{:S(2)}, u32[]{:S(2)}) async-start(bf16[16,8,896]{2,1,0:T(8,128)(2,1)} %bitcast.14), calls=%async_computation.1 | async-start | bytes 458752 | tf_op jit(solution)/shard_map/all_to_all | solution.py:844
  27.2 7.2 %shard_map.187 = (bf16[8,512,256]{2,1,0:T(8,128)(2,1)}, f32[8,64,128]{2,1,0:T(8,128)}, f32[8,64,128]{2,1,0:T(8,128)}, f32[8,8192]{1,0:T(8,128)}, f32[8,8192]{1,0:T(8,128)}) custom-call(f32[128]{0:T(128)} %rate_any.3, f32[128]{0:T(128)} %skip_any.3, s32[8]{0:T(128)} %len_any.3, bf16[8,8,256]{2,1,0:T(8,128)(2,1)} %dt_any.3, ...), custom_call_target="tpu_custom_call", output_to_operand_aliasing={{0}: (16, {})} | custom-call | flops 2013265920 | bytes 8388608 | tf_op jit(solution)/shard_map/pallas_call | solution.py:851
  34.4 0.8 %all-to-all-done.1.back_any = bf16[16,8,896]{2,1,0:T(8,128)(2,1)} async-done(((bf16[16,8,896]{2,1,0:T(8,128)(2,1)}), bf16[16,8,896]{2,1,0:T(8,128)(2,1)}, u32[]{:S(2)}, u32[]{:S(2)}) %all-to-all-start.1) | async-done | bytes 229408 | tf_op jit(solution)/shard_map/all_to_all | solution.py:844
  35.2 2.3 %shard_map.188 = (bf16[3,2,8192]{2,1,0:T(2,128)(2,1)}, bf16[3,2,8192]{2,1,0:T(2,128)(2,1)}) custom-call(bf16[16,8,896]{2,1,0:T(8,128)(2,1)} %all-to-all-done.1.back_any, f32[8,64,128]{2,1,0:T(8,128)} %get-tuple-element.21.own_any, f32[8,64,128]{2,1,0:T(8,128)} %get-tuple-element.22.ownsum_any, f32[8,8192]{1,0:T(8,128)} %get-tuple-element.23.fade_any, ...), custom_call_target="tpu_custom_call" | custom-call | bytes 2097152 | tf_op jit(solution)/shard_map/pallas_call | solution.py:912
Async XLA Ops:
  0.6 9.7 %collective-permute-start = (bf16[64,16,256]{2,1,0:T(8,128)(2,1)}, bf16[64,16,256]{2,1,0:T(8,128)(2,1)}, u32[]{:S(2)}, u32[]{:S(2)}) collective-permute-start(bf16[64,16,256]{2,1,0:T(8,128)(2,1)} %pages_any.1), channel_id=1, source_target_pairs={{0,1},{1,0},{2,3},{3,2},{4,5},{5,4},{6,7},{7,6},{8,9},{9,8},{10,11... | collective-permute-start | bytes 1572872 | tf_op jit(solution)/shard_map/ppermute | solution.py:768
  2.8 14.3 %all-to-all-start = ((bf16[16,8,640]{2,1,0:T(8,128)(2,1)}), bf16[16,8,640]{2,1,0:T(8,128)(2,1)}, u32[]{:S(2)}, u32[]{:S(2)}) async-start(bf16[16,8,640]{2,1,0:T(8,128)(2,1)} %bitcast.15), calls=%async_computation | async-start | bytes 327680 | tf_op jit(solution)/shard_map/all_to_all | solution.py:785
  22.1 13.1 %all-to-all-start.1 = ((bf16[16,8,896]{2,1,0:T(8,128)(2,1)}), bf16[16,8,896]{2,1,0:T(8,128)(2,1)}, u32[]{:S(2)}, u32[]{:S(2)}) async-start(bf16[16,8,896]{2,1,0:T(8,128)(2,1)} %bitcast.14), calls=%async_computation.1 | async-start | bytes 458752 | tf_op jit(solution)/shard_map/all_to_all | solution.py:844

commit v10 on v9

--- a/solution.py
+++ b/solution.py
@@ -369,6 +369,9 @@
     scores = jnp.zeros((heads * rows, keys), f32)
     for pair in range(prompts // 2):
         scores = scores + dot_nt(query_ref[pair], key_ref[pair])
+    copies[3].wait()
+    for copy in states:
+        copy.wait()
     seen = jnp.concatenate([lengths[:, :1]] * heads, axis=0) > iota((heads * rows, keys), 1) + begin
     scores = jnp.where(seen, scores * SCORE, NONE)
     highest = jnp.maximum(jnp.max(scores, axis=1, keepdims=True), FLOOR)
@@ -378,7 +381,6 @@
     safe = jnp.where(some, total, 1.0)
     result = jnp.where(some, highest + jnp.log2(safe), NONE)
     weight = weight.astype(bf16)
-    copies[3].wait()
     targets = jnp.concatenate([target] * heads, axis=0)
     value = jnp.zeros((heads * rows, HD), f32)
     for pair in range(prompts // 2):
@@ -406,7 +408,6 @@
     found = jnp.zeros((rows, width), f32)
     for r in range(prompts):
         picked = jnp.where(target == r, readout, 0.0).astype(bf16)
-        states[r].wait()
         found = found + dot_nt(picked, state_ref[r])
     if width < LANES:
         found = jnp.concatenate([found, jnp.zeros((rows, LANES - width), f32)], axis=-1)

time: 37.9 us -> 37.4 us (0.987)
  Pallas kernels: 22.8 us -> 22.4 us
    pallas_call x1, Pallas kernels: 5.01 us -> 4.53 us  [on_device(): call(serve_kernel, shape((all_rows, HALF + max(LANES, width) - LANES), bf...]
where the time goes in v10:
time: 37.4 us; the launch traced here: 37 us
  Pallas kernels  22.4 us (60%)
  starting transfers between devices  13.2 us (35%)
  waiting for transfers between devices  0.79 us (2%)
  between operations  0.67 us (2%)
    all_to_all x1, starting transfers between devices, on_device(): lax.all_to_all(send, 'heads', split_axis=0, concat_axis=0, tiled=True, ax...  7.53 us
    pallas_call x1, Pallas kernels, on_device(): call(prompt_kernel, (shape(prompt_x.shape, bf16), shape((KVH, count, HD),...  7.19 us
    pallas_call x1, Pallas kernels, on_device(): call(state_kernel, (shape((prompts, width, NS), bf16), shape((prompts //...  6.71 us
    all_to_all x1, starting transfers between devices, on_device(): lax.all_to_all(back, 'heads', split_axis=0, concat_axis=0, tiled=True, ax...  5.13 us
    pallas_call x1, Pallas kernels, on_device(): call(serve_kernel, shape((all_rows, HALF + max(LANES, width) - LANES), bf...  4.53 us
    pallas_call x1, Pallas kernels, on_device(): call(functools.partial(merge_kernel, width), (shape(step_x.shape, bf16),...  2.26 us
    pallas_call x1, Pallas kernels, on_device(): call(functools.partial(pack_kernel, group, ways), shape((all_rows, HALF +...  1.68 us
    all_to_all x1, waiting for transfers between devices, on_device(): lax.all_to_all(back, 'heads', split_axis=0, concat_axis=0, tiled=True, ax...  0.78 us
  transfers between devices with their start and end apart: 3, of which 1 were waited for; matrix products, arithmetic and copies ran while one was open for 0% of the time, Pallas kernels for 42%

profile of v10, /device:TPU:0, one launch (start us, length us, event | category | flops | bytes accessed | tf_op | source)
XLA Modules:
  0.0 37.0 jit_solution(12939264336783150217)
XLA Ops:
  0.6 0.5 %collective-permute-start = (bf16[64,16,256]{2,1,0:T(8,128)(2,1)}, bf16[64,16,256]{2,1,0:T(8,128)(2,1)}, u32[]{:S(2)}, u32[]{:S(2)}) collective-permute-start(bf16[64,16,256]{2,1,0:T(8,128)(2,1)} %pages_any.1), channel_id=1, source_target_pairs={{0,1},{1,0},{2,3},{3,2},{4,5},{5,4},{6,7},{7,6},{8,9},{9,8},{10,11... | collective-permute-start | bytes 1572872 | tf_op jit(solution)/shard_map/ppermute | solution.py:769
  1.1 1.7 %shard_map.184 = bf16[128,640]{1,0:T(8,128)(2,1)} custom-call(bf16[3,2,8192]{2,1,0:T(2,128)(2,1)} %bitcast.18, bf16[3,2,1024]{2,1,0:T(2,128)(2,1)} %bitcast.19), custom_call_target="tpu_custom_call" | custom-call | bytes 524288 | tf_op jit(solution)/shard_map/pallas_call | solution.py:770
  2.8 7.5 %all-to-all-start = ((bf16[16,8,640]{2,1,0:T(8,128)(2,1)}), bf16[16,8,640]{2,1,0:T(8,128)(2,1)}, u32[]{:S(2)}, u32[]{:S(2)}) async-start(bf16[16,8,640]{2,1,0:T(8,128)(2,1)} %bitcast.15), calls=%async_computation | async-start | bytes 327680 | tf_op jit(solution)/shard_map/all_to_all | solution.py:786
  10.4 0.0 collective-permute-done.other_any
  10.4 6.7 %shard_map.185 = (bf16[8,512,256]{2,1,0:T(8,128)(2,1)}, bf16[4,256,256]{2,1,0:T(8,128)(2,1)}, bf16[4,256,256]{2,1,0:T(8,128)(2,1)}, s32[128,128]{1,0:T(8,128)}, bf16[8,512,256]{2,1,0:T(8,128)(2,1)}) custom-call(f32[128]{0:T(128)} %rate_any.3, f32[128]{0:T(128)} %skip_any.3, s32[8]{0:T(128)} %len_any.3, s32[2,16]{1,0:T(2,128)} %bitcast.26, ...), custom_call_target="tpu_custom_call" | custom-call | flops 1207959552 | bytes 6291456 | tf_op jit(solution)/shard_map/pallas_call | solution.py:801
  17.1 0.0 all-to-all-done
  17.1 4.5 %shard_map.186.after_any = bf16[128,896]{1,0:T(8,128)(2,1)} custom-call(bf16[128,640]{1,0:T(8,128)(2,1)} %bitcast.9.recv_any, bf16[4,256,256]{2,1,0:T(8,128)(2,1)} %get-tuple-element.15.key_any, bf16[4,256,256]{2,1,0:T(8,128)(2,1)} %get-tuple-element.16.value_any, s32[128,128]{1,0:T(8,128)} %get-tuple-element.17.code_any, ...), custom_call_target="tpu_custom_call" | custom-call | flops 134217728 | bytes 4194304 | tf_op jit(solution)/shard_map/pallas_call | solution.py:836
  21.6 5.1 %all-to-all-start.1 = ((bf16[16,8,896]{2,1,0:T(8,128)(2,1)}), bf16[16,8,896]{2,1,0:T(8,128)(2,1)}, u32[]{:S(2)}, u32[]{:S(2)}) async-start(bf16[16,8,896]{2,1,0:T(8,128)(2,1)} %bitcast.14), calls=%async_computation.1 | async-start | bytes 458752 | tf_op jit(solution)/shard_map/all_to_all | solution.py:845
  26.8 7.2 %shard_map.187 = (bf16[8,512,256]{2,1,0:T(8,128)(2,1)}, f32[8,64,128]{2,1,0:T(8,128)}, f32[8,64,128]{2,1,0:T(8,128)}, f32[8,8192]{1,0:T(8,128)}, f32[8,8192]{1,0:T(8,128)}) custom-call(f32[128]{0:T(128)} %rate_any.3, f32[128]{0:T(128)} %skip_any.3, s32[8]{0:T(128)} %len_any.3, bf16[8,8,256]{2,1,0:T(8,128)(2,1)} %dt_any.3, ...), custom_call_target="tpu_custom_call", output_to_operand_aliasing={{0}: (16, {})} | custom-call | flops 2013265920 | bytes 8388608 | tf_op jit(solution)/shard_map/pallas_call | solution.py:852
  34.0 0.8 %all-to-all-done.1.back_any = bf16[16,8,896]{2,1,0:T(8,128)(2,1)} async-done(((bf16[16,8,896]{2,1,0:T(8,128)(2,1)}), bf16[16,8,896]{2,1,0:T(8,128)(2,1)}, u32[]{:S(2)}, u32[]{:S(2)}) %all-to-all-start.1) | async-done | bytes 229408 | tf_op jit(solution)/shard_map/all_to_all | solution.py:845
  34.7 2.3 %shard_map.188 = (bf16[3,2,8192]{2,1,0:T(2,128)(2,1)}, bf16[3,2,8192]{2,1,0:T(2,128)(2,1)}) custom-call(bf16[16,8,896]{2,1,0:T(8,128)(2,1)} %all-to-all-done.1.back_any, f32[8,64,128]{2,1,0:T(8,128)} %get-tuple-element.21.own_any, f32[8,64,128]{2,1,0:T(8,128)} %get-tuple-element.22.ownsum_any, f32[8,8192]{1,0:T(8,128)} %get-tuple-element.23.fade_any, ...), custom_call_target="tpu_custom_call" | custom-call | bytes 2097152 | tf_op jit(solution)/shard_map/pallas_call | solution.py:913
Async XLA Ops:
  0.6 9.7 %collective-permute-start = (bf16[64,16,256]{2,1,0:T(8,128)(2,1)}, bf16[64,16,256]{2,1,0:T(8,128)(2,1)}, u32[]{:S(2)}, u32[]{:S(2)}) collective-permute-start(bf16[64,16,256]{2,1,0:T(8,128)(2,1)} %pages_any.1), channel_id=1, source_target_pairs={{0,1},{1,0},{2,3},{3,2},{4,5},{5,4},{6,7},{7,6},{8,9},{9,8},{10,11... | collective-permute-start | bytes 1572872 | tf_op jit(solution)/shard_map/ppermute | solution.py:769
  2.8 14.3 %all-to-all-start = ((bf16[16,8,640]{2,1,0:T(8,128)(2,1)}), bf16[16,8,640]{2,1,0:T(8,128)(2,1)}, u32[]{:S(2)}, u32[]{:S(2)}) async-start(bf16[16,8,640]{2,1,0:T(8,128)(2,1)} %bitcast.15), calls=%async_computation | async-start | bytes 327680 | tf_op jit(solution)/shard_map/all_to_all | solution.py:786
  21.6 13.1 %all-to-all-start.1 = ((bf16[16,8,896]{2,1,0:T(8,128)(2,1)}), bf16[16,8,896]{2,1,0:T(8,128)(2,1)}, u32[]{:S(2)}, u32[]{:S(2)}) async-start(bf16[16,8,896]{2,1,0:T(8,128)(2,1)} %bitcast.14), calls=%async_computation.1 | async-start | bytes 458752 | tf_op jit(solution)/shard_map/all_to_all | solution.py:845

commit v11 on v10

--- a/solution.py
+++ b/solution.py
@@ -39,7 +39,7 @@
 
 def exchange_order(owners):
     middle = owners // 4
-    return [middle] + [d for d in range(owners) if d != middle]
+    return [middle] + [d for d in reversed(range(owners)) if d != middle]
 
 
 def dot_nt(left, right):
@@ -263,26 +263,26 @@
     pages = fetches([(pages_any, pages_held.at[core]), (other_any, pages_held.at[1 - core])], sems, len(smalls))
     for r in range(prompts):
         ask(r)
+    for r in range(EARLY):
+        c_copy(r).start()
     sign_tables(signs, True)
     level_masks(masks)
     for copy in smalls:
         copy.wait()
     head_factors(first, dt_ref, rate_ref, skip_ref, len_ref, signs, w_in, w_out, w_skip, w_tail)
 
-    def one(r, _):
-        x_copy(r).wait()
-        b_copy(r).wait()
-        width = x_held.shape[1]
-        inputs = x_held[r].astype(f32).reshape(group, HP, length)
-        scaled = (inputs * w_tail[r][:, None, :]).astype(bf16).reshape(width, length)
-        state_held[r] = jnp.dot(scaled, b_held[r], preferred_element_type=f32).astype(bf16)
-        state_copy(r).start()
-        return 0
-
-    lax.fori_loop(0, prompts, one, 0, unroll=2)
-    for r in range(EARLY):
-        c_copy(r).start()
-
+    width = x_held.shape[1]
+    for begin in range(0, prompts, prompts // 2):
+        some = range(begin, begin + prompts // 2)
+        for r in some:
+            x_copy(r).wait()
+            b_copy(r).wait()
+        for r in some:
+            inputs = x_held[r].astype(f32).reshape(group, HP, length)
+            scaled = (inputs * w_tail[r][:, None, :]).astype(bf16).reshape(width, length)
+            state_held[r] = jnp.dot(scaled, b_held[r], preferred_element_type=f32).astype(bf16)
+        for r in some:
+            state_copy(r).start()
     spread = table_ref.shape[1] // owner_ref.shape[1]
     for copy in pages:
         copy.wait()
@@ -313,13 +313,12 @@
         code_held[rank * SUB : (rank + 2) * SUB, :] = block
     marks = fetches([(key_held, key_any), (value_held, value_any), (code_held, code_any)], sems)
 
-    def early(r, _):
+    for r in range(EARLY):
         c_copy(r).wait()
+    for r in range(EARLY):
         prompt_result(r, x_held, b_held, c_held, w_in, w_out, w_skip, masks, out_held)
+    for r in range(EARLY):
         out_copy(r).start()
-        return 0
-
-    lax.fori_loop(0, EARLY, early, 0, unroll=2)
     for copy in marks:
         copy.wait()
     for r in range(prompts):
@@ -533,19 +532,25 @@
         [(own_ref, own_any), (ownsum_ref, ownsum_any), (fade_ref, fade_any), (local_ref, local_any)], sems
     )
 
-    def one(r, _):
-        @pl.when(r + AHEAD < prompts)
+    def some(n, _):
+        begin = EARLY + n * AHEAD
+
+        @pl.when(begin + AHEAD < prompts)
         def _():
-            ask(r + AHEAD)
-
-        x_copy(r).wait()
-        b_copy(r).wait()
-        c_copy(r).wait()
-        prompt_result(r, x_held, b_held, c_held, w_in, w_out, w_skip, masks, out_held)
-        out_copy(r).start()
+            for r in range(AHEAD):
+                ask(begin + AHEAD + r)
+
+        for r in range(AHEAD):
+            x_copy(begin + r).wait()
+            b_copy(begin + r).wait()
+            c_copy(begin + r).wait()
+        for r in range(AHEAD):
+            prompt_result(begin + r, x_held, b_held, c_held, w_in, w_out, w_skip, masks, out_held)
+        for r in range(AHEAD):
+            out_copy(begin + r).start()
         return 0
 
-    lax.fori_loop(EARLY, prompts, one, 0, unroll=2)
+    lax.fori_loop(0, (prompts - EARLY) // AHEAD, some, 0)
     for copy in outs:
         copy.wait()
     for r in range(EARLY, prompts):

time: 37.4 us -> 37.3 us (level)
  waiting for transfers between devices: 0.79 us -> 3.36 us
  Pallas kernels: 22.4 us -> 20.6 us
  starting transfers between devices: 13.2 us -> 12.2 us
    all_to_all x1, waiting for transfers between devices: 0.01 us -> 1.82 us  [on_device(): lax.all_to_all(send, 'heads', split_axis=0, concat_axis=0, tiled=True, ax...]
    pallas_call x1, Pallas kernels: 6.71 us -> 5.29 us  [on_device(): call(state_kernel, (shape((prompts, width, NS), bf16), shape((prompts //...]
    all_to_all x1, starting transfers between devices: 5.13 us -> 4.08 us  [on_device(): lax.all_to_all(back, 'heads', split_axis=0, concat_axis=0, tiled=True, ax...]
    all_to_all x1, waiting for transfers between devices: 0.78 us -> 1.54 us  [on_device(): lax.all_to_all(back, 'heads', split_axis=0, concat_axis=0, tiled=True, ax...]
  transfers between devices with their start and end apart: 3 -> 3, of which waited for: 1 -> 2; matrix products, arithmetic and copies ran while one was open for 0% -> 0% of each run, Pallas kernels for 42% -> 38%
where the time goes in v11:
time: 37.3 us; the launch traced here: 36.8 us
  Pallas kernels  20.6 us (55%)
  starting transfers between devices  12.2 us (33%)
  waiting for transfers between devices  3.36 us (9%)
  between operations  0.67 us (2%)
    all_to_all x1, starting transfers between devices, on_device(): lax.all_to_all(send, 'heads', split_axis=0, concat_axis=0, tiled=True, ax...  7.57 us
    pallas_call x1, Pallas kernels, on_device(): call(prompt_kernel, (shape(prompt_x.shape, bf16), shape((KVH, count, HD),...  6.87 us
    pallas_call x1, Pallas kernels, on_device(): call(state_kernel, (shape((prompts, width, NS), bf16), shape((prompts //...  5.29 us
    pallas_call x1, Pallas kernels, on_device(): call(serve_kernel, shape((all_rows, HALF + max(LANES, width) - LANES), bf...  4.53 us
    all_to_all x1, starting transfers between devices, on_device(): lax.all_to_all(back, 'heads', split_axis=0, concat_axis=0, tiled=True, ax...  4.08 us
    pallas_call x1, Pallas kernels, on_device(): call(functools.partial(merge_kernel, width), (shape(step_x.shape, bf16),...  2.26 us
    all_to_all x1, waiting for transfers between devices, on_device(): lax.all_to_all(send, 'heads', split_axis=0, concat_axis=0, tiled=True, ax...  1.82 us
    pallas_call x1, Pallas kernels, on_device(): call(functools.partial(pack_kernel, group, ways), shape((all_rows, HALF +...  1.68 us
  transfers between devices with their start and end apart: 3, of which 2 were waited for; matrix products, arithmetic and copies ran while one was open for 0% of the time, Pallas kernels for 38%

profile of v11, /device:TPU:0, one launch (start us, length us, event | category | flops | bytes accessed | tf_op | source)
XLA Modules:
  0.0 36.8 jit_solution(14919901819193183675)
XLA Ops:
  0.6 0.5 %collective-permute-start = (bf16[64,16,256]{2,1,0:T(8,128)(2,1)}, bf16[64,16,256]{2,1,0:T(8,128)(2,1)}, u32[]{:S(2)}, u32[]{:S(2)}) collective-permute-start(bf16[64,16,256]{2,1,0:T(8,128)(2,1)} %pages_any.1), channel_id=1, source_target_pairs={{0,1},{1,0},{2,3},{3,2},{4,5},{5,4},{6,7},{7,6},{8,9},{9,8},{10,11... | collective-permute-start | bytes 1572872 | tf_op jit(solution)/shard_map/ppermute | solution.py:774
  1.1 1.7 %shard_map.184 = bf16[128,640]{1,0:T(8,128)(2,1)} custom-call(bf16[3,2,8192]{2,1,0:T(2,128)(2,1)} %bitcast.18, bf16[3,2,1024]{2,1,0:T(2,128)(2,1)} %bitcast.19), custom_call_target="tpu_custom_call" | custom-call | bytes 524288 | tf_op jit(solution)/shard_map/pallas_call | solution.py:775
  2.8 7.6 %all-to-all-start = ((bf16[16,8,640]{2,1,0:T(8,128)(2,1)}), bf16[16,8,640]{2,1,0:T(8,128)(2,1)}, u32[]{:S(2)}, u32[]{:S(2)}) async-start(bf16[16,8,640]{2,1,0:T(8,128)(2,1)} %bitcast.15), calls=%async_computation | async-start | bytes 327680 | tf_op jit(solution)/shard_map/all_to_all | solution.py:791
  10.4 0.0 collective-permute-done.other_any
  10.4 5.3 %shard_map.185 = (bf16[8,512,256]{2,1,0:T(8,128)(2,1)}, bf16[4,256,256]{2,1,0:T(8,128)(2,1)}, bf16[4,256,256]{2,1,0:T(8,128)(2,1)}, s32[128,128]{1,0:T(8,128)}, bf16[8,512,256]{2,1,0:T(8,128)(2,1)}) custom-call(f32[128]{0:T(128)} %rate_any.3, f32[128]{0:T(128)} %skip_any.3, s32[8]{0:T(128)} %len_any.3, s32[2,16]{1,0:T(2,128)} %bitcast.26, ...), custom_call_target="tpu_custom_call" | custom-call | flops 1207959552 | bytes 6291456 | tf_op jit(solution)/shard_map/pallas_call | solution.py:806
  15.7 1.8 %all-to-all-done = bf16[16,8,640]{2,1,0:T(8,128)(2,1)} async-done(((bf16[16,8,640]{2,1,0:T(8,128)(2,1)}), bf16[16,8,640]{2,1,0:T(8,128)(2,1)}, u32[]{:S(2)}, u32[]{:S(2)}) %all-to-all-start) | async-done | bytes 163872 | tf_op jit(solution)/shard_map/all_to_all | solution.py:791
  17.5 4.5 %shard_map.186.after_any = bf16[128,896]{1,0:T(8,128)(2,1)} custom-call(bf16[128,640]{1,0:T(8,128)(2,1)} %bitcast.9.recv_any, bf16[4,256,256]{2,1,0:T(8,128)(2,1)} %get-tuple-element.15.key_any, bf16[4,256,256]{2,1,0:T(8,128)(2,1)} %get-tuple-element.16.value_any, s32[128,128]{1,0:T(8,128)} %get-tuple-element.17.code_any, ...), custom_call_target="tpu_custom_call" | custom-call | flops 134217728 | bytes 4194304 | tf_op jit(solution)/shard_map/pallas_call | solution.py:841
  22.1 4.1 %all-to-all-start.1 = ((bf16[16,8,896]{2,1,0:T(8,128)(2,1)}), bf16[16,8,896]{2,1,0:T(8,128)(2,1)}, u32[]{:S(2)}, u32[]{:S(2)}) async-start(bf16[16,8,896]{2,1,0:T(8,128)(2,1)} %bitcast.14), calls=%async_computation.1 | async-start | bytes 458752 | tf_op jit(solution)/shard_map/all_to_all | solution.py:850
  26.2 6.9 %shard_map.187 = (bf16[8,512,256]{2,1,0:T(8,128)(2,1)}, f32[8,64,128]{2,1,0:T(8,128)}, f32[8,64,128]{2,1,0:T(8,128)}, f32[8,8192]{1,0:T(8,128)}, f32[8,8192]{1,0:T(8,128)}) custom-call(f32[128]{0:T(128)} %rate_any.3, f32[128]{0:T(128)} %skip_any.3, s32[8]{0:T(128)} %len_any.3, bf16[8,8,256]{2,1,0:T(8,128)(2,1)} %dt_any.3, ...), custom_call_target="tpu_custom_call", output_to_operand_aliasing={{0}: (16, {})} | custom-call | flops 2013265920 | bytes 8388608 | tf_op jit(solution)/shard_map/pallas_call | solution.py:857
  33.0 1.5 %all-to-all-done.1.back_any = bf16[16,8,896]{2,1,0:T(8,128)(2,1)} async-done(((bf16[16,8,896]{2,1,0:T(8,128)(2,1)}), bf16[16,8,896]{2,1,0:T(8,128)(2,1)}, u32[]{:S(2)}, u32[]{:S(2)}) %all-to-all-start.1) | async-done | bytes 229408 | tf_op jit(solution)/shard_map/all_to_all | solution.py:850
  34.6 2.3 %shard_map.188 = (bf16[3,2,8192]{2,1,0:T(2,128)(2,1)}, bf16[3,2,8192]{2,1,0:T(2,128)(2,1)}) custom-call(bf16[16,8,896]{2,1,0:T(8,128)(2,1)} %all-to-all-done.1.back_any, f32[8,64,128]{2,1,0:T(8,128)} %get-tuple-element.21.own_any, f32[8,64,128]{2,1,0:T(8,128)} %get-tuple-element.22.ownsum_any, f32[8,8192]{1,0:T(8,128)} %get-tuple-element.23.fade_any, ...), custom_call_target="tpu_custom_call" | custom-call | bytes 2097152 | tf_op jit(solution)/shard_map/pallas_call | solution.py:918
Async XLA Ops:
  0.6 9.8 %collective-permute-start = (bf16[64,16,256]{2,1,0:T(8,128)(2,1)}, bf16[64,16,256]{2,1,0:T(8,128)(2,1)}, u32[]{:S(2)}, u32[]{:S(2)}) collective-permute-start(bf16[64,16,256]{2,1,0:T(8,128)(2,1)} %pages_any.1), channel_id=1, source_target_pairs={{0,1},{1,0},{2,3},{3,2},{4,5},{5,4},{6,7},{7,6},{8,9},{9,8},{10,11... | collective-permute-start | bytes 1572872 | tf_op jit(solution)/shard_map/ppermute | solution.py:774
  2.8 14.7 %all-to-all-start = ((bf16[16,8,640]{2,1,0:T(8,128)(2,1)}), bf16[16,8,640]{2,1,0:T(8,128)(2,1)}, u32[]{:S(2)}, u32[]{:S(2)}) async-start(bf16[16,8,640]{2,1,0:T(8,128)(2,1)} %bitcast.15), calls=%async_computation | async-start | bytes 327680 | tf_op jit(solution)/shard_map/all_to_all | solution.py:791
  22.1 12.5 %all-to-all-start.1 = ((bf16[16,8,896]{2,1,0:T(8,128)(2,1)}), bf16[16,8,896]{2,1,0:T(8,128)(2,1)}, u32[]{:S(2)}, u32[]{:S(2)}) async-start(bf16[16,8,896]{2,1,0:T(8,128)(2,1)} %bitcast.14), calls=%async_computation.1 | async-start | bytes 458752 | tf_op jit(solution)/shard_map/all_to_all | solution.py:850

commit v12 on v11

--- a/solution.py
+++ b/solution.py
@@ -38,8 +38,8 @@
 
 
 def exchange_order(owners):
-    middle = owners // 4
-    return [middle] + [d for d in reversed(range(owners)) if d != middle]
+    first = owners * 5 // 8
+    return [first] + [d for d in range(owners) if d != first]
 
 
 def dot_nt(left, right):
@@ -568,6 +568,8 @@
     key = iota((count, SUB), 1)
     seen = (key % rows == pair % rows) & (key <= pair) & (key < rows * steps)
     seen = seen | ((pair >= rows * steps) & (key == 0))
+    lane = iota((count, LANES), 1)
+    sums = jnp.zeros((count, LANES), f32)
     for v in range(KVH):
         halves = [send_ref[order.index(v * ways + n), :, :HALF].astype(f32) for n in range(2)]
         parts = [half[:, g * HD : (g + 1) * HD] for g in range(HALF // HD) for half in halves]
@@ -579,8 +581,9 @@
         weight = jnp.exp2(scores - highest)
         total = jnp.sum(weight, axis=1, keepdims=True)
         weight = (weight / total).astype(bf16)
-        own_ref[v] = jnp.dot(weight, values, preferred_element_type=f32)
-        ownsum_ref[v] = jnp.broadcast_to(highest + jnp.log2(total), (count, HD))
+        own_ref[v] = jnp.dot(weight, values, preferred_element_type=f32).astype(bf16)
+        sums = jnp.where(lane == v, highest + jnp.log2(total), sums)
+    ownsum_ref[...] = sums
 
 
 def own_mixer(rates_ref, skips_ref, sx_ref, sb_ref, sc_ref, sdt_ref, c_rows, x_rows, fade_ref, local_ref):
@@ -657,7 +660,7 @@
     sems,
 ):
     copies = fetches([(back_any, back_ref), (fade_any, fade_ref), (local_any, local_ref)], sems)
-    rest = fetches([(own_any, own_ref), (ownsum_any, ownsum_ref)], sems, len(copies))
+    copies += fetches([(own_any, own_ref), (ownsum_any, ownsum_ref)], sems, len(copies))
     for copy in copies:
         copy.wait()
     owners = back_ref.shape[0]
@@ -675,9 +678,6 @@
         mixed[:, columns] = found * fade_ref[:, columns] + local_ref[:, columns]
     for k in range(steps):
         mixer_ref[k] = mixed[k * rows : (k + 1) * rows, :].astype(bf16)
-    outs = fetches([(mixer_ref, mixer_any)], sems)
-    for copy in rest:
-        copy.wait()
     lane = iota((2, SUB, LANES), 2)
     mine = (lane // 16 == iota((2, SUB, LANES), 1)) & (lane % 16 < 12)
     for v in range(KVH):
@@ -689,7 +689,7 @@
             pieces.append(jnp.where(mine, jnp.broadcast_to(packed, (2, SUB, LANES)), 0.0))
         for g in range(HALF // HD):
             part = slice(g * 2 * SUB, (g + 1) * 2 * SUB)
-            own_sum = ownsum_ref[v, part, :]
+            own_sum = jnp.broadcast_to(ownsum_ref[part, v : v + 1], (2 * SUB, HD))
             wide = []
             for piece in pieces:
                 one = jnp.sum(jnp.where(lane % 4 == g, piece, 0.0), axis=-1, keepdims=True)
@@ -697,7 +697,7 @@
             highest = functools.reduce(jnp.maximum, wide, own_sum)
             weight = jnp.exp2(own_sum - highest)
             total = weight
-            value = weight * own_ref[v, part, :]
+            value = weight * own_ref[v, part, :].astype(f32)
             for one, block in zip(wide, blocks):
                 weight = jnp.exp2(one - highest)
                 total = total + weight
@@ -708,8 +708,7 @@
             attended[:, start + HALF : start + HALF + HD] = value[SUB:]
     for k in range(steps):
         attention_ref[k] = attended[k * rows : (k + 1) * rows, :].astype(bf16)
-    outs += fetches([(attention_ref, attention_any)], sems, 1)
-    for copy in outs:
+    for copy in fetches([(mixer_ref, mixer_any), (attention_ref, attention_any)], sems):
         copy.wait()
 
 
@@ -858,8 +857,8 @@
         prompt_kernel,
         (
             shape(prompt_x.shape, bf16),
-            shape((KVH, count, HD), f32),
-            shape((KVH, count, HD), f32),
+            shape((KVH, count, HD), bf16),
+            shape((count, LANES), f32),
             shape((SUB, channels), f32),
             shape((SUB, channels), f32),
         ),
@@ -868,8 +867,8 @@
         block
         + tables
         + [
-            vmem((KVH, count, HD), f32),
-            vmem((KVH, count, HD), f32),
+            vmem((KVH, count, HD), bf16),
+            vmem((count, LANES), f32),
             vmem((SUB, channels), f32),
             vmem((SUB, channels), f32),
             vmem((SUB, fresh_cache.shape[2]), f32),

time: 37.3 us -> 37.3 us (level)
  waiting for transfers between devices: 3.36 us -> 0.01 us
  starting transfers between devices: 12.2 us -> 15.4 us
    all_to_all x1, starting transfers between devices: 4.08 us -> 6.38 us  [on_device(): lax.all_to_all(back, 'heads', split_axis=0, concat_axis=0, tiled=True, ax...]
    all_to_all x1, waiting for transfers between devices: 1.82 us -> 0.01 us  [on_device(): lax.all_to_all(send, 'heads', split_axis=0, concat_axis=0, tiled=True, ax...]
    all_to_all x1, waiting for transfers between devices: 1.54 us -> 0.01 us  [on_device(): lax.all_to_all(back, 'heads', split_axis=0, concat_axis=0, tiled=True, ax...]
    all_to_all x1, starting transfers between devices: 7.57 us -> 8.47 us  [on_device(): lax.all_to_all(send, 'heads', split_axis=0, concat_axis=0, tiled=True, ax...]
  transfers between devices with their start and end apart: 3 -> 3, of which waited for: 2 -> 0; matrix products, arithmetic and copies ran while one was open for 0% -> 0% of each run, Pallas kernels for 38% -> 38%
where the time goes in v12:
time: 37.3 us; the launch traced here: 36.9 us
  Pallas kernels  20.8 us (56%)
  starting transfers between devices  15.4 us (41%)
  between operations  0.68 us (2%)
    all_to_all x1, starting transfers between devices, on_device(): lax.all_to_all(send, 'heads', split_axis=0, concat_axis=0, tiled=True, ax...  8.47 us
    pallas_call x1, Pallas kernels, on_device(): call(prompt_kernel, (shape(prompt_x.shape, bf16), shape((KVH, count, HD),...  6.89 us
    all_to_all x1, starting transfers between devices, on_device(): lax.all_to_all(back, 'heads', split_axis=0, concat_axis=0, tiled=True, ax...  6.38 us
    pallas_call x1, Pallas kernels, on_device(): call(state_kernel, (shape((prompts, width, NS), bf16), shape((prompts //...  5.29 us
    pallas_call x1, Pallas kernels, on_device(): call(serve_kernel, shape((all_rows, HALF + max(LANES, width) - LANES), bf...  4.54 us
    pallas_call x1, Pallas kernels, on_device(): call(functools.partial(merge_kernel, width), (shape(step_x.shape, bf16),...  2.42 us
    pallas_call x1, Pallas kernels, on_device(): call(functools.partial(pack_kernel, group, ways), shape((all_rows, HALF +...  1.68 us
  transfers between devices with their start and end apart: 3, of which 0 were waited for; matrix products, arithmetic and copies ran while one was open for 0% of the time, Pallas kernels for 38%

profile of v12, /device:TPU:0, one launch (start us, length us, event | category | flops | bytes accessed | tf_op | source)
XLA Modules:
  0.0 36.9 jit_solution(9908441543210720417)
XLA Ops:
  0.6 0.5 %collective-permute-start = (bf16[64,16,256]{2,1,0:T(8,128)(2,1)}, bf16[64,16,256]{2,1,0:T(8,128)(2,1)}, u32[]{:S(2)}, u32[]{:S(2)}) collective-permute-start(bf16[64,16,256]{2,1,0:T(8,128)(2,1)} %pages_any.1), channel_id=1, source_target_pairs={{0,1},{1,0},{2,3},{3,2},{4,5},{5,4},{6,7},{7,6},{8,9},{9,8},{10,11... | collective-permute-start | bytes 1572872 | tf_op jit(solution)/shard_map/ppermute | solution.py:773
  1.1 1.7 %shard_map.184 = bf16[128,640]{1,0:T(8,128)(2,1)} custom-call(bf16[3,2,8192]{2,1,0:T(2,128)(2,1)} %bitcast.18, bf16[3,2,1024]{2,1,0:T(2,128)(2,1)} %bitcast.19), custom_call_target="tpu_custom_call" | custom-call | bytes 524288 | tf_op jit(solution)/shard_map/pallas_call | solution.py:774
  2.8 8.5 %all-to-all-start = ((bf16[16,8,640]{2,1,0:T(8,128)(2,1)}), bf16[16,8,640]{2,1,0:T(8,128)(2,1)}, u32[]{:S(2)}, u32[]{:S(2)}) async-start(bf16[16,8,640]{2,1,0:T(8,128)(2,1)} %bitcast.15), calls=%async_computation | async-start | bytes 327680 | tf_op jit(solution)/shard_map/all_to_all | solution.py:790
  11.3 0.0 collective-permute-done.other_any
  11.3 5.3 %shard_map.185 = (bf16[8,512,256]{2,1,0:T(8,128)(2,1)}, bf16[4,256,256]{2,1,0:T(8,128)(2,1)}, bf16[4,256,256]{2,1,0:T(8,128)(2,1)}, s32[128,128]{1,0:T(8,128)}, bf16[8,512,256]{2,1,0:T(8,128)(2,1)}) custom-call(f32[128]{0:T(128)} %rate_any.3, f32[128]{0:T(128)} %skip_any.3, s32[8]{0:T(128)} %len_any.3, s32[2,16]{1,0:T(2,128)} %bitcast.26, ...), custom_call_target="tpu_custom_call" | custom-call | flops 1207959552 | bytes 6291456 | tf_op jit(solution)/shard_map/pallas_call | solution.py:805
  16.6 0.0 all-to-all-done
  16.6 4.5 %shard_map.186.after_any = bf16[128,896]{1,0:T(8,128)(2,1)} custom-call(bf16[128,640]{1,0:T(8,128)(2,1)} %bitcast.9.recv_any, bf16[4,256,256]{2,1,0:T(8,128)(2,1)} %get-tuple-element.15.key_any, bf16[4,256,256]{2,1,0:T(8,128)(2,1)} %get-tuple-element.16.value_any, s32[128,128]{1,0:T(8,128)} %get-tuple-element.17.code_any, ...), custom_call_target="tpu_custom_call" | custom-call | flops 134217728 | bytes 4194304 | tf_op jit(solution)/shard_map/pallas_call | solution.py:840
  21.2 6.4 %all-to-all-start.1 = ((bf16[16,8,896]{2,1,0:T(8,128)(2,1)}), bf16[16,8,896]{2,1,0:T(8,128)(2,1)}, u32[]{:S(2)}, u32[]{:S(2)}) async-start(bf16[16,8,896]{2,1,0:T(8,128)(2,1)} %bitcast.14), calls=%async_computation.1 | async-start | bytes 458752 | tf_op jit(solution)/shard_map/all_to_all | solution.py:849
  27.5 6.9 %shard_map.187 = (bf16[8,512,256]{2,1,0:T(8,128)(2,1)}, bf16[8,64,128]{2,1,0:T(8,128)(2,1)}, f32[64,128]{1,0:T(8,128)}, f32[8,8192]{1,0:T(8,128)}, f32[8,8192]{1,0:T(8,128)}) custom-call(f32[128]{0:T(128)} %rate_any.3, f32[128]{0:T(128)} %skip_any.3, s32[8]{0:T(128)} %len_any.3, bf16[8,8,256]{2,1,0:T(8,128)(2,1)} %dt_any.3, ...), custom_call_target="tpu_custom_call", output_to_operand_aliasing={{0}: (16, {})} | custom-call | flops 2013265920 | bytes 8388608 | tf_op jit(solution)/shard_map/pallas_call | solution.py:856
  34.4 0.0 all-to-all-done.1.back_any
  34.4 2.4 %shard_map.188 = (bf16[3,2,8192]{2,1,0:T(2,128)(2,1)}, bf16[3,2,8192]{2,1,0:T(2,128)(2,1)}) custom-call(bf16[16,8,896]{2,1,0:T(8,128)(2,1)} %all-to-all-done.1.back_any, bf16[8,64,128]{2,1,0:T(8,128)(2,1)} %get-tuple-element.21.own_any, f32[64,128]{1,0:T(8,128)} %get-tuple-element.22.ownsum_any, f32[8,8192]{1,0:T(8,128)} %get-tuple-element.23.fade_any, ...), custom_call_target="tpu_custom_call" | custom-call | bytes 2097152 | tf_op jit(solution)/shard_map/pallas_call | solution.py:917
Async XLA Ops:
  0.6 10.7 %collective-permute-start = (bf16[64,16,256]{2,1,0:T(8,128)(2,1)}, bf16[64,16,256]{2,1,0:T(8,128)(2,1)}, u32[]{:S(2)}, u32[]{:S(2)}) collective-permute-start(bf16[64,16,256]{2,1,0:T(8,128)(2,1)} %pages_any.1), channel_id=1, source_target_pairs={{0,1},{1,0},{2,3},{3,2},{4,5},{5,4},{6,7},{7,6},{8,9},{9,8},{10,11... | collective-permute-start | bytes 1572872 | tf_op jit(solution)/shard_map/ppermute | solution.py:773
  2.8 13.8 %all-to-all-start = ((bf16[16,8,640]{2,1,0:T(8,128)(2,1)}), bf16[16,8,640]{2,1,0:T(8,128)(2,1)}, u32[]{:S(2)}, u32[]{:S(2)}) async-start(bf16[16,8,640]{2,1,0:T(8,128)(2,1)} %bitcast.15), calls=%async_computation | async-start | bytes 327680 | tf_op jit(solution)/shard_map/all_to_all | solution.py:790
  21.2 13.3 %all-to-all-start.1 = ((bf16[16,8,896]{2,1,0:T(8,128)(2,1)}), bf16[16,8,896]{2,1,0:T(8,128)(2,1)}, u32[]{:S(2)}, u32[]{:S(2)}) async-start(bf16[16,8,896]{2,1,0:T(8,128)(2,1)} %bitcast.14), calls=%async_computation.1 | async-start | bytes 458752 | tf_op jit(solution)/shard_map/all_to_all | solution.py:849

commit v13 on v12

--- a/solution.py
+++ b/solution.py
@@ -16,6 +16,7 @@
 PAGE = 16
 PAGES = 16
 LANES = 128
+ROWS16 = 16
 SUB = 8
 HALF = 512
 LEVELS = (128, 64, 32, 16)
@@ -112,7 +113,7 @@
         signs[len(LEVELS)] = jnp.where(j > i, 1.0, 0.0).astype(bf16)
 
 
-def head_factors(first, dt_ref, rate_ref, skip_ref, len_ref, signs, w_in, w_out, w_skip, w_tail):
+def head_factors(first, some, dt_ref, rate_ref, skip_ref, len_ref, signs, w_in, w_out, w_skip, w_tail):
     group, prompts, length = dt_ref.shape
     row = iota((prompts, length), 0)
     lens = jnp.zeros((prompts, length), jnp.int32)
@@ -137,7 +138,9 @@
                 up, down = jnp.exp2(gap), jnp.exp2(-gap)
             else:
                 up, down = jnp.exp2(jnp.minimum(gap, 0.0)), jnp.exp2(-jnp.maximum(gap, 0.0))
-            w_in[l, :, h, :] = up * moved[h]
+            enter = up * moved[h]
+            for r in some:
+                w_in[l, r, h] = jnp.broadcast_to(enter[r : r + 1], w_in.shape[3:]).astype(bf16)
             w_out[l, :, h, :] = jnp.where(valid, down, 0.0)
 
 
@@ -158,17 +161,19 @@
     width, length = x_held.shape[1], x_held.shape[2]
     group = width // HP
     half = length // 2
-    inputs = x_held[r].astype(f32).reshape(group, HP, length)
+    given = x_held[r]
+    inputs = given.astype(f32).reshape(group, HP, length)
+    given = given.reshape(group, HP // ROWS16, ROWS16, length)
     scores = dot_nt(b_held[r], c_held[r]).astype(bf16)
     total = inputs * w_skip[r][:, None, :]
     left, right = total[..., :half], total[..., half:]
     for l, n in enumerate(LEVELS):
         if 2 * n == length:
-            scaled = (inputs[..., :half] * w_in[l, r][:, None, :half]).astype(bf16).reshape(width, half)
+            scaled = (given[..., :half] * w_in[l, r][:, None, :, :half]).reshape(width, half)
             added = jnp.dot(scaled, scores[:half, half:], preferred_element_type=f32)
             right = right + added.reshape(group, HP, half) * w_out[l, r][:, None, half:]
         else:
-            scaled = (inputs * w_in[l, r][:, None, :]).astype(bf16).reshape(width, length)
+            scaled = (given * w_in[l, r][:, None]).reshape(width, length)
             added = jnp.dot(scaled, scores * masks[l], preferred_element_type=f32)
             added = added.reshape(group, HP, length) * w_out[l, r][:, None, :]
             left = left + added[..., :half]
@@ -269,7 +274,9 @@
     level_masks(masks)
     for copy in smalls:
         copy.wait()
-    head_factors(first, dt_ref, rate_ref, skip_ref, len_ref, signs, w_in, w_out, w_skip, w_tail)
+    head_factors(
+        first, range(EARLY), dt_ref, rate_ref, skip_ref, len_ref, signs, w_in, w_out, w_skip, w_tail
+    )
 
     width = x_held.shape[1]
     for begin in range(0, prompts, prompts // 2):
@@ -525,7 +532,9 @@
     level_masks(masks)
     for copy in smalls:
         copy.wait()
-    head_factors(first, dt_ref, rate_ref, skip_ref, len_ref, signs, w_in, w_out, w_skip, None)
+    head_factors(
+        first, range(EARLY, prompts), dt_ref, rate_ref, skip_ref, len_ref, signs, w_in, w_out, w_skip, None
+    )
     own_attention(send_ref, fresh_ref, fresh_held, own_ref, ownsum_ref)
     own_mixer(rates_ref, skips_ref, sx_ref, sb_ref, sc_ref, sdt_ref, c_rows, x_rows, fade_ref, local_ref)
     outs = fetches(
@@ -660,7 +669,7 @@
     sems,
 ):
     copies = fetches([(back_any, back_ref), (fade_any, fade_ref), (local_any, local_ref)], sems)
-    copies += fetches([(own_any, own_ref), (ownsum_any, ownsum_ref)], sems, len(copies))
+    rest = fetches([(own_any, own_ref), (ownsum_any, ownsum_ref)], sems, len(copies))
     for copy in copies:
         copy.wait()
     owners = back_ref.shape[0]
@@ -678,6 +687,9 @@
         mixed[:, columns] = found * fade_ref[:, columns] + local_ref[:, columns]
     for k in range(steps):
         mixer_ref[k] = mixed[k * rows : (k + 1) * rows, :].astype(bf16)
+    outs = fetches([(mixer_ref, mixer_any)], sems)
+    for copy in rest:
+        copy.wait()
     lane = iota((2, SUB, LANES), 2)
     mine = (lane // 16 == iota((2, SUB, LANES), 1)) & (lane % 16 < 12)
     for v in range(KVH):
@@ -708,7 +720,8 @@
             attended[:, start + HALF : start + HALF + HD] = value[SUB:]
     for k in range(steps):
         attention_ref[k] = attended[k * rows : (k + 1) * rows, :].astype(bf16)
-    for copy in fetches([(mixer_ref, mixer_any), (attention_ref, attention_any)], sems):
+    outs += fetches([(attention_ref, attention_any)], sems, 1)
+    for copy in outs:
         copy.wait()
 
 
@@ -796,7 +809,7 @@
         vmem((prompts, length, NS), bf16),
         vmem((prompts, length, NS), bf16),
         vmem((prompts, width, length), bf16),
-        vmem((levels, prompts, group, length), f32),
+        vmem((levels, prompts, group, ROWS16, length), bf16),
         vmem((levels, prompts, group, length), f32),
         vmem((prompts, group, length), f32),
     ]

time: 37.3 us -> 37.3 us (level)
  no operation moved by 1% of the time
where the time goes in v13:
time: 37.3 us; the launch traced here: 36.8 us
  Pallas kernels  20.8 us (56%)
  starting transfers between devices  15.4 us (41%)
  between operations  0.68 us (2%)
    all_to_all x1, starting transfers between devices, on_device(): lax.all_to_all(send, 'heads', split_axis=0, concat_axis=0, tiled=True, ax...  8.47 us
    pallas_call x1, Pallas kernels, on_device(): call(prompt_kernel, (shape(prompt_x.shape, bf16), shape((KVH, count, HD),...  6.88 us
    all_to_all x1, starting transfers between devices, on_device(): lax.all_to_all(back, 'heads', split_axis=0, concat_axis=0, tiled=True, ax...  6.38 us
    pallas_call x1, Pallas kernels, on_device(): call(state_kernel, (shape((prompts, width, NS), bf16), shape((prompts //...  5.28 us
    pallas_call x1, Pallas kernels, on_device(): call(serve_kernel, shape((all_rows, HALF + max(LANES, width) - LANES), bf...  4.54 us
    pallas_call x1, Pallas kernels, on_device(): call(functools.partial(merge_kernel, width), (shape(step_x.shape, bf16),...  2.41 us
    pallas_call x1, Pallas kernels, on_device(): call(functools.partial(pack_kernel, group, ways), shape((all_rows, HALF +...  1.68 us
  transfers between devices with their start and end apart: 3, of which 0 were waited for; matrix products, arithmetic and copies ran while one was open for 0% of the time, Pallas kernels for 38%

profile of v13, /device:TPU:0, one launch (start us, length us, event | category | flops | bytes accessed | tf_op | source)
XLA Modules:
  0.0 36.8 jit_solution(17048286059678847876)
XLA Ops:
  0.6 0.5 %collective-permute-start = (bf16[64,16,256]{2,1,0:T(8,128)(2,1)}, bf16[64,16,256]{2,1,0:T(8,128)(2,1)}, u32[]{:S(2)}, u32[]{:S(2)}) collective-permute-start(bf16[64,16,256]{2,1,0:T(8,128)(2,1)} %pages_any.1), channel_id=1, source_target_pairs={{0,1},{1,0},{2,3},{3,2},{4,5},{5,4},{6,7},{7,6},{8,9},{9,8},{10,11... | collective-permute-start | bytes 1572872 | tf_op jit(solution)/shard_map/ppermute | solution.py:786
  1.1 1.7 %shard_map.184 = bf16[128,640]{1,0:T(8,128)(2,1)} custom-call(bf16[3,2,8192]{2,1,0:T(2,128)(2,1)} %bitcast.18, bf16[3,2,1024]{2,1,0:T(2,128)(2,1)} %bitcast.19), custom_call_target="tpu_custom_call" | custom-call | bytes 524288 | tf_op jit(solution)/shard_map/pallas_call | solution.py:787
  2.8 8.5 %all-to-all-start = ((bf16[16,8,640]{2,1,0:T(8,128)(2,1)}), bf16[16,8,640]{2,1,0:T(8,128)(2,1)}, u32[]{:S(2)}, u32[]{:S(2)}) async-start(bf16[16,8,640]{2,1,0:T(8,128)(2,1)} %bitcast.15), calls=%async_computation | async-start | bytes 327680 | tf_op jit(solution)/shard_map/all_to_all | solution.py:803
  11.3 0.0 collective-permute-done.other_any
  11.3 5.3 %shard_map.185 = (bf16[8,512,256]{2,1,0:T(8,128)(2,1)}, bf16[4,256,256]{2,1,0:T(8,128)(2,1)}, bf16[4,256,256]{2,1,0:T(8,128)(2,1)}, s32[128,128]{1,0:T(8,128)}, bf16[8,512,256]{2,1,0:T(8,128)(2,1)}) custom-call(f32[128]{0:T(128)} %rate_any.3, f32[128]{0:T(128)} %skip_any.3, s32[8]{0:T(128)} %len_any.3, s32[2,16]{1,0:T(2,128)} %bitcast.26, ...), custom_call_target="tpu_custom_call" | custom-call | flops 1207959552 | bytes 6291456 | tf_op jit(solution)/shard_map/pallas_call | solution.py:818
  16.6 0.0 all-to-all-done
  16.6 4.5 %shard_map.186.after_any = bf16[128,896]{1,0:T(8,128)(2,1)} custom-call(bf16[128,640]{1,0:T(8,128)(2,1)} %bitcast.9.recv_any, bf16[4,256,256]{2,1,0:T(8,128)(2,1)} %get-tuple-element.15.key_any, bf16[4,256,256]{2,1,0:T(8,128)(2,1)} %get-tuple-element.16.value_any, s32[128,128]{1,0:T(8,128)} %get-tuple-element.17.code_any, ...), custom_call_target="tpu_custom_call" | custom-call | flops 134217728 | bytes 4194304 | tf_op jit(solution)/shard_map/pallas_call | solution.py:853
  21.2 6.4 %all-to-all-start.1 = ((bf16[16,8,896]{2,1,0:T(8,128)(2,1)}), bf16[16,8,896]{2,1,0:T(8,128)(2,1)}, u32[]{:S(2)}, u32[]{:S(2)}) async-start(bf16[16,8,896]{2,1,0:T(8,128)(2,1)} %bitcast.14), calls=%async_computation.1 | async-start | bytes 458752 | tf_op jit(solution)/shard_map/all_to_all | solution.py:862
  27.5 6.9 %shard_map.187 = (bf16[8,512,256]{2,1,0:T(8,128)(2,1)}, bf16[8,64,128]{2,1,0:T(8,128)(2,1)}, f32[64,128]{1,0:T(8,128)}, f32[8,8192]{1,0:T(8,128)}, f32[8,8192]{1,0:T(8,128)}) custom-call(f32[128]{0:T(128)} %rate_any.3, f32[128]{0:T(128)} %skip_any.3, s32[8]{0:T(128)} %len_any.3, bf16[8,8,256]{2,1,0:T(8,128)(2,1)} %dt_any.3, ...), custom_call_target="tpu_custom_call", output_to_operand_aliasing={{0}: (16, {})} | custom-call | flops 2013265920 | bytes 8388608 | tf_op jit(solution)/shard_map/pallas_call | solution.py:869
  34.4 0.0 all-to-all-done.1.back_any
  34.4 2.4 %shard_map.188 = (bf16[3,2,8192]{2,1,0:T(2,128)(2,1)}, bf16[3,2,8192]{2,1,0:T(2,128)(2,1)}) custom-call(bf16[16,8,896]{2,1,0:T(8,128)(2,1)} %all-to-all-done.1.back_any, bf16[8,64,128]{2,1,0:T(8,128)(2,1)} %get-tuple-element.21.own_any, f32[64,128]{1,0:T(8,128)} %get-tuple-element.22.ownsum_any, f32[8,8192]{1,0:T(8,128)} %get-tuple-element.23.fade_any, ...), custom_call_target="tpu_custom_call" | custom-call | bytes 2097152 | tf_op jit(solution)/shard_map/pallas_call | solution.py:930
Async XLA Ops:
  0.6 10.7 %collective-permute-start = (bf16[64,16,256]{2,1,0:T(8,128)(2,1)}, bf16[64,16,256]{2,1,0:T(8,128)(2,1)}, u32[]{:S(2)}, u32[]{:S(2)}) collective-permute-start(bf16[64,16,256]{2,1,0:T(8,128)(2,1)} %pages_any.1), channel_id=1, source_target_pairs={{0,1},{1,0},{2,3},{3,2},{4,5},{5,4},{6,7},{7,6},{8,9},{9,8},{10,11... | collective-permute-start | bytes 1572872 | tf_op jit(solution)/shard_map/ppermute | solution.py:786
  2.8 13.8 %all-to-all-start = ((bf16[16,8,640]{2,1,0:T(8,128)(2,1)}), bf16[16,8,640]{2,1,0:T(8,128)(2,1)}, u32[]{:S(2)}, u32[]{:S(2)}) async-start(bf16[16,8,640]{2,1,0:T(8,128)(2,1)} %bitcast.15), calls=%async_computation | async-start | bytes 327680 | tf_op jit(solution)/shard_map/all_to_all | solution.py:803
  21.2 13.3 %all-to-all-start.1 = ((bf16[16,8,896]{2,1,0:T(8,128)(2,1)}), bf16[16,8,896]{2,1,0:T(8,128)(2,1)}, u32[]{:S(2)}, u32[]{:S(2)}) async-start(bf16[16,8,896]{2,1,0:T(8,128)(2,1)} %bitcast.14), calls=%async_computation.1 | async-start | bytes 458752 | tf_op jit(solution)/shard_map/all_to_all | solution.py:862

commit v14 on v11

--- a/solution.py
+++ b/solution.py
@@ -38,8 +38,8 @@
 
 
 def exchange_order(owners):
-    middle = owners // 4
-    return [middle] + [d for d in reversed(range(owners)) if d != middle]
+    first = owners // 2
+    return [first] + [d for d in range(owners) if d != first]
 
 
 def dot_nt(left, right):

time: 37.3 us -> 36.5 us (0.979)
  waiting for transfers between devices: 3.36 us -> 0.99 us
  starting transfers between devices: 12.2 us -> 13.7 us
    all_to_all x1, starting transfers between devices: 4.08 us -> 5.69 us  [on_device(): lax.all_to_all(back, 'heads', split_axis=0, concat_axis=0, tiled=True, ax...]
    all_to_all x1, waiting for transfers between devices: 1.82 us -> 0.59 us  [on_device(): lax.all_to_all(send, 'heads', split_axis=0, concat_axis=0, tiled=True, ax...]
    all_to_all x1, waiting for transfers between devices: 1.54 us -> 0.41 us  [on_device(): lax.all_to_all(back, 'heads', split_axis=0, concat_axis=0, tiled=True, ax...]
where the time goes in v14:
time: 36.5 us; the launch traced here: 36 us
  Pallas kernels  20.6 us (56%)
  starting transfers between devices  13.7 us (38%)
  waiting for transfers between devices  0.99 us (3%)
  between operations  0.67 us (2%)
    all_to_all x1, starting transfers between devices, on_device(): lax.all_to_all(send, 'heads', split_axis=0, concat_axis=0, tiled=True, ax...  7.53 us
    pallas_call x1, Pallas kernels, on_device(): call(prompt_kernel, (shape(prompt_x.shape, bf16), shape((KVH, count, HD),...  6.87 us
    all_to_all x1, starting transfers between devices, on_device(): lax.all_to_all(back, 'heads', split_axis=0, concat_axis=0, tiled=True, ax...  5.69 us
    pallas_call x1, Pallas kernels, on_device(): call(state_kernel, (shape((prompts, width, NS), bf16), shape((prompts //...  5.29 us
    pallas_call x1, Pallas kernels, on_device(): call(serve_kernel, shape((all_rows, HALF + max(LANES, width) - LANES), bf...  4.53 us
    pallas_call x1, Pallas kernels, on_device(): call(functools.partial(merge_kernel, width), (shape(step_x.shape, bf16),...  2.26 us
    pallas_call x1, Pallas kernels, on_device(): call(functools.partial(pack_kernel, group, ways), shape((all_rows, HALF +...  1.68 us
  transfers between devices with their start and end apart: 3, of which 2 were waited for; matrix products, arithmetic and copies ran while one was open for 0% of the time, Pallas kernels for 38%

profile of v14, /device:TPU:0, one launch (start us, length us, event | category | flops | bytes accessed | tf_op | source)
XLA Modules:
  0.0 36.0 jit_solution(162890990888141161)
XLA Ops:
  0.6 0.5 %collective-permute-start = (bf16[64,16,256]{2,1,0:T(8,128)(2,1)}, bf16[64,16,256]{2,1,0:T(8,128)(2,1)}, u32[]{:S(2)}, u32[]{:S(2)}) collective-permute-start(bf16[64,16,256]{2,1,0:T(8,128)(2,1)} %pages_any.1), channel_id=1, source_target_pairs={{0,1},{1,0},{2,3},{3,2},{4,5},{5,4},{6,7},{7,6},{8,9},{9,8},{10,11... | collective-permute-start | bytes 1572872 | tf_op jit(solution)/shard_map/ppermute | solution.py:774
  1.1 1.7 %shard_map.184 = bf16[128,640]{1,0:T(8,128)(2,1)} custom-call(bf16[3,2,8192]{2,1,0:T(2,128)(2,1)} %bitcast.18, bf16[3,2,1024]{2,1,0:T(2,128)(2,1)} %bitcast.19), custom_call_target="tpu_custom_call" | custom-call | bytes 524288 | tf_op jit(solution)/shard_map/pallas_call | solution.py:775
  2.8 7.5 %all-to-all-start = ((bf16[16,8,640]{2,1,0:T(8,128)(2,1)}), bf16[16,8,640]{2,1,0:T(8,128)(2,1)}, u32[]{:S(2)}, u32[]{:S(2)}) async-start(bf16[16,8,640]{2,1,0:T(8,128)(2,1)} %bitcast.15), calls=%async_computation | async-start | bytes 327680 | tf_op jit(solution)/shard_map/all_to_all | solution.py:791
  10.4 0.0 collective-permute-done.other_any
  10.4 5.3 %shard_map.185 = (bf16[8,512,256]{2,1,0:T(8,128)(2,1)}, bf16[4,256,256]{2,1,0:T(8,128)(2,1)}, bf16[4,256,256]{2,1,0:T(8,128)(2,1)}, s32[128,128]{1,0:T(8,128)}, bf16[8,512,256]{2,1,0:T(8,128)(2,1)}) custom-call(f32[128]{0:T(128)} %rate_any.3, f32[128]{0:T(128)} %skip_any.3, s32[8]{0:T(128)} %len_any.3, s32[2,16]{1,0:T(2,128)} %bitcast.26, ...), custom_call_target="tpu_custom_call" | custom-call | flops 1207959552 | bytes 6291456 | tf_op jit(solution)/shard_map/pallas_call | solution.py:806
  15.7 0.6 %all-to-all-done = bf16[16,8,640]{2,1,0:T(8,128)(2,1)} async-done(((bf16[16,8,640]{2,1,0:T(8,128)(2,1)}), bf16[16,8,640]{2,1,0:T(8,128)(2,1)}, u32[]{:S(2)}, u32[]{:S(2)}) %all-to-all-start) | async-done | bytes 163872 | tf_op jit(solution)/shard_map/all_to_all | solution.py:791
  16.3 4.5 %shard_map.186.after_any = bf16[128,896]{1,0:T(8,128)(2,1)} custom-call(bf16[128,640]{1,0:T(8,128)(2,1)} %bitcast.9.recv_any, bf16[4,256,256]{2,1,0:T(8,128)(2,1)} %get-tuple-element.15.key_any, bf16[4,256,256]{2,1,0:T(8,128)(2,1)} %get-tuple-element.16.value_any, s32[128,128]{1,0:T(8,128)} %get-tuple-element.17.code_any, ...), custom_call_target="tpu_custom_call" | custom-call | flops 134217728 | bytes 4194304 | tf_op jit(solution)/shard_map/pallas_call | solution.py:841
  20.8 5.7 %all-to-all-start.1 = ((bf16[16,8,896]{2,1,0:T(8,128)(2,1)}), bf16[16,8,896]{2,1,0:T(8,128)(2,1)}, u32[]{:S(2)}, u32[]{:S(2)}) async-start(bf16[16,8,896]{2,1,0:T(8,128)(2,1)} %bitcast.14), calls=%async_computation.1 | async-start | bytes 458752 | tf_op jit(solution)/shard_map/all_to_all | solution.py:850
  26.5 6.9 %shard_map.187 = (bf16[8,512,256]{2,1,0:T(8,128)(2,1)}, f32[8,64,128]{2,1,0:T(8,128)}, f32[8,64,128]{2,1,0:T(8,128)}, f32[8,8192]{1,0:T(8,128)}, f32[8,8192]{1,0:T(8,128)}) custom-call(f32[128]{0:T(128)} %rate_any.3, f32[128]{0:T(128)} %skip_any.3, s32[8]{0:T(128)} %len_any.3, bf16[8,8,256]{2,1,0:T(8,128)(2,1)} %dt_any.3, ...), custom_call_target="tpu_custom_call", output_to_operand_aliasing={{0}: (16, {})} | custom-call | flops 2013265920 | bytes 8388608 | tf_op jit(solution)/shard_map/pallas_call | solution.py:857
  33.4 0.4 %all-to-all-done.1.back_any = bf16[16,8,896]{2,1,0:T(8,128)(2,1)} async-done(((bf16[16,8,896]{2,1,0:T(8,128)(2,1)}), bf16[16,8,896]{2,1,0:T(8,128)(2,1)}, u32[]{:S(2)}, u32[]{:S(2)}) %all-to-all-start.1) | async-done | bytes 229408 | tf_op jit(solution)/shard_map/all_to_all | solution.py:850
  33.8 2.3 %shard_map.188 = (bf16[3,2,8192]{2,1,0:T(2,128)(2,1)}, bf16[3,2,8192]{2,1,0:T(2,128)(2,1)}) custom-call(bf16[16,8,896]{2,1,0:T(8,128)(2,1)} %all-to-all-done.1.back_any, f32[8,64,128]{2,1,0:T(8,128)} %get-tuple-element.21.own_any, f32[8,64,128]{2,1,0:T(8,128)} %get-tuple-element.22.ownsum_any, f32[8,8192]{1,0:T(8,128)} %get-tuple-element.23.fade_any, ...), custom_call_target="tpu_custom_call" | custom-call | bytes 2097152 | tf_op jit(solution)/shard_map/pallas_call | solution.py:918
Async XLA Ops:
  0.6 9.7 %collective-permute-start = (bf16[64,16,256]{2,1,0:T(8,128)(2,1)}, bf16[64,16,256]{2,1,0:T(8,128)(2,1)}, u32[]{:S(2)}, u32[]{:S(2)}) collective-permute-start(bf16[64,16,256]{2,1,0:T(8,128)(2,1)} %pages_any.1), channel_id=1, source_target_pairs={{0,1},{1,0},{2,3},{3,2},{4,5},{5,4},{6,7},{7,6},{8,9},{9,8},{10,11... | collective-permute-start | bytes 1572872 | tf_op jit(solution)/shard_map/ppermute | solution.py:774
  2.8 13.4 %all-to-all-start = ((bf16[16,8,640]{2,1,0:T(8,128)(2,1)}), bf16[16,8,640]{2,1,0:T(8,128)(2,1)}, u32[]{:S(2)}, u32[]{:S(2)}) async-start(bf16[16,8,640]{2,1,0:T(8,128)(2,1)} %bitcast.15), calls=%async_computation | async-start | bytes 327680 | tf_op jit(solution)/shard_map/all_to_all | solution.py:791
  20.8 13.0 %all-to-all-start.1 = ((bf16[16,8,896]{2,1,0:T(8,128)(2,1)}), bf16[16,8,896]{2,1,0:T(8,128)(2,1)}, u32[]{:S(2)}, u32[]{:S(2)}) async-start(bf16[16,8,896]{2,1,0:T(8,128)(2,1)} %bitcast.14), calls=%async_computation.1 | async-start | bytes 458752 | tf_op jit(solution)/shard_map/all_to_all | solution.py:850

commit v15 on v14

--- a/solution.py
+++ b/solution.py
@@ -75,9 +75,8 @@
 
 def pack_kernel(group, ways, q_any, c_any, out_ref, q_ref, c_ref, q_held, c_held, rest, sems):
     owners = out_ref.shape[0] // SUB
-    for copy in fetches([(q_any, q_ref), (c_any, c_ref)], sems):
-        copy.wait()
-    stack_rows(q_ref, q_held)
+    c_copy, q_copy = fetches([(c_any, c_ref), (q_any, q_ref)], sems)
+    c_copy.wait()
     stack_rows(c_ref, c_held)
     span = 2 * HALF
     slots = spare(HALF // LANES + 1, 0)
@@ -88,6 +87,8 @@
             rest[e, row : row + 1, b * LANES : (b + 1) * LANES] = c_held[
                 pair : pair + 1, e * NS + LANES : (e + 1) * NS
             ]
+    q_copy.wait()
+    stack_rows(q_ref, q_held)
     real = iota((SUB, HALF), 0) < PAIRS
     order = exchange_order(owners)
     for rank in range(0, owners, 2):

time: 36.5 us -> 36.5 us (level)
  no operation moved by 1% of the time
where the time goes in v15:
time: 36.5 us; the launch traced here: 36 us
  Pallas kernels  20.6 us (56%)
  starting transfers between devices  13.7 us (38%)
  waiting for transfers between devices  1 us (3%)
  between operations  0.67 us (2%)
    all_to_all x1, starting transfers between devices, on_device(): lax.all_to_all(send, 'heads', split_axis=0, concat_axis=0, tiled=True, ax...  7.53 us
    pallas_call x1, Pallas kernels, on_device(): call(prompt_kernel, (shape(prompt_x.shape, bf16), shape((KVH, count, HD),...  6.86 us
    all_to_all x1, starting transfers between devices, on_device(): lax.all_to_all(back, 'heads', split_axis=0, concat_axis=0, tiled=True, ax...  5.69 us
    pallas_call x1, Pallas kernels, on_device(): call(state_kernel, (shape((prompts, width, NS), bf16), shape((prompts //...  5.29 us
    pallas_call x1, Pallas kernels, on_device(): call(serve_kernel, shape((all_rows, HALF + max(LANES, width) - LANES), bf...  4.53 us
    pallas_call x1, Pallas kernels, on_device(): call(functools.partial(merge_kernel, width), (shape(step_x.shape, bf16),...  2.26 us
    pallas_call x1, Pallas kernels, on_device(): call(functools.partial(pack_kernel, group, ways), shape((all_rows, HALF +...  1.67 us
  transfers between devices with their start and end apart: 3, of which 2 were waited for; matrix products, arithmetic and copies ran while one was open for 0% of the time, Pallas kernels for 38%

profile of v15, /device:TPU:0, one launch (start us, length us, event | category | flops | bytes accessed | tf_op | source)
XLA Modules:
  0.0 36.0 jit_solution(1393487802089009872)
XLA Ops:
  0.6 0.5 %collective-permute-start = (bf16[64,16,256]{2,1,0:T(8,128)(2,1)}, bf16[64,16,256]{2,1,0:T(8,128)(2,1)}, u32[]{:S(2)}, u32[]{:S(2)}) collective-permute-start(bf16[64,16,256]{2,1,0:T(8,128)(2,1)} %pages_any.1), channel_id=1, source_target_pairs={{0,1},{1,0},{2,3},{3,2},{4,5},{5,4},{6,7},{7,6},{8,9},{9,8},{10,11... | collective-permute-start | bytes 1572872 | tf_op jit(solution)/shard_map/ppermute | solution.py:775
  1.1 1.7 %shard_map.184 = bf16[128,640]{1,0:T(8,128)(2,1)} custom-call(bf16[3,2,8192]{2,1,0:T(2,128)(2,1)} %bitcast.18, bf16[3,2,1024]{2,1,0:T(2,128)(2,1)} %bitcast.19), custom_call_target="tpu_custom_call" | custom-call | bytes 524288 | tf_op jit(solution)/shard_map/pallas_call | solution.py:776
  2.8 7.5 %all-to-all-start = ((bf16[16,8,640]{2,1,0:T(8,128)(2,1)}), bf16[16,8,640]{2,1,0:T(8,128)(2,1)}, u32[]{:S(2)}, u32[]{:S(2)}) async-start(bf16[16,8,640]{2,1,0:T(8,128)(2,1)} %bitcast.15), calls=%async_computation | async-start | bytes 327680 | tf_op jit(solution)/shard_map/all_to_all | solution.py:792
  10.4 0.0 collective-permute-done.other_any
  10.4 5.3 %shard_map.185 = (bf16[8,512,256]{2,1,0:T(8,128)(2,1)}, bf16[4,256,256]{2,1,0:T(8,128)(2,1)}, bf16[4,256,256]{2,1,0:T(8,128)(2,1)}, s32[128,128]{1,0:T(8,128)}, bf16[8,512,256]{2,1,0:T(8,128)(2,1)}) custom-call(f32[128]{0:T(128)} %rate_any.3, f32[128]{0:T(128)} %skip_any.3, s32[8]{0:T(128)} %len_any.3, s32[2,16]{1,0:T(2,128)} %bitcast.26, ...), custom_call_target="tpu_custom_call" | custom-call | flops 1207959552 | bytes 6291456 | tf_op jit(solution)/shard_map/pallas_call | solution.py:807
  15.7 0.6 %all-to-all-done = bf16[16,8,640]{2,1,0:T(8,128)(2,1)} async-done(((bf16[16,8,640]{2,1,0:T(8,128)(2,1)}), bf16[16,8,640]{2,1,0:T(8,128)(2,1)}, u32[]{:S(2)}, u32[]{:S(2)}) %all-to-all-start) | async-done | bytes 163872 | tf_op jit(solution)/shard_map/all_to_all | solution.py:792
  16.2 4.5 %shard_map.186.after_any = bf16[128,896]{1,0:T(8,128)(2,1)} custom-call(bf16[128,640]{1,0:T(8,128)(2,1)} %bitcast.9.recv_any, bf16[4,256,256]{2,1,0:T(8,128)(2,1)} %get-tuple-element.15.key_any, bf16[4,256,256]{2,1,0:T(8,128)(2,1)} %get-tuple-element.16.value_any, s32[128,128]{1,0:T(8,128)} %get-tuple-element.17.code_any, ...), custom_call_target="tpu_custom_call" | custom-call | flops 134217728 | bytes 4194304 | tf_op jit(solution)/shard_map/pallas_call | solution.py:842
  20.8 5.7 %all-to-all-start.1 = ((bf16[16,8,896]{2,1,0:T(8,128)(2,1)}), bf16[16,8,896]{2,1,0:T(8,128)(2,1)}, u32[]{:S(2)}, u32[]{:S(2)}) async-start(bf16[16,8,896]{2,1,0:T(8,128)(2,1)} %bitcast.14), calls=%async_computation.1 | async-start | bytes 458752 | tf_op jit(solution)/shard_map/all_to_all | solution.py:851
  26.5 6.9 %shard_map.187 = (bf16[8,512,256]{2,1,0:T(8,128)(2,1)}, f32[8,64,128]{2,1,0:T(8,128)}, f32[8,64,128]{2,1,0:T(8,128)}, f32[8,8192]{1,0:T(8,128)}, f32[8,8192]{1,0:T(8,128)}) custom-call(f32[128]{0:T(128)} %rate_any.3, f32[128]{0:T(128)} %skip_any.3, s32[8]{0:T(128)} %len_any.3, bf16[8,8,256]{2,1,0:T(8,128)(2,1)} %dt_any.3, ...), custom_call_target="tpu_custom_call", output_to_operand_aliasing={{0}: (16, {})} | custom-call | flops 2013265920 | bytes 8388608 | tf_op jit(solution)/shard_map/pallas_call | solution.py:858
  33.3 0.4 %all-to-all-done.1.back_any = bf16[16,8,896]{2,1,0:T(8,128)(2,1)} async-done(((bf16[16,8,896]{2,1,0:T(8,128)(2,1)}), bf16[16,8,896]{2,1,0:T(8,128)(2,1)}, u32[]{:S(2)}, u32[]{:S(2)}) %all-to-all-start.1) | async-done | bytes 229408 | tf_op jit(solution)/shard_map/all_to_all | solution.py:851
  33.8 2.3 %shard_map.188 = (bf16[3,2,8192]{2,1,0:T(2,128)(2,1)}, bf16[3,2,8192]{2,1,0:T(2,128)(2,1)}) custom-call(bf16[16,8,896]{2,1,0:T(8,128)(2,1)} %all-to-all-done.1.back_any, f32[8,64,128]{2,1,0:T(8,128)} %get-tuple-element.21.own_any, f32[8,64,128]{2,1,0:T(8,128)} %get-tuple-element.22.ownsum_any, f32[8,8192]{1,0:T(8,128)} %get-tuple-element.23.fade_any, ...), custom_call_target="tpu_custom_call" | custom-call | bytes 2097152 | tf_op jit(solution)/shard_map/pallas_call | solution.py:919
Async XLA Ops:
  0.6 9.7 %collective-permute-start = (bf16[64,16,256]{2,1,0:T(8,128)(2,1)}, bf16[64,16,256]{2,1,0:T(8,128)(2,1)}, u32[]{:S(2)}, u32[]{:S(2)}) collective-permute-start(bf16[64,16,256]{2,1,0:T(8,128)(2,1)} %pages_any.1), channel_id=1, source_target_pairs={{0,1},{1,0},{2,3},{3,2},{4,5},{5,4},{6,7},{7,6},{8,9},{9,8},{10,11... | collective-permute-start | bytes 1572872 | tf_op jit(solution)/shard_map/ppermute | solution.py:775
  2.8 13.4 %all-to-all-start = ((bf16[16,8,640]{2,1,0:T(8,128)(2,1)}), bf16[16,8,640]{2,1,0:T(8,128)(2,1)}, u32[]{:S(2)}, u32[]{:S(2)}) async-start(bf16[16,8,640]{2,1,0:T(8,128)(2,1)} %bitcast.15), calls=%async_computation | async-start | bytes 327680 | tf_op jit(solution)/shard_map/all_to_all | solution.py:792
  20.8 13.0 %all-to-all-start.1 = ((bf16[16,8,896]{2,1,0:T(8,128)(2,1)}), bf16[16,8,896]{2,1,0:T(8,128)(2,1)}, u32[]{:S(2)}, u32[]{:S(2)}) async-start(bf16[16,8,896]{2,1,0:T(8,128)(2,1)} %bitcast.14), calls=%async_computation.1 | async-start | bytes 458752 | tf_op jit(solution)/shard_map/all_to_all | solution.py:851

commit v16 on v15

--- a/solution.py
+++ b/solution.py
@@ -370,7 +370,7 @@
     for pair in range(prompts // 2):
         scores = scores + dot_nt(query_ref[pair], key_ref[pair])
     copies[3].wait()
-    for copy in states:
+    for copy in states[: prompts // 2]:
         copy.wait()
     seen = jnp.concatenate([lengths[:, :1]] * heads, axis=0) > iota((heads * rows, keys), 1) + begin
     scores = jnp.where(seen, scores * SCORE, NONE)
@@ -407,6 +407,8 @@
     target = jnp.concatenate([target, target], axis=-1)
     found = jnp.zeros((rows, width), f32)
     for r in range(prompts):
+        if r >= prompts // 2:
+            states[r].wait()
         picked = jnp.where(target == r, readout, 0.0).astype(bf16)
         found = found + dot_nt(picked, state_ref[r])
     if width < LANES:

time: 36.5 us -> 36.6 us (level)
  no operation moved by 1% of the time
where the time goes in v16:
time: 36.6 us; the launch traced here: 36.1 us
  Pallas kernels  20.7 us (57%)
  starting transfers between devices  13.7 us (37%)
  waiting for transfers between devices  1 us (3%)
  between operations  0.67 us (2%)
    all_to_all x1, starting transfers between devices, on_device(): lax.all_to_all(send, 'heads', split_axis=0, concat_axis=0, tiled=True, ax...  7.53 us
    pallas_call x1, Pallas kernels, on_device(): call(prompt_kernel, (shape(prompt_x.shape, bf16), shape((KVH, count, HD),...  6.86 us
    all_to_all x1, starting transfers between devices, on_device(): lax.all_to_all(back, 'heads', split_axis=0, concat_axis=0, tiled=True, ax...  5.69 us
    pallas_call x1, Pallas kernels, on_device(): call(state_kernel, (shape((prompts, width, NS), bf16), shape((prompts //...  5.29 us
    pallas_call x1, Pallas kernels, on_device(): call(serve_kernel, shape((all_rows, HALF + max(LANES, width) - LANES), bf...  4.64 us
    pallas_call x1, Pallas kernels, on_device(): call(functools.partial(merge_kernel, width), (shape(step_x.shape, bf16),...  2.26 us
    pallas_call x1, Pallas kernels, on_device(): call(functools.partial(pack_kernel, group, ways), shape((all_rows, HALF +...  1.67 us
  transfers between devices with their start and end apart: 3, of which 2 were waited for; matrix products, arithmetic and copies ran while one was open for 0% of the time, Pallas kernels for 38%

profile of v16, /device:TPU:0, one launch (start us, length us, event | category | flops | bytes accessed | tf_op | source)
XLA Modules:
  0.0 36.1 jit_solution(18055787471165782913)
XLA Ops:
  0.6 0.5 %collective-permute-start = (bf16[64,16,256]{2,1,0:T(8,128)(2,1)}, bf16[64,16,256]{2,1,0:T(8,128)(2,1)}, u32[]{:S(2)}, u32[]{:S(2)}) collective-permute-start(bf16[64,16,256]{2,1,0:T(8,128)(2,1)} %pages_any.1), channel_id=1, source_target_pairs={{0,1},{1,0},{2,3},{3,2},{4,5},{5,4},{6,7},{7,6},{8,9},{9,8},{10,11... | collective-permute-start | bytes 1572872 | tf_op jit(solution)/shard_map/ppermute | solution.py:777
  1.1 1.7 %shard_map.184 = bf16[128,640]{1,0:T(8,128)(2,1)} custom-call(bf16[3,2,8192]{2,1,0:T(2,128)(2,1)} %bitcast.18, bf16[3,2,1024]{2,1,0:T(2,128)(2,1)} %bitcast.19), custom_call_target="tpu_custom_call" | custom-call | bytes 524288 | tf_op jit(solution)/shard_map/pallas_call | solution.py:778
  2.8 7.5 %all-to-all-start = ((bf16[16,8,640]{2,1,0:T(8,128)(2,1)}), bf16[16,8,640]{2,1,0:T(8,128)(2,1)}, u32[]{:S(2)}, u32[]{:S(2)}) async-start(bf16[16,8,640]{2,1,0:T(8,128)(2,1)} %bitcast.15), calls=%async_computation | async-start | bytes 327680 | tf_op jit(solution)/shard_map/all_to_all | solution.py:794
  10.4 0.0 collective-permute-done.other_any
  10.4 5.3 %shard_map.185 = (bf16[8,512,256]{2,1,0:T(8,128)(2,1)}, bf16[4,256,256]{2,1,0:T(8,128)(2,1)}, bf16[4,256,256]{2,1,0:T(8,128)(2,1)}, s32[128,128]{1,0:T(8,128)}, bf16[8,512,256]{2,1,0:T(8,128)(2,1)}) custom-call(f32[128]{0:T(128)} %rate_any.3, f32[128]{0:T(128)} %skip_any.3, s32[8]{0:T(128)} %len_any.3, s32[2,16]{1,0:T(2,128)} %bitcast.26, ...), custom_call_target="tpu_custom_call" | custom-call | flops 1207959552 | bytes 6291456 | tf_op jit(solution)/shard_map/pallas_call | solution.py:809
  15.7 0.6 %all-to-all-done = bf16[16,8,640]{2,1,0:T(8,128)(2,1)} async-done(((bf16[16,8,640]{2,1,0:T(8,128)(2,1)}), bf16[16,8,640]{2,1,0:T(8,128)(2,1)}, u32[]{:S(2)}, u32[]{:S(2)}) %all-to-all-start) | async-done | bytes 163872 | tf_op jit(solution)/shard_map/all_to_all | solution.py:794
  16.2 4.6 %shard_map.186.after_any = bf16[128,896]{1,0:T(8,128)(2,1)} custom-call(bf16[128,640]{1,0:T(8,128)(2,1)} %bitcast.9.recv_any, bf16[4,256,256]{2,1,0:T(8,128)(2,1)} %get-tuple-element.15.key_any, bf16[4,256,256]{2,1,0:T(8,128)(2,1)} %get-tuple-element.16.value_any, s32[128,128]{1,0:T(8,128)} %get-tuple-element.17.code_any, ...), custom_call_target="tpu_custom_call" | custom-call | flops 134217728 | bytes 4194304 | tf_op jit(solution)/shard_map/pallas_call | solution.py:844
  20.9 5.7 %all-to-all-start.1 = ((bf16[16,8,896]{2,1,0:T(8,128)(2,1)}), bf16[16,8,896]{2,1,0:T(8,128)(2,1)}, u32[]{:S(2)}, u32[]{:S(2)}) async-start(bf16[16,8,896]{2,1,0:T(8,128)(2,1)} %bitcast.14), calls=%async_computation.1 | async-start | bytes 458752 | tf_op jit(solution)/shard_map/all_to_all | solution.py:853
  26.6 6.9 %shard_map.187 = (bf16[8,512,256]{2,1,0:T(8,128)(2,1)}, f32[8,64,128]{2,1,0:T(8,128)}, f32[8,64,128]{2,1,0:T(8,128)}, f32[8,8192]{1,0:T(8,128)}, f32[8,8192]{1,0:T(8,128)}) custom-call(f32[128]{0:T(128)} %rate_any.3, f32[128]{0:T(128)} %skip_any.3, s32[8]{0:T(128)} %len_any.3, bf16[8,8,256]{2,1,0:T(8,128)(2,1)} %dt_any.3, ...), custom_call_target="tpu_custom_call", output_to_operand_aliasing={{0}: (16, {})} | custom-call | flops 2013265920 | bytes 8388608 | tf_op jit(solution)/shard_map/pallas_call | solution.py:860
  33.5 0.4 %all-to-all-done.1.back_any = bf16[16,8,896]{2,1,0:T(8,128)(2,1)} async-done(((bf16[16,8,896]{2,1,0:T(8,128)(2,1)}), bf16[16,8,896]{2,1,0:T(8,128)(2,1)}, u32[]{:S(2)}, u32[]{:S(2)}) %all-to-all-start.1) | async-done | bytes 229408 | tf_op jit(solution)/shard_map/all_to_all | solution.py:853
  33.9 2.3 %shard_map.188 = (bf16[3,2,8192]{2,1,0:T(2,128)(2,1)}, bf16[3,2,8192]{2,1,0:T(2,128)(2,1)}) custom-call(bf16[16,8,896]{2,1,0:T(8,128)(2,1)} %all-to-all-done.1.back_any, f32[8,64,128]{2,1,0:T(8,128)} %get-tuple-element.21.own_any, f32[8,64,128]{2,1,0:T(8,128)} %get-tuple-element.22.ownsum_any, f32[8,8192]{1,0:T(8,128)} %get-tuple-element.23.fade_any, ...), custom_call_target="tpu_custom_call" | custom-call | bytes 2097152 | tf_op jit(solution)/shard_map/pallas_call | solution.py:921
Async XLA Ops:
  0.6 9.7 %collective-permute-start = (bf16[64,16,256]{2,1,0:T(8,128)(2,1)}, bf16[64,16,256]{2,1,0:T(8,128)(2,1)}, u32[]{:S(2)}, u32[]{:S(2)}) collective-permute-start(bf16[64,16,256]{2,1,0:T(8,128)(2,1)} %pages_any.1), channel_id=1, source_target_pairs={{0,1},{1,0},{2,3},{3,2},{4,5},{5,4},{6,7},{7,6},{8,9},{9,8},{10,11... | collective-permute-start | bytes 1572872 | tf_op jit(solution)/shard_map/ppermute | solution.py:777
  2.8 13.4 %all-to-all-start = ((bf16[16,8,640]{2,1,0:T(8,128)(2,1)}), bf16[16,8,640]{2,1,0:T(8,128)(2,1)}, u32[]{:S(2)}, u32[]{:S(2)}) async-start(bf16[16,8,640]{2,1,0:T(8,128)(2,1)} %bitcast.15), calls=%async_computation | async-start | bytes 327680 | tf_op jit(solution)/shard_map/all_to_all | solution.py:794
  20.9 13.0 %all-to-all-start.1 = ((bf16[16,8,896]{2,1,0:T(8,128)(2,1)}), bf16[16,8,896]{2,1,0:T(8,128)(2,1)}, u32[]{:S(2)}, u32[]{:S(2)}) async-start(bf16[16,8,896]{2,1,0:T(8,128)(2,1)} %bitcast.14), calls=%async_computation.1 | async-start | bytes 458752 | tf_op jit(solution)/shard_map/all_to_all | solution.py:853
